TPU v7x, 512 devices: a whole 4x4x16 slice. The times are simulated.
512 devices in a mesh: fsdp: 64 (over x_lo, z, core), sp: 8 (over y, x_hi).
Axes of the slice: x: 4 (x_hi: 2, x_lo: 2; x = x_hi * 2 + x_lo), y: 4, z: 16, core: 2. Of those that a mesh axis runs over, the one named last changes fastest.
Arguments:
- qkv_txt: bfloat16 [64, 3, 256, 2048], P('fsdp', None, 'sp'), may hold values from -5 to 5
- qkv_img: bfloat16 [64, 3, 768, 2048], P('fsdp', None, 'sp'), may hold values from -5 to 5
- dy_txt: bfloat16 [64, 256, 3072], P('fsdp', 'sp'), may hold values from -6 to 6
- dy_img: bfloat16 [64, 768, 3072], P('fsdp', 'sp'), may hold values from -16 to 16
- wv_txt: bfloat16 [3072, 2048], P('fsdp', 'sp'), may hold values from -0.109375 to 0.109375
- sc_txt: float32 [3072, 16], P('fsdp', 'sp'), may hold values from 0.5 to 2
- wv_img: bfloat16 [3072, 2048], P('fsdp', 'sp'), may hold values from -0.109375 to 0.109375
- sc_img: float32 [3072, 16], P('fsdp', 'sp'), may hold values from 0.5 to 2
Outputs:
- grad_qkv_txt: bfloat16 [64, 3, 256, 2048], P('fsdp', None, 'sp')
- grad_qkv_img: bfloat16 [64, 3, 768, 2048], P('fsdp', None, 'sp')
- grad_w_img: float32 [3072, 2048], P('fsdp', 'sp')
All inputs are finite; a program needn't handle non-finite values.
Results may differ from a plain program's by a relative error of at most 0.02.
Values may be sent and summed in bfloat16 or wider, within the bound.
No kernel may reach another device: no remote copies, remote signals or barrier semaphores. Data moves between devices by JAX's collectives and lax.ppermute only.
A program may use at most 64 MiB of HBM per device.

v0:
```python
import math

import jax
import jax.numpy as jnp
from jax import lax
from jax.sharding import PartitionSpec as P

HD = 128


def dequant(values, scales):
    return (values.astype(jnp.float32) * jnp.repeat(scales, HD, axis=1)).astype(jnp.bfloat16)


def contract_first(left, right):
    return lax.dot_general(
        left, right, (((0,), (0,)), ((), ())), preferred_element_type=jnp.float32
    )


def contract_last(left, right):
    return lax.dot_general(
        left, right, (((1,), (1,)), ((), ())), preferred_element_type=jnp.float32
    )


def head_forward(query_head, key_head, value_head, factor):
    scores = contract_last(query_head, key_head) * factor
    highest = jnp.max(scores, axis=-1, keepdims=True)
    weights = jnp.exp(scores - highest)
    probs = weights / jnp.sum(weights, axis=-1, keepdims=True)
    probs_low = probs.astype(jnp.bfloat16)
    attended = jnp.dot(probs_low, value_head, preferred_element_type=jnp.float32).astype(
        jnp.bfloat16
    )
    return (probs, probs_low, attended)


def head_backward(
    query_head, key_head, value_head, probs, probs_low, attended_head, grad_head, factor
):
    delta = jnp.sum(grad_head.astype(jnp.float32) * attended_head.astype(jnp.float32), axis=-1)
    prob_grad = contract_last(grad_head, value_head)
    score_grad = (probs * (prob_grad - delta[:, None])).astype(jnp.bfloat16)
    grad_query = (
        jnp.dot(score_grad, key_head, preferred_element_type=jnp.float32) * factor
    ).astype(jnp.bfloat16)
    grad_keys = (contract_first(score_grad, query_head) * factor).astype(jnp.bfloat16)
    grad_values = contract_first(probs_low, grad_head).astype(jnp.bfloat16)
    return (grad_query, grad_keys, grad_values)


def local(qkv_txt, qkv_img, dy_txt, dy_img, wv_txt, sc_txt, wv_img, sc_img):
    w_txt, w_img = (
        lax.all_gather(dequant(wv_txt, sc_txt), "fsdp", axis=0, tiled=True),
        lax.all_gather(dequant(wv_img, sc_img), "fsdp", axis=0, tiled=True),
    )
    heads_txt, heads_img = (
        lax.all_to_all(qkv_txt, "sp", split_axis=3, concat_axis=2, tiled=True),
        lax.all_to_all(qkv_img, "sp", split_axis=3, concat_axis=2, tiled=True),
    )
    text_rows = heads_txt.shape[2]
    joint = jnp.concatenate([heads_txt[0], heads_img[0]], axis=1)
    queries, keyset, valueset = (joint[0], joint[1], joint[2])
    features = joint.shape[2]
    count = features // HD
    factor = 1.0 / math.sqrt(HD)
    windows = [slice(head * HD, (head + 1) * HD) for head in range(count)]
    query_parts, key_parts, value_parts = ([], [], [])
    full_txt, full_img = (
        lax.all_gather(dy_txt, "sp", axis=1, tiled=True),
        lax.all_gather(dy_img, "sp", axis=1, tiled=True),
    )
    grad_out = jnp.concatenate(
        [
            jnp.dot(full_txt[0], w_txt, preferred_element_type=jnp.float32).astype(jnp.bfloat16),
            jnp.dot(full_img[0], w_img, preferred_element_type=jnp.float32).astype(jnp.bfloat16),
        ],
        axis=0,
    )
    attended_parts = []
    for window in windows:
        query_head, key_head, value_head = (
            queries[:, window],
            keyset[:, window],
            valueset[:, window],
        )
        probs, probs_low, attended_head = head_forward(query_head, key_head, value_head, factor)
        attended_parts.append(attended_head)
        grad_query, grad_keys, grad_values = head_backward(
            query_head,
            key_head,
            value_head,
            probs,
            probs_low,
            attended_head,
            grad_out[:, window],
            factor,
        )
        query_parts.append(grad_query)
        key_parts.append(grad_keys)
        value_parts.append(grad_values)
    attended = jnp.concatenate(attended_parts, axis=1)
    weight_term = contract_first(full_img[0], attended[text_rows:])
    grads = jnp.stack(
        [
            jnp.concatenate(query_parts, axis=1),
            jnp.concatenate(key_parts, axis=1),
            jnp.concatenate(value_parts, axis=1),
        ]
    )
    back_txt, back_img = (
        lax.all_to_all(grads[None, :, :text_rows], "sp", split_axis=2, concat_axis=3, tiled=True),
        lax.all_to_all(grads[None, :, text_rows:], "sp", split_axis=2, concat_axis=3, tiled=True),
    )
    weight_grad = lax.psum_scatter(
        weight_term, "fsdp", scatter_dimension=0, tiled=True
    ) / lax.axis_size("fsdp")
    return (back_txt, back_img, weight_grad)


def solution(mesh):
    placed = (
        P("fsdp", None, "sp", None),
        P("fsdp", None, "sp", None),
        P("fsdp", "sp", None),
        P("fsdp", "sp", None),
        P("fsdp", "sp"),
        P("fsdp", "sp"),
        P("fsdp", "sp"),
        P("fsdp", "sp"),
    )
    return jax.shard_map(
        local,
        mesh=mesh,
        in_specs=placed,
        out_specs=(P("fsdp", None, "sp", None), P("fsdp", None, "sp", None), P("fsdp", "sp")),
        check_vma=False,
    )
```

profile of v0, /device:TPU:8, one launch (start us, length us, event | category | flops | bytes accessed | tf_op | source)
XLA Modules:
  0.0 669.5 jit_solution(12873890185147749207)
XLA Ops:
  7.2 0.7 all-gather.7.cloned.1.call-update
  8.0 0.8 copy.45
  8.8 1.4 fusion.56
  10.3 0.8 copy.46
  11.1 1.4 fusion.55
  13.1 2.8 copy.39
  15.9 2.5 reshape.24
  18.4 9.2 %all-to-all-start = ((bf16[8,2,12288]{2,1,0:T(2,128)(2,1)}), bf16[8,2,12288]{2,1,0:T(2,128)(2,1)S(1)}, u32[]{:S(2)}, u32[]{:S(2)}) async-start(bf16[8,2,12288]{2,1,0:T(2,128)(2,1)} %reshape.24), calls=%async_computation | async-start | bytes 786432 | tf_op jit(solution)/shard_map/all_to_all | solution.py:59
  27.6 2.5 copy.42
  30.1 5.2 all-to-all-done
  35.3 6.0 all-to-all-start.1
  41.3 1.3 reshape.25
  42.7 1.0 copy.60
  43.7 21.7 %all-to-all-done.1 = bf16[1,3,96,2048]{2,1,0,3:T(4,128)(2,1)} async-done(((bf16[1,3,96,2048]{2,1,0,3:T(4,128)(2,1)}), bf16[1,3,96,2048]{2,1,0,3:T(4,128)(2,1)}, u32[]{:S(2)}, u32[]{:S(2)}) %all-to-all-start.1) | async-done | bytes 1179680 | tf_op jit(solution)/shard_map/all_to_all | solution.py:60
  65.4 2.8 copy.62
  68.4 0.7 multiply_reduce_fusion
  69.1 0.7 fusion.10
  69.8 0.7 multiply_reduce_fusion.1
  70.6 2.0 copy-done
  72.6 0.7 fusion.8
  73.4 1.0 convolution_convert_fusion.2
  74.4 10.3 %all-gather.7.cloned.1.call-done = bf16[1,256,3072]{2,1,0:T(8,128)(2,1)} async-done(((bf16[1,32,3072]{2,1,0:T(8,128)(2,1)}), bf16[1,256,3072]{2,1,0:T(8,128)(2,1)}) %all-gather.7.cloned.1.call-update) | async-done | bytes 1572880 | tf_op jit(solution)/shard_map/all_gather | solution.py:71
  84.7 123.8 %all-gather.5.cloned.1.call-done = bf16[3072,256]{1,0:T(8,128)(2,1)} async-done(((bf16[48,256]{1,0:T(8,128)(2,1)}), bf16[3072,256]{1,0:T(8,128)(2,1)}) %all-gather.5.cloned.1.call-update) | async-done | bytes 1572880 | tf_op jit(solution)/shard_map/all_gather | solution.py:55
  208.4 2.4 fusion.27
  211.0 118.3 %all-gather.9.cloned.1.call-done = bf16[3072,256]{1,0:T(8,128)(2,1)} async-done(((bf16[48,256]{1,0:T(8,128)(2,1)}), bf16[3072,256]{1,0:T(8,128)(2,1)}) %all-gather.9.cloned.1.call-update) | async-done | bytes 1572880 | tf_op jit(solution)/shard_map/all_gather | solution.py:56
  329.3 89.2 %all-gather.11.cloned.1.call-done = bf16[1,768,3072]{2,1,0:T(8,128)(2,1)} async-done(((bf16[1,96,3072]{2,1,0:T(8,128)(2,1)}), bf16[1,768,3072]{2,1,0:T(8,128)(2,1)}) %all-gather.11.cloned.1.call-update) | async-done | bytes 4718608 | tf_op jit(solution)/shard_map/all_gather | solution.py:72
  418.5 4.4 fusion.16
  422.9 1.0 multiply_reduce_fusion.3
  424.2 3.0 fusion.4
  427.2 3.5 copy.63
  430.8 3.4 convolution_convert_fusion
  434.2 1.1 convolution_convert_fusion.1
  435.3 1.1 copy-done.4
  436.4 1.2 multiply_convert_fusion
  438.1 0.8 fusion.22
  438.9 1.2 multiply_convert_fusion.1
  440.6 0.8 fusion.21
  441.6 1.1 copy.50
  442.7 5.2 all-to-all-start.2
  448.0 2.2 copy.53
  450.1 7.6 %all-to-all-done.2 = bf16[1,3,256,256]{3,1,0,2:T(4,128)(2,1)S(1)} async-done(((bf16[1,3,256,256]{3,1,0,2:T(4,128)(2,1)}), bf16[1,3,256,256]{3,1,0,2:T(4,128)(2,1)S(1)}, u32[]{:S(2)}, u32[]{:S(2)}) %all-to-all-start.2) | async-done | bytes 393248 | tf_op jit(solution)/shard_map/all_to_all | solution.py:113
  457.8 5.6 all-to-all-start.3
  463.4 0.8 copy.65
  464.2 19.8 %all-to-all-done.3 = bf16[1,3,768,256]{3,1,0,2:T(4,128)(2,1)S(1)} async-done(((bf16[1,3,768,256]{3,1,0,2:T(4,128)(2,1)}), bf16[1,3,768,256]{3,1,0,2:T(4,128)(2,1)S(1)}, u32[]{:S(2)}, u32[]{:S(2)}) %all-to-all-start.3) | async-done | bytes 1179680 | tf_op jit(solution)/shard_map/all_to_all | solution.py:114
  484.2 1.2 copy.66
  485.4 176.0 %reduce-scatter.4.cloned.1.call-done = f32[48,256]{1,0:T(8,128)} async-done(((f32[3072,256]{1,0:T(8,128)}), f32[48,256]{1,0:T(8,128)}) %reduce-scatter.4.cloned.1.call-update) | async-done | bytes 49168
  661.4 0.9 copy.64
  662.3 0.7 copy.56
  (37 shorter events, 2.9 us)
Async XLA Ops:
  7.2 20.4 %copy-start.5 = (bf16[1,3,96,2048]{3,2,1,0:T(8,128)(2,1)S(1)}, bf16[1,3,96,2048]{3,2,1,0:T(8,128)(2,1)}, u32[]{:S(2)}) copy-start(bf16[1,3,96,2048]{3,2,1,0:T(8,128)(2,1)} %param.9) | copy-start | bytes 3538948
  7.2 77.5 %all-gather.7.cloned.1.call-start = ((), (), s32[]{:S(2)}) async-start(), calls=%async_computation.6 | async-start | bytes 1769472 | tf_op jit(solution)/shard_map/all_gather | solution.py:71
  7.9 200.5 %all-gather.5.cloned.1.call-start = ((), (), s32[]{:S(2)}) async-start(), calls=%async_computation.5 | async-start | bytes 1597440 | tf_op jit(solution)/shard_map/all_gather | solution.py:55
  10.2 319.1 %all-gather.9.cloned.1.call-start = ((), (), s32[]{:S(2)}) async-start(), calls=%async_computation.7 | async-start | bytes 1597440 | tf_op jit(solution)/shard_map/all_gather | solution.py:56
  12.5 406.0 %all-gather.11.cloned.1.call-start = ((), (), s32[]{:S(2)}) async-start(), calls=%async_computation.8 | async-start | bytes 5308416 | tf_op jit(solution)/shard_map/all_gather | solution.py:72
  18.4 16.9 %all-to-all-start = ((bf16[8,2,12288]{2,1,0:T(2,128)(2,1)}), bf16[8,2,12288]{2,1,0:T(2,128)(2,1)S(1)}, u32[]{:S(2)}, u32[]{:S(2)}) async-start(bf16[8,2,12288]{2,1,0:T(2,128)(2,1)} %reshape.24), calls=%async_computation | async-start | bytes 786432 | tf_op jit(solution)/shard_map/all_to_all | solution.py:59
  35.3 30.1 %all-to-all-start.1 = ((bf16[1,3,96,2048]{2,1,0,3:T(4,128)(2,1)}), bf16[1,3,96,2048]{2,1,0,3:T(4,128)(2,1)}, u32[]{:S(2)}, u32[]{:S(2)}) async-start(bf16[1,3,96,2048]{2,1,0,3:T(4,128)(2,1)} %copy.42), calls=%async_computation.1 | async-start | bytes 4194304 | tf_op jit(solution)/shard_map/all_to_all | solution.py:60
  41.3 620.0 %reduce-scatter.4.cloned.1.call-start = ((), (), s32[]{:S(2)}) async-start(), calls=%async_computation.9 | async-start | bytes 3194880
  69.1 4.2 copy-start.3
  70.6 2.1 copy-start
  418.5 4.4 copy-start.1
  418.5 5.5 slice-start
  422.9 1.3 slice-start.1
  430.8 3.5 copy-start.2
  434.2 2.2 copy-start.4
  442.7 15.1 %all-to-all-start.2 = ((bf16[1,3,256,256]{3,1,0,2:T(4,128)(2,1)}), bf16[1,3,256,256]{3,1,0,2:T(4,128)(2,1)S(1)}, u32[]{:S(2)}, u32[]{:S(2)}) async-start(bf16[1,3,256,256]{3,1,0,2:T(4,128)(2,1)} %copy.50), calls=%async_computation.2 | async-start | bytes 1048576 | tf_op jit(solution)/shard_map/all_to_all | solution.py:113
  457.8 26.3 %all-to-all-start.3 = ((bf16[1,3,768,256]{3,1,0,2:T(4,128)(2,1)}), bf16[1,3,768,256]{3,1,0,2:T(4,128)(2,1)S(1)}, u32[]{:S(2)}, u32[]{:S(2)}) async-start(bf16[1,3,768,256]{3,1,0,2:T(4,128)(2,1)} %copy.53), calls=%async_computation.3 | async-start | bytes 3145728 | tf_op jit(solution)/shard_map/all_to_all | solution.py:114
Sparse Core Ops, SparseCore 0:
  11.2 73.4 all-gather.6
  87.4 120.9 all-gather.4
  211.1 118.0 all-gather.8
  332.3 86.1 all-gather.10
  430.9 230.4 reduce-scatter.3
where the time goes:
time: 670 us; the launch traced here: 669 us
  waiting for transfers between devices  573 us (86%)
  local copies, waits for them, and re-layouts  28.7 us (4%)
  starting transfers between devices  26.2 us (4%)
  matrix products  22.8 us (3%)
  between operations  14 us (2%)
    unnamed x6, waiting for transfers between devices  177 us
    all_gather x1, waiting for transfers between devices, local(): lax.all_gather(dequant(wv_txt, sc_txt), 'fsdp', axis=0, tiled=True)  124 us
    all_gather x1, waiting for transfers between devices, local(): lax.all_gather(dequant(wv_img, sc_img), 'fsdp', axis=0, tiled=True)  118 us
    all_gather x1, waiting for transfers between devices, local(): lax.all_gather(dy_img, 'sp', axis=1, tiled=True)  89.2 us
    all_to_all x1, waiting for transfers between devices, local(): lax.all_to_all(qkv_img, 'sp', split_axis=3, concat_axis=2, tiled=True)  21.7 us
    all_to_all x1, waiting for transfers between devices, local(): lax.all_to_all(grads[None, :, text_rows:], 'sp', split_axis=2, concat_axi...  19.8 us
    unnamed x25, local copies, waits for them, and re-layouts  19.2 us
  transfers between devices with their start and end apart: 9, of which 9 were waited for; matrix products, arithmetic and copies ran while one was open for 6% of the time, Pallas kernels for 0%

commit v1 on v0

v1 whole, which is shorter than its diff:
```python
import functools
import math

import jax
import jax.numpy as jnp
from jax import lax
from jax.experimental import pallas as pl
from jax.experimental.pallas import tpu as pltpu
from jax.sharding import PartitionSpec as P

HD = 128
SP = 8
TXT = 32
IMG = 96
TOK = TXT + IMG
ALL_TXT = SP * TXT
LENGTH = SP * TOK
COLS = 256
D = 3072
ROWS = 48
HEADS = COLS // HD
CHUNK = 256
FACTOR = 1.0 / math.sqrt(HD)
LOG2E = 1.4426950408889634
SCALE2 = FACTOR * LOG2E
AXES = ("fsdp", "sp")
VMEM_LIMIT = 48 * 1024 * 1024


def number(x_lo, z, core, y, x_hi):
    return ((x_lo * 16 + z) * 2 + core) * SP + y * 2 + x_hi


def every():
    return [
        (x_lo, z, core, y, x_hi)
        for x_lo in range(2)
        for z in range(16)
        for core in range(2)
        for y in range(4)
        for x_hi in range(2)
    ]


def route(target):
    return [(number(*d), number(*target(*d))) for d in every()]


SWAP_CORE = route(lambda x_lo, z, core, y, x_hi: (x_lo, z, 1 - core, y, x_hi))
SWAP_X_LO = route(lambda x_lo, z, core, y, x_hi: (1 - x_lo, z, core, y, x_hi))
SWAP_X_HI = route(lambda x_lo, z, core, y, x_hi: (x_lo, z, core, y, 1 - x_hi))
FROM_Y = {
    k: route(lambda x_lo, z, core, y, x_hi, k=k: (x_lo, z, core, (y - k) % 4, x_hi))
    for k in (1, 2, 3)
}
Z_GROUPS = [
    [number(x_lo, z, core, y, x_hi) for z in range(16)]
    for x_lo in range(2)
    for core in range(2)
    for y in range(4)
    for x_hi in range(2)
]


def send(x, pairs):
    return lax.ppermute(x, AXES, pairs)


def dequant(values, scales):
    return (values.astype(jnp.float32) * jnp.repeat(scales, HD, axis=1)).astype(jnp.bfloat16)


def dot(a, b):
    return jnp.dot(a, b, preferred_element_type=jnp.float32)


def dot_last(a, b):
    return lax.dot_general(a, b, (((1,), (1,)), ((), ())), preferred_element_type=jnp.float32)


def transposed(x):
    return x.astype(jnp.float32).T


def load_qkv(x_ref, joint, sems):
    copies = []
    for r in range(SP):
        copies.append(
            pltpu.make_async_copy(
                x_ref.at[r, :, pl.ds(0, TXT), :],
                joint.at[:, pl.ds(r * TXT, TXT), :],
                sems.at[2 * r],
            )
        )
        copies.append(
            pltpu.make_async_copy(
                x_ref.at[r, :, pl.ds(TXT, IMG), :],
                joint.at[:, pl.ds(ALL_TXT + r * IMG, IMG), :],
                sems.at[2 * r + 1],
            )
        )
    for copy in copies:
        copy.start()
    return copies


def forward_kernel(x_ref, att_ref, lse_ref, joint, sems):
    for copy in load_qkv(x_ref, joint, sems):
        copy.wait()
    for head in range(HEADS):
        window = slice(head * HD, (head + 1) * HD)
        keys = joint[1, :, window]
        values_t = transposed(joint[2, :, window]).astype(jnp.bfloat16)
        for chunk in range(LENGTH // CHUNK):
            rows = slice(chunk * CHUNK, (chunk + 1) * CHUNK)
            scores = dot_last(keys, joint[0, rows, window])
            highest = jnp.max(scores, axis=0, keepdims=True)
            weights = jnp.exp2((scores - highest) * SCALE2)
            total = jnp.sum(weights, axis=0, keepdims=True)
            att_t = dot(values_t, weights.astype(jnp.bfloat16)) / total
            att_ref[rows, window] = att_t.T.astype(jnp.bfloat16)
            lse_ref[head : head + 1, rows] = highest * SCALE2 + jnp.log2(total)


def forward(x):
    return pl.pallas_call(
        forward_kernel,
        out_shape=(
            jax.ShapeDtypeStruct((LENGTH, COLS), jnp.bfloat16),
            jax.ShapeDtypeStruct((HEADS, LENGTH), jnp.float32),
        ),
        in_specs=[pl.BlockSpec(memory_space=pl.ANY)],
        out_specs=(
            pl.BlockSpec(memory_space=pltpu.VMEM),
            pl.BlockSpec(memory_space=pltpu.VMEM),
        ),
        scratch_shapes=[
            pltpu.VMEM((3, LENGTH, COLS), jnp.bfloat16),
            pltpu.SemaphoreType.DMA((2 * SP,)),
        ],
        compiler_params=pltpu.CompilerParams(vmem_limit_bytes=VMEM_LIMIT),
        cost_estimate=pl.CostEstimate(
            flops=HEADS * 4 * LENGTH * LENGTH * HD,
            bytes_accessed=4 * LENGTH * COLS * 2,
            transcendentals=HEADS * LENGTH * LENGTH,
        ),
        name="attention_forward",
    )(x)


def slots(sp):
    y, x_hi = sp // 2, sp % 2
    return [((y + k) % 4) * 2 + x_hi for k in range(4)] + [
        ((y + k) % 4) * 2 + 1 - x_hi for k in range(4)
    ]


def load_dy(place_ref, pieces, text, image, sems):
    copies = []
    for n, piece in enumerate(pieces):
        slot = place_ref[n]
        if text is not None:
            copies.append(
                pltpu.make_async_copy(
                    piece.at[pl.ds(0, TXT), :],
                    text.at[pl.ds(pl.multiple_of(slot * TXT, TXT), TXT), :],
                    sems.at[2 * n],
                )
            )
        copies.append(
            pltpu.make_async_copy(
                piece.at[pl.ds(TXT, IMG), :],
                image.at[pl.ds(pl.multiple_of(slot * IMG, TXT), IMG), :],
                sems.at[2 * n + 1],
            )
        )
    for copy in copies:
        copy.start()
    return copies


BAND = 8 * 2 * ROWS


def term_kernel(place_ref, *refs):
    pieces, (att_ref, keep_ref, give_ref, image, sems) = refs[:SP], refs[SP:]
    copies = load_dy(place_ref, pieces, None, image, sems)
    att_t = transposed(att_ref[ALL_TXT:, :]).astype(jnp.bfloat16)
    for copy in copies:
        copy.wait()
    core, x_lo = place_ref[SP], place_ref[SP + 1]
    for band in range(D // BAND):
        term = dot(att_t, image[:, band * BAND : (band + 1) * BAND]).T.astype(jnp.bfloat16)
        far = (x_lo + band // 2) % 2
        for j in range(8):
            z = (band % 2) * 8 + j
            low = term[(2 * j) * ROWS : (2 * j + 1) * ROWS]
            high = term[(2 * j + 1) * ROWS : (2 * j + 2) * ROWS]
            keep_ref[far, z] = jnp.where(core == 0, low, high)
            give_ref[far, z] = jnp.where(core == 0, high, low)


def weight_term(place, pieces, att):
    half = jax.ShapeDtypeStruct((2, 16, ROWS, COLS), jnp.bfloat16)
    return pl.pallas_call(
        term_kernel,
        out_shape=(half, half),
        in_specs=[pl.BlockSpec(memory_space=pltpu.SMEM)]
        + [pl.BlockSpec(memory_space=pl.ANY)] * SP
        + [pl.BlockSpec(memory_space=pltpu.VMEM)],
        out_specs=(
            pl.BlockSpec(memory_space=pltpu.VMEM),
            pl.BlockSpec(memory_space=pltpu.VMEM),
        ),
        scratch_shapes=[
            pltpu.VMEM((SP * IMG, D), jnp.bfloat16),
            pltpu.SemaphoreType.DMA((2 * SP,)),
        ],
        compiler_params=pltpu.CompilerParams(vmem_limit_bytes=VMEM_LIMIT),
        cost_estimate=pl.CostEstimate(
            flops=2 * SP * IMG * D * COLS,
            bytes_accessed=SP * IMG * D * 2 + D * COLS * 2,
            transcendentals=0,
        ),
        name="weight_term",
    )(place, *pieces, att)


def head_backward(head, joint, grad, att, lse, probs, slopes, out_ref):
    window = slice(head * HD, (head + 1) * HD)
    keys, values = joint[1, :, window], joint[2, :, window]
    keys_t = transposed(keys).astype(jnp.bfloat16)

    def put(member, first, block):
        for r in range(SP):
            lo, hi = r * TXT - first, (r + 1) * TXT - first
            if 0 <= lo < block.shape[0]:
                out_ref[r, member, :TXT, :] = block[lo:hi]
            lo, hi = ALL_TXT + r * IMG - first, ALL_TXT + (r + 1) * IMG - first
            start, stop = max(lo, 0), min(hi, block.shape[0])
            if start < stop:
                out_ref[r, member, TXT + start - lo : TXT + stop - lo, :] = block[start:stop]

    for chunk in range(LENGTH // CHUNK):
        rows = slice(chunk * CHUNK, (chunk + 1) * CHUNK)
        out_grad = grad[rows, window]
        product = out_grad.astype(jnp.float32) * att[rows, window].astype(jnp.float32)
        delta = jnp.sum(product.T, axis=0, keepdims=True)
        scores = dot_last(keys, joint[0, rows, window])
        weights = jnp.exp2(scores * SCALE2 - lse[head : head + 1, rows])
        probs[:, rows] = weights.astype(jnp.bfloat16)
        slope = (weights * (dot_last(values, out_grad) - delta)).astype(jnp.bfloat16)
        slopes[:, rows] = slope
        grad_query = (dot(keys_t, slope) * FACTOR).T.astype(jnp.bfloat16)
        put(0, chunk * CHUNK, grad_query)
    put(1, 0, (dot(slopes[...], joint[0, :, window]) * FACTOR).astype(jnp.bfloat16))
    put(2, 0, dot(probs[...], grad[:, window]).astype(jnp.bfloat16))


def first_kernel(place_ref, *refs):
    pieces, rest = refs[:SP], refs[SP:]
    w_ref, x_ref, att, lse, out_ref, grad, text, image, weight, joint, probs, slopes = rest[:12]
    dy_sems, qkv_sems, w_sems = rest[12:]
    copies = [
        pltpu.make_async_copy(
            w_ref.at[:, x_lo, :, stream], weight.at[stream, x_lo], w_sems.at[2 * stream + x_lo]
        )
        for stream in range(2)
        for x_lo in range(2)
    ]
    for copy in copies:
        copy.start()
    copies += load_dy(place_ref, pieces, text, image, dy_sems)
    copies += load_qkv(x_ref, joint, qkv_sems)
    for copy in copies:
        copy.wait()
    grad[:ALL_TXT, :] = dot(text[...], weight[0].reshape(D, COLS)).astype(jnp.bfloat16)
    grad[ALL_TXT:, :] = dot(image[...], weight[1].reshape(D, COLS)).astype(jnp.bfloat16)
    head_backward(0, joint, grad, att, lse, probs, slopes, out_ref)


def second_kernel(x_ref, grad, att, lse, out_ref, joint, probs, slopes, qkv_sems):
    for copy in load_qkv(x_ref, joint, qkv_sems):
        copy.wait()
    head_backward(1, joint, grad, att, lse, probs, slopes, out_ref)


ANY = pl.BlockSpec(memory_space=pl.ANY)
VMEM = pl.BlockSpec(memory_space=pltpu.VMEM)
BLOCKS = jax.ShapeDtypeStruct((SP, 3, TOK, HD), jnp.bfloat16)
JOINT = pltpu.VMEM((3, LENGTH, COLS), jnp.bfloat16)
SQUARE = pltpu.VMEM((LENGTH, LENGTH), jnp.bfloat16)
BACK_FLOPS = 10 * LENGTH * LENGTH * HD


def backward_first(place, pieces, w, x, att, lse):
    return pl.pallas_call(
        first_kernel,
        out_shape=(BLOCKS, jax.ShapeDtypeStruct((LENGTH, COLS), jnp.bfloat16)),
        in_specs=[pl.BlockSpec(memory_space=pltpu.SMEM)] + [ANY] * (SP + 2) + [VMEM] * 2,
        out_specs=(VMEM, VMEM),
        scratch_shapes=[
            pltpu.VMEM((ALL_TXT, D), jnp.bfloat16),
            pltpu.VMEM((SP * IMG, D), jnp.bfloat16),
            pltpu.VMEM((2, 2, 16, 2, ROWS, COLS), jnp.bfloat16),
            JOINT,
            SQUARE,
            SQUARE,
            pltpu.SemaphoreType.DMA((2 * SP,)),
            pltpu.SemaphoreType.DMA((2 * SP,)),
            pltpu.SemaphoreType.DMA((4,)),
        ],
        compiler_params=pltpu.CompilerParams(vmem_limit_bytes=VMEM_LIMIT),
        cost_estimate=pl.CostEstimate(
            flops=BACK_FLOPS + 2 * LENGTH * D * COLS,
            bytes_accessed=LENGTH * D * 2 + 2 * D * COLS * 2 + 5 * LENGTH * COLS * 2,
            transcendentals=LENGTH * LENGTH,
        ),
        name="backward_first_head",
    )(place, *pieces, w, x, att, lse)


def backward_second(x, grad, att, lse):
    return pl.pallas_call(
        second_kernel,
        out_shape=BLOCKS,
        in_specs=[ANY] + [VMEM] * 3,
        out_specs=VMEM,
        scratch_shapes=[JOINT, SQUARE, SQUARE, pltpu.SemaphoreType.DMA((2 * SP,))],
        compiler_params=pltpu.CompilerParams(vmem_limit_bytes=VMEM_LIMIT),
        cost_estimate=pl.CostEstimate(
            flops=BACK_FLOPS,
            bytes_accessed=6 * LENGTH * COLS * 2,
            transcendentals=LENGTH * LENGTH,
        ),
        name="backward_second_head",
    )(x, grad, att, lse)


def gather_weights(wv_txt, sc_txt, wv_img, sc_img, core, x_lo):
    own = jnp.stack([dequant(wv_txt, sc_txt), dequant(wv_img, sc_img)])
    other = send(own, SWAP_CORE)
    pair = jnp.where(core == 0, jnp.stack([own, other]), jnp.stack([other, own]))
    other = send(pair, SWAP_X_LO)
    four = jnp.where(x_lo == 0, jnp.stack([pair, other]), jnp.stack([other, pair]))
    return lax.all_gather(four, AXES, axis=0, axis_index_groups=Z_GROUPS)


def sum_over_samples(keep, give):
    near = keep.astype(jnp.float32) + send(give, SWAP_CORE).astype(jnp.float32)
    far = send(near[1].astype(jnp.bfloat16), SWAP_X_LO)
    four = (near[0] + far.astype(jnp.float32)).astype(jnp.bfloat16)
    parts = lax.all_to_all(four, AXES, 0, 0, axis_index_groups=Z_GROUPS, tiled=True)
    return jnp.sum(parts.astype(jnp.float32), axis=0) * (1.0 / 64)


def local(qkv_txt, qkv_img, dy_txt, dy_img, wv_txt, sc_txt, wv_img, sc_img):
    fsdp, sp = lax.axis_index("fsdp"), lax.axis_index("sp")
    core, x_lo = fsdp % 2, fsdp // 32
    place = jnp.stack(slots(sp) + [core, x_lo]).astype(jnp.int32)

    w = gather_weights(wv_txt, sc_txt, wv_img, sc_img, core, x_lo)

    own = jnp.concatenate([dy_txt[0], dy_img[0]], axis=0)
    other = send(own, SWAP_X_HI)
    pieces = (
        [own]
        + [send(own, FROM_Y[k]) for k in (1, 2, 3)]
        + [other]
        + [send(other, FROM_Y[k]) for k in (1, 2, 3)]
    )

    x = jnp.concatenate(
        [qkv_txt[0].reshape(3, TXT, SP, COLS), qkv_img[0].reshape(3, IMG, SP, COLS)], axis=1
    ).transpose(2, 0, 1, 3)
    x = lax.all_to_all(x, "sp", 0, 0, tiled=True)

    att, lse = forward(x)
    keep, give = weight_term(place, pieces, att)
    weight_grad = sum_over_samples(keep, give)

    first, grad = backward_first(place, pieces, w, x, att, lse)
    second = backward_second(x, grad, att, lse)
    back = jnp.stack(
        [lax.all_to_all(part, "sp", 0, 0, tiled=True) for part in (first, second)], axis=3
    )
    back = back.transpose(1, 2, 0, 3, 4).reshape(1, 3, TOK, SP * COLS)
    return (back[:, :, :TXT], back[:, :, TXT:], weight_grad)


def solution(mesh):
    placed = (
        P("fsdp", None, "sp", None),
        P("fsdp", None, "sp", None),
        P("fsdp", "sp", None),
        P("fsdp", "sp", None),
        P("fsdp", "sp"),
        P("fsdp", "sp"),
        P("fsdp", "sp"),
        P("fsdp", "sp"),
    )
    return jax.shard_map(
        local,
        mesh=mesh,
        in_specs=placed,
        out_specs=(P("fsdp", None, "sp", None), P("fsdp", None, "sp", None), P("fsdp", "sp")),
        check_vma=False,
    )
```

time: 670 us -> 229 us (0.34)
  the two profiles are of different devices: /device:TPU:8 before, /device:TPU:32 now
where the time goes in v1:
time: 229 us; the launch traced here: 228 us
  waiting for transfers between devices  105 us (46%)
  starting transfers between devices  69.1 us (30%)
  Pallas kernels  26.8 us (12%)
  between operations  14.5 us (6%)
  local copies, waits for them, and re-layouts  6.92 us (3%)
  other arithmetic  5.88 us (3%)
    ppermute x11, waiting for transfers between devices, send(): return lax.ppermute(x, AXES, pairs)  49.9 us
    ppermute x11, starting transfers between devices, send(): return lax.ppermute(x, AXES, pairs)  39.4 us
    all_to_all x1, waiting for transfers between devices, local(): x = lax.all_to_all(x, 'sp', 0, 0, tiled=True)  25.2 us
    all_to_all x2, waiting for transfers between devices, local(): lax.all_to_all(part, 'sp', 0, 0, tiled=True)  19.6 us
    all_to_all x1, starting transfers between devices, sum_over_samples(): lax.all_to_all(four, AXES, 0, 0, axis_index_groups=Z_GROUPS, tiled=True)  15.2 us
    pallas_call x1, Pallas kernels, backward_first(): pl.pallas_call(first_kernel, out_shape=(BLOCKS, jax.ShapeDtypeStruct((LEN...  11 us
    all_to_all x1, waiting for transfers between devices, sum_over_samples(): lax.all_to_all(four, AXES, 0, 0, axis_index_groups=Z_GROUPS, tiled=True)  10.5 us
    all_to_all x2, starting transfers between devices, local(): lax.all_to_all(part, 'sp', 0, 0, tiled=True)  10.3 us
  transfers between devices with their start and end apart: 16, of which 13 were waited for; matrix products, arithmetic and copies ran while one was open for 2% of the time, Pallas kernels for 12%

profile of v1, /device:TPU:32, one launch (start us, length us, event | category | flops | bytes accessed | tf_op | source)
XLA Modules:
  0.0 228.5 jit_solution(17458678211584331728)
XLA Ops:
  7.2 0.8 copy.20
  8.1 0.8 copy.21
  8.9 0.1 broadcast_in_dim.7
  9.1 0.8 fusion.6
  9.9 1.9 collective-permute-start.7
  11.8 1.2 collective-permute-done.7
  13.0 3.4 %collective-permute-start.8 = (bf16[2,2,48,256]{3,2,1,0:T(8,128)(2,1)S(1)}, bf16[2,2,48,256]{3,2,1,0:T(8,128)(2,1)S(1)}, u32[]{:S(2)}, u32[]{:S(2)}) collective-permute-start(bf16[2,2,48,256]{3,2,1,0:T(8,128)(2,1)S(1)} %maximum_select_fusion.2), channel_id=1, source_target_pairs={{0,256},{1,257},{2,258},{3,259},{4,260},{5,261},{6,262},{7,263},{8... | collective-permute-start | bytes 294920 | tf_op jit(solution)/shard_map/ppermute | solution.py:66
  16.4 3.3 %collective-permute-done.8 = bf16[2,2,48,256]{3,2,1,0:T(8,128)(2,1)S(1)} collective-permute-done((bf16[2,2,48,256]{3,2,1,0:T(8,128)(2,1)S(1)}, bf16[2,2,48,256]{3,2,1,0:T(8,128)(2,1)S(1)}, u32[]{:S(2)}, u32[]{:S(2)}) %collective-permute-start.8) | collective-permute-done | bytes 98336 | tf_op jit(solution)/shard_map/ppermute | solution.py:66
  19.7 0.7 maximum_select_fusion
  20.6 5.1 %collective-permute-start.3 = (bf16[128,3072]{1,0:T(8,128)(2,1)S(1)}, bf16[128,3072]{1,0:T(8,128)(2,1)S(1)}, u32[]{:S(2)}, u32[]{:S(2)}) collective-permute-start(bf16[128,3072]{1,0:T(8,128)(2,1)S(1)} %pad_maximum_fusion.refs_0_), channel_id=1, source_target_pairs={{0,1},{1,0},{2,3},{3,2},{4,5},{5,4},{6,7},{7,6},{8,9},{9,8},{10,11... | collective-permute-start | bytes 2359304 | tf_op jit(solution)/shard_map/ppermute | solution.py:66
  25.6 3.5 %collective-permute-start.2 = (bf16[128,3072]{1,0:T(8,128)(2,1)S(1)}, bf16[128,3072]{1,0:T(8,128)(2,1)}, u32[]{:S(2)}, u32[]{:S(2)}) collective-permute-start(bf16[128,3072]{1,0:T(8,128)(2,1)S(1)} %pad_maximum_fusion.refs_0_), channel_id=1, source_target_pairs={{0,2},{1,3},{2,4},{3,5},{4,6},{5,7},{6,0},{7,1},{8,10},{9,11},{10,... | collective-permute-start | bytes 2359304 | tf_op jit(solution)/shard_map/ppermute | solution.py:66
  29.3 0.3 copy.30
  29.7 0.3 copy.23
  30.0 1.3 maximum_bitcast_fusion
  31.2 4.2 %all-to-all-start = ((bf16[8,3,128,256]{3,2,1,0:T(8,128)(2,1)}), bf16[8,3,128,256]{3,2,1,0:T(8,128)(2,1)S(1)}, u32[]{:S(2)}, u32[]{:S(2)}) async-start(bf16[8,3,128,256]{3,2,1,0:T(8,128)(2,1)} %maximum_bitcast_fusion), calls=%async_computation | async-start | bytes 3145728 | tf_op jit(solution)/shard_map/all_to_all | solution.py:376
  35.4 5.4 %collective-permute-start.1 = (bf16[128,3072]{1,0:T(8,128)(2,1)S(1)}, bf16[128,3072]{1,0:T(8,128)(2,1)}, u32[]{:S(2)}, u32[]{:S(2)}) collective-permute-start(bf16[128,3072]{1,0:T(8,128)(2,1)S(1)} %pad_maximum_fusion.refs_0_), channel_id=1, source_target_pairs={{0,4},{1,5},{2,6},{3,7},{4,0},{5,1},{6,2},{7,3},{8,12},{9,13},{10,... | collective-permute-start | bytes 2359304 | tf_op jit(solution)/shard_map/ppermute | solution.py:66
  40.8 3.1 %collective-permute-start = (bf16[128,3072]{1,0:T(8,128)(2,1)S(1)}, bf16[128,3072]{1,0:T(8,128)(2,1)}, u32[]{:S(2)}, u32[]{:S(2)}) collective-permute-start(bf16[128,3072]{1,0:T(8,128)(2,1)S(1)} %pad_maximum_fusion.refs_0_), channel_id=1, source_target_pairs={{0,6},{1,7},{2,0},{3,1},{4,2},{5,3},{6,4},{7,5},{8,14},{9,15},{10,... | collective-permute-start | bytes 2359304 | tf_op jit(solution)/shard_map/ppermute | solution.py:66
  43.9 0.7 collective-permute-done.3.refs_4_
  44.6 3.5 %collective-permute-start.6 = (bf16[128,3072]{1,0:T(8,128)(2,1)S(1)}, bf16[128,3072]{1,0:T(8,128)(2,1)}, u32[]{:S(2)}, u32[]{:S(2)}) collective-permute-start(bf16[128,3072]{1,0:T(8,128)(2,1)S(1)} %collective-permute-done.3.refs_4_), channel_id=1, source_target_pairs={{0,2},{1,3},{2,4},{3,5},{4,6},{5,7},{6,0},{7,1},{8,10},{9,11},{10,... | collective-permute-start | bytes 2359304 | tf_op jit(solution)/shard_map/ppermute | solution.py:66
  48.1 4.8 %collective-permute-start.5 = (bf16[128,3072]{1,0:T(8,128)(2,1)S(1)}, bf16[128,3072]{1,0:T(8,128)(2,1)}, u32[]{:S(2)}, u32[]{:S(2)}) collective-permute-start(bf16[128,3072]{1,0:T(8,128)(2,1)S(1)} %collective-permute-done.3.refs_4_), channel_id=1, source_target_pairs={{0,4},{1,5},{2,6},{3,7},{4,0},{5,1},{6,2},{7,3},{8,12},{9,13},{10,... | collective-permute-start | bytes 2359304 | tf_op jit(solution)/shard_map/ppermute | solution.py:66
  52.9 3.4 %collective-permute-start.4 = (bf16[128,3072]{1,0:T(8,128)(2,1)S(1)}, bf16[128,3072]{1,0:T(8,128)(2,1)}, u32[]{:S(2)}, u32[]{:S(2)}) collective-permute-start(bf16[128,3072]{1,0:T(8,128)(2,1)S(1)} %collective-permute-done.3.refs_4_), channel_id=1, source_target_pairs={{0,6},{1,7},{2,0},{3,1},{4,2},{5,3},{6,4},{7,5},{8,14},{9,15},{10,... | collective-permute-start | bytes 2359304 | tf_op jit(solution)/shard_map/ppermute | solution.py:66
  56.5 25.2 %all-to-all-done.x_ref.refs_9_ = bf16[8,3,128,256]{3,2,1,0:T(8,128)(2,1)S(1)} async-done(((bf16[8,3,128,256]{3,2,1,0:T(8,128)(2,1)}), bf16[8,3,128,256]{3,2,1,0:T(8,128)(2,1)S(1)}, u32[]{:S(2)}, u32[]{:S(2)}) %all-to-all-start) | async-done | bytes 1572896 | tf_op jit(solution)/shard_map/all_to_all | solution.py:376
  81.7 6.7 %attention_forward.1 = (bf16[1024,256]{1,0:T(8,128)(2,1)S(1)}, f32[2,1024]{1,0:T(2,128)S(1)}) custom-call(bf16[8,3,128,256]{3,2,1,0:T(8,128)(2,1)S(1)} %all-to-all-done.x_ref.refs_9_), custom_call_target="tpu_custom_call" | custom-call | flops 1073741824 | bytes 2097152 | tf_op jit(solution)/shard_map/attention_forward/pallas_call | solution.py:126
  88.4 1.5 collective-permute-done.refs_1_
  90.0 8.8 %collective-permute-done.6.refs_7_ = bf16[128,3072]{1,0:T(8,128)(2,1)} collective-permute-done((bf16[128,3072]{1,0:T(8,128)(2,1)S(1)}, bf16[128,3072]{1,0:T(8,128)(2,1)}, u32[]{:S(2)}, u32[]{:S(2)}) %collective-permute-start.6) | collective-permute-done | bytes 786464 | tf_op jit(solution)/shard_map/ppermute | solution.py:66
  98.8 17.2 %collective-permute-done.5.refs_6_ = bf16[128,3072]{1,0:T(8,128)(2,1)} collective-permute-done((bf16[128,3072]{1,0:T(8,128)(2,1)S(1)}, bf16[128,3072]{1,0:T(8,128)(2,1)}, u32[]{:S(2)}, u32[]{:S(2)}) %collective-permute-start.5) | collective-permute-done | bytes 786464 | tf_op jit(solution)/shard_map/ppermute | solution.py:66
  116.0 5.2 %collective-permute-done.4.refs_5_ = bf16[128,3072]{1,0:T(8,128)(2,1)} collective-permute-done((bf16[128,3072]{1,0:T(8,128)(2,1)S(1)}, bf16[128,3072]{1,0:T(8,128)(2,1)}, u32[]{:S(2)}, u32[]{:S(2)}) %collective-permute-start.4) | collective-permute-done | bytes 786464 | tf_op jit(solution)/shard_map/ppermute | solution.py:66
  121.2 4.3 %weight_term.1 = (bf16[2,16,48,256]{3,2,1,0:T(8,128)(2,1)S(1)}, bf16[2,16,48,256]{3,2,1,0:T(8,128)(2,1)S(1)}) custom-call(s32[10]{0:T(128)S(1)} %stack.97.place_ref, bf16[128,3072]{1,0:T(8,128)(2,1)S(1)} %pad_maximum_fusion.refs_0_, bf16[128,3072]{1,0:T(8,128)(2,1)} %collective-permute-done.refs_1_, bf16[128,3072]{1,0:T(8,128)(2,1)} %collective-permute-done.1.refs_2_, ...), custom_call_target="tpu_custom_call" | custom-call | flops 1207959552 | bytes 6291456 | tf_op jit(solution)/shard_map/weight_term/pallas_call | solution.py:205
  125.5 1.9 collective-permute-start.9
  127.4 2.3 collective-permute-done.9
  129.7 0.2 convert_add_fusion
  130.0 3.5 %collective-permute-start.10 = (bf16[16,48,256]{2,1,0:T(8,128)(2,1)S(1)}, bf16[16,48,256]{2,1,0:T(8,128)(2,1)S(1)}, u32[]{:S(2)}, u32[]{:S(2)}) collective-permute-start(bf16[16,48,256]{2,1,0:T(8,128)(2,1)S(1)} %fusion.2), channel_id=1, source_target_pairs={{0,256},{1,257},{2,258},{3,259},{4,260},{5,261},{6,262},{7,263},{8... | collective-permute-start | bytes 1179656 | tf_op jit(solution)/shard_map/ppermute | solution.py:66
  133.4 9.7 %collective-permute-done.10 = bf16[16,48,256]{2,1,0:T(8,128)(2,1)S(1)} collective-permute-done((bf16[16,48,256]{2,1,0:T(8,128)(2,1)S(1)}, bf16[16,48,256]{2,1,0:T(8,128)(2,1)S(1)}, u32[]{:S(2)}, u32[]{:S(2)}) %collective-permute-start.10) | collective-permute-done | bytes 393248 | tf_op jit(solution)/shard_map/ppermute | solution.py:66
  143.2 0.8 fusion.1
  144.0 15.2 %all-to-all-start.3 = ((bf16[16,48,256]{2,1,0:T(8,128)(2,1)}), bf16[16,48,256]{2,1,0:T(8,128)(2,1)S(1)}, u32[]{:S(2)}, u32[]{:S(2)}) async-start(bf16[16,48,256]{2,1,0:T(8,128)(2,1)} %fusion.1), calls=%async_computation.3 | async-start | bytes 786432 | tf_op jit(solution)/shard_map/all_to_all | solution.py:353
  159.3 11.0 %backward_first_head.1 = (bf16[8,3,128,128]{3,2,1,0:T(8,128)(2,1)}, bf16[1024,256]{1,0:T(8,128)(2,1)S(1)}) custom-call(s32[10]{0:T(128)S(1)} %stack.97.place_ref, bf16[128,3072]{1,0:T(8,128)(2,1)S(1)} %pad_maximum_fusion.refs_0_, bf16[128,3072]{1,0:T(8,128)(2,1)} %collective-permute-done.refs_1_, bf16[128,3072]{1,0:T(8,128)(2,1)} %collective-permute-done.1.refs_2_, ...), custom_call_target="tpu_custom_call" | custom-call | flops 2952790016 | bytes 12058624 | tf_op jit(solution)/shard_map/backward_first_head/pallas_call | solution.py:297
  170.3 10.5 %all-to-all-done.3 = bf16[16,48,256]{2,1,0:T(8,128)(2,1)S(1)} async-done(((bf16[16,48,256]{2,1,0:T(8,128)(2,1)}), bf16[16,48,256]{2,1,0:T(8,128)(2,1)S(1)}, u32[]{:S(2)}, u32[]{:S(2)}) %all-to-all-start.3) | async-done | bytes 393248 | tf_op jit(solution)/shard_map/all_to_all | solution.py:353
  180.8 6.7 %all-to-all-start.1 = ((bf16[8,3,128,128]{3,2,1,0:T(8,128)(2,1)}), bf16[8,3,128,128]{3,2,1,0:T(8,128)(2,1)}, u32[]{:S(2)}, u32[]{:S(2)}) async-start(bf16[8,3,128,128]{3,2,1,0:T(8,128)(2,1)} %get-tuple-element.11), calls=%async_computation.1 | async-start | bytes 1572864 | tf_op jit(solution)/shard_map/all_to_all | solution.py:385
  187.6 4.8 %backward_second_head.1 = bf16[8,3,128,128]{3,2,1,0:T(8,128)(2,1)} custom-call(bf16[8,3,128,256]{3,2,1,0:T(8,128)(2,1)S(1)} %copy-done.1, bf16[1024,256]{1,0:T(8,128)(2,1)S(1)} %get-tuple-element.12.grad, bf16[1024,256]{1,0:T(8,128)(2,1)S(1)} %copy-done.3, f32[2,1024]{1,0:T(2,128)S(1)} %get-tuple-element.10.refs_11_.lse), custom_call_target="tpu_custom_call" | custom-call | flops 1342177280 | bytes 3145728 | tf_op jit(solution)/shard_map/backward_second_head/pallas_call | solution.py:324
  192.3 8.2 %all-to-all-done.1 = bf16[8,3,128,128]{3,2,1,0:T(8,128)(2,1)} async-done(((bf16[8,3,128,128]{3,2,1,0:T(8,128)(2,1)}), bf16[8,3,128,128]{3,2,1,0:T(8,128)(2,1)}, u32[]{:S(2)}, u32[]{:S(2)}) %all-to-all-start.1) | async-done | bytes 786464 | tf_op jit(solution)/shard_map/all_to_all | solution.py:385
  200.6 3.5 %all-to-all-start.2 = ((bf16[8,3,128,128]{3,2,1,0:T(8,128)(2,1)}), bf16[8,3,128,128]{3,2,1,0:T(8,128)(2,1)S(1)}, u32[]{:S(2)}, u32[]{:S(2)}) async-start(bf16[8,3,128,128]{3,2,1,0:T(8,128)(2,1)} %backward_second_head.1), calls=%async_computation.2 | async-start | bytes 1572864 | tf_op jit(solution)/shard_map/all_to_all | solution.py:385
  204.2 0.6 broadcast_multiply_fusion
  204.8 11.4 %all-to-all-done.2 = bf16[8,3,128,128]{3,2,1,0:T(8,128)(2,1)S(1)} async-done(((bf16[8,3,128,128]{3,2,1,0:T(8,128)(2,1)}), bf16[8,3,128,128]{3,2,1,0:T(8,128)(2,1)S(1)}, u32[]{:S(2)}, u32[]{:S(2)}) %all-to-all-start.2) | async-done | bytes 786464 | tf_op jit(solution)/shard_map/all_to_all | solution.py:385
  216.2 1.3 maximum_bitcast_fusion.1
  217.5 0.9 copy.24
  218.4 0.5 slice.18
  218.9 1.3 copy.25
  220.2 1.5 copy.26
  (31 shorter events, 0.7 us)
Async XLA Ops:
  7.2 13.3 %copy-start.5 = (bf16[1,96,3072]{2,1,0:T(8,128)(2,1)S(1)}, bf16[1,96,3072]{2,1,0:T(8,128)(2,1)}, u32[]{:S(2)}) copy-start(bf16[1,96,3072]{2,1,0:T(8,128)(2,1)} %param.11) | copy-start | bytes 1769476
  7.2 13.3 %copy-start.7 = (bf16[1,32,3072]{2,1,0:T(8,128)(2,1)S(1)}, bf16[1,32,3072]{2,1,0:T(8,128)(2,1)}, u32[]{:S(2)}) copy-start(bf16[1,32,3072]{2,1,0:T(8,128)(2,1)} %param.10) | copy-start | bytes 589828
  7.2 152.0 %all-gather.2.cloned.1.call-start = ((), (), s32[]{:S(2)}) async-start(), calls=%async_computation.4 | async-start | bytes 3342336 | tf_op jit(solution)/shard_map/all_gather | solution.py:346
  8.9 20.2 %copy-start.6 = (bf16[1,3,32,2048]{3,2,1,0:T(8,128)(2,1)S(1)}, bf16[1,3,32,2048]{3,2,1,0:T(8,128)(2,1)}, u32[]{:S(2)}) copy-start(bf16[1,3,32,2048]{3,2,1,0:T(8,128)(2,1)} %param.8) | copy-start | bytes 1179652
  9.9 3.1 %collective-permute-start.7 = (bf16[2,48,256]{2,1,0:T(8,128)(2,1)S(1)}, bf16[2,48,256]{2,1,0:T(8,128)(2,1)S(1)}, u32[]{:S(2)}, u32[]{:S(2)}) collective-permute-start(bf16[2,48,256]{2,1,0:T(8,128)(2,1)S(1)} %get-tuple-element.23), channel_id=1, source_target_pairs={{0,8},{1,9},{2,10},{3,11},{4,12},{5,13},{6,14},{7,15},{8,0},{9,1},... | collective-permute-start | bytes 147464 | tf_op jit(solution)/shard_map/ppermute | solution.py:66
  13.0 6.8 %collective-permute-start.8 = (bf16[2,2,48,256]{3,2,1,0:T(8,128)(2,1)S(1)}, bf16[2,2,48,256]{3,2,1,0:T(8,128)(2,1)S(1)}, u32[]{:S(2)}, u32[]{:S(2)}) collective-permute-start(bf16[2,2,48,256]{3,2,1,0:T(8,128)(2,1)S(1)} %maximum_select_fusion.2), channel_id=1, source_target_pairs={{0,256},{1,257},{2,258},{3,259},{4,260},{5,261},{6,262},{7,263},{8... | collective-permute-start | bytes 294920 | tf_op jit(solution)/shard_map/ppermute | solution.py:66
  20.5 8.8 %copy-start.4 = (bf16[1,3,96,2048]{3,2,1,0:T(8,128)(2,1)S(1)}, bf16[1,3,96,2048]{3,2,1,0:T(8,128)(2,1)}, u32[]{:S(2)}) copy-start(bf16[1,3,96,2048]{3,2,1,0:T(8,128)(2,1)} %param.9) | copy-start | bytes 3538948
  20.6 24.0 %collective-permute-start.3 = (bf16[128,3072]{1,0:T(8,128)(2,1)S(1)}, bf16[128,3072]{1,0:T(8,128)(2,1)S(1)}, u32[]{:S(2)}, u32[]{:S(2)}) collective-permute-start(bf16[128,3072]{1,0:T(8,128)(2,1)S(1)} %pad_maximum_fusion.refs_0_), channel_id=1, source_target_pairs={{0,1},{1,0},{2,3},{3,2},{4,5},{5,4},{6,7},{7,6},{8,9},{9,8},{10,11... | collective-permute-start | bytes 2359304 | tf_op jit(solution)/shard_map/ppermute | solution.py:66
  25.6 27.2 %collective-permute-start.2 = (bf16[128,3072]{1,0:T(8,128)(2,1)S(1)}, bf16[128,3072]{1,0:T(8,128)(2,1)}, u32[]{:S(2)}, u32[]{:S(2)}) collective-permute-start(bf16[128,3072]{1,0:T(8,128)(2,1)S(1)} %pad_maximum_fusion.refs_0_), channel_id=1, source_target_pairs={{0,2},{1,3},{2,4},{3,5},{4,6},{5,7},{6,0},{7,1},{8,10},{9,11},{10,... | collective-permute-start | bytes 2359304 | tf_op jit(solution)/shard_map/ppermute | solution.py:66
  31.2 50.5 %all-to-all-start = ((bf16[8,3,128,256]{3,2,1,0:T(8,128)(2,1)}), bf16[8,3,128,256]{3,2,1,0:T(8,128)(2,1)S(1)}, u32[]{:S(2)}, u32[]{:S(2)}) async-start(bf16[8,3,128,256]{3,2,1,0:T(8,128)(2,1)} %maximum_bitcast_fusion), calls=%async_computation | async-start | bytes 3145728 | tf_op jit(solution)/shard_map/all_to_all | solution.py:376
  35.4 53.0 %collective-permute-start.1 = (bf16[128,3072]{1,0:T(8,128)(2,1)S(1)}, bf16[128,3072]{1,0:T(8,128)(2,1)}, u32[]{:S(2)}, u32[]{:S(2)}) collective-permute-start(bf16[128,3072]{1,0:T(8,128)(2,1)S(1)} %pad_maximum_fusion.refs_0_), channel_id=1, source_target_pairs={{0,4},{1,5},{2,6},{3,7},{4,0},{5,1},{6,2},{7,3},{8,12},{9,13},{10,... | collective-permute-start | bytes 2359304 | tf_op jit(solution)/shard_map/ppermute | solution.py:66
  40.8 49.1 %collective-permute-start = (bf16[128,3072]{1,0:T(8,128)(2,1)S(1)}, bf16[128,3072]{1,0:T(8,128)(2,1)}, u32[]{:S(2)}, u32[]{:S(2)}) collective-permute-start(bf16[128,3072]{1,0:T(8,128)(2,1)S(1)} %pad_maximum_fusion.refs_0_), channel_id=1, source_target_pairs={{0,6},{1,7},{2,0},{3,1},{4,2},{5,3},{6,4},{7,5},{8,14},{9,15},{10,... | collective-permute-start | bytes 2359304 | tf_op jit(solution)/shard_map/ppermute | solution.py:66
  44.6 54.2 %collective-permute-start.6 = (bf16[128,3072]{1,0:T(8,128)(2,1)S(1)}, bf16[128,3072]{1,0:T(8,128)(2,1)}, u32[]{:S(2)}, u32[]{:S(2)}) collective-permute-start(bf16[128,3072]{1,0:T(8,128)(2,1)S(1)} %collective-permute-done.3.refs_4_), channel_id=1, source_target_pairs={{0,2},{1,3},{2,4},{3,5},{4,6},{5,7},{6,0},{7,1},{8,10},{9,11},{10,... | collective-permute-start | bytes 2359304 | tf_op jit(solution)/shard_map/ppermute | solution.py:66
  48.1 67.9 %collective-permute-start.5 = (bf16[128,3072]{1,0:T(8,128)(2,1)S(1)}, bf16[128,3072]{1,0:T(8,128)(2,1)}, u32[]{:S(2)}, u32[]{:S(2)}) collective-permute-start(bf16[128,3072]{1,0:T(8,128)(2,1)S(1)} %collective-permute-done.3.refs_4_), channel_id=1, source_target_pairs={{0,4},{1,5},{2,6},{3,7},{4,0},{5,1},{6,2},{7,3},{8,12},{9,13},{10,... | collective-permute-start | bytes 2359304 | tf_op jit(solution)/shard_map/ppermute | solution.py:66
  52.9 68.3 %collective-permute-start.4 = (bf16[128,3072]{1,0:T(8,128)(2,1)S(1)}, bf16[128,3072]{1,0:T(8,128)(2,1)}, u32[]{:S(2)}, u32[]{:S(2)}) collective-permute-start(bf16[128,3072]{1,0:T(8,128)(2,1)S(1)} %collective-permute-done.3.refs_4_), channel_id=1, source_target_pairs={{0,6},{1,7},{2,0},{3,1},{4,2},{5,3},{6,4},{7,5},{8,14},{9,15},{10,... | collective-permute-start | bytes 2359304 | tf_op jit(solution)/shard_map/ppermute | solution.py:66
  81.7 6.7 %copy-start = (bf16[8,3,128,256]{3,2,1,0:T(8,128)(2,1)}, bf16[8,3,128,256]{3,2,1,0:T(8,128)(2,1)S(1)}, u32[]{:S(2)}) copy-start(bf16[8,3,128,256]{3,2,1,0:T(8,128)(2,1)S(1)} %all-to-all-done.x_ref.refs_9_) | copy-start | bytes 4718596
  88.4 37.1 %copy-start.2 = (bf16[1024,256]{1,0:T(8,128)(2,1)}, bf16[1024,256]{1,0:T(8,128)(2,1)S(1)}, u32[]{:S(2)}) copy-start(bf16[1024,256]{1,0:T(8,128)(2,1)S(1)} %get-tuple-element.9.refs_10_.att.refs_8_) | copy-start | bytes 1572868
  125.5 4.2 %collective-permute-start.9 = (bf16[2,16,48,256]{3,2,1,0:T(8,128)(2,1)S(1)}, bf16[2,16,48,256]{3,2,1,0:T(8,128)(2,1)S(1)}, u32[]{:S(2)}, u32[]{:S(2)}) collective-permute-start(bf16[2,16,48,256]{3,2,1,0:T(8,128)(2,1)S(1)} %get-tuple-element.14), channel_id=1, source_target_pairs={{0,8},{1,9},{2,10},{3,11},{4,12},{5,13},{6,14},{7,15},{8,0},{9,1},... | collective-permute-start | bytes 2359304 | tf_op jit(solution)/shard_map/ppermute | solution.py:66
  129.9 29.3 %copy-start.3 = (bf16[1024,256]{1,0:T(8,128)(2,1)S(1)}, bf16[1024,256]{1,0:T(8,128)(2,1)}, u32[]{:S(2)}) copy-start(bf16[1024,256]{1,0:T(8,128)(2,1)} %copy-done.2) | copy-start | bytes 1572868
  130.0 13.2 %collective-permute-start.10 = (bf16[16,48,256]{2,1,0:T(8,128)(2,1)S(1)}, bf16[16,48,256]{2,1,0:T(8,128)(2,1)S(1)}, u32[]{:S(2)}, u32[]{:S(2)}) collective-permute-start(bf16[16,48,256]{2,1,0:T(8,128)(2,1)S(1)} %fusion.2), channel_id=1, source_target_pairs={{0,256},{1,257},{2,258},{3,259},{4,260},{5,261},{6,262},{7,263},{8... | collective-permute-start | bytes 1179656 | tf_op jit(solution)/shard_map/ppermute | solution.py:66
  144.0 36.8 %all-to-all-start.3 = ((bf16[16,48,256]{2,1,0:T(8,128)(2,1)}), bf16[16,48,256]{2,1,0:T(8,128)(2,1)S(1)}, u32[]{:S(2)}, u32[]{:S(2)}) async-start(bf16[16,48,256]{2,1,0:T(8,128)(2,1)} %fusion.1), calls=%async_computation.3 | async-start | bytes 786432 | tf_op jit(solution)/shard_map/all_to_all | solution.py:353
  170.3 17.3 %copy-start.1 = (bf16[8,3,128,256]{3,2,1,0:T(8,128)(2,1)S(1)}, bf16[8,3,128,256]{3,2,1,0:T(8,128)(2,1)}, u32[]{:S(2)}) copy-start(bf16[8,3,128,256]{3,2,1,0:T(8,128)(2,1)} %copy-done) | copy-start | bytes 4718596
  180.8 19.8 %all-to-all-start.1 = ((bf16[8,3,128,128]{3,2,1,0:T(8,128)(2,1)}), bf16[8,3,128,128]{3,2,1,0:T(8,128)(2,1)}, u32[]{:S(2)}, u32[]{:S(2)}) async-start(bf16[8,3,128,128]{3,2,1,0:T(8,128)(2,1)} %get-tuple-element.11), calls=%async_computation.1 | async-start | bytes 1572864 | tf_op jit(solution)/shard_map/all_to_all | solution.py:385
  200.6 15.6 %all-to-all-start.2 = ((bf16[8,3,128,128]{3,2,1,0:T(8,128)(2,1)}), bf16[8,3,128,128]{3,2,1,0:T(8,128)(2,1)S(1)}, u32[]{:S(2)}, u32[]{:S(2)}) async-start(bf16[8,3,128,128]{3,2,1,0:T(8,128)(2,1)} %backward_second_head.1), calls=%async_computation.2 | async-start | bytes 1572864 | tf_op jit(solution)/shard_map/all_to_all | solution.py:385
Sparse Core Ops, SparseCore 0:
  20.6 80.1 all-gather.1

commit v2 on v1

v2 whole, which is shorter than its diff:
```python
import functools
import math

import jax
import jax.numpy as jnp
from jax import lax
from jax.experimental import pallas as pl
from jax.experimental.pallas import tpu as pltpu
from jax.sharding import PartitionSpec as P

HD = 128
SP = 8
TXT = 32
IMG = 96
TOK = TXT + IMG
ALL_TXT = SP * TXT
ALL_IMG = SP * IMG
LENGTH = SP * TOK
COLS = 256
D = 3072
ROWS = 48
HEADS = COLS // HD
CHUNK = 256
FACTOR = 1.0 / math.sqrt(HD)
LOG2E = 1.4426950408889634
SCALE2 = FACTOR * LOG2E
AXES = ("fsdp", "sp")
VMEM_LIMIT = 48 * 1024 * 1024
LIGHT = pl.CostEstimate(flops=1000, bytes_accessed=1000, transcendentals=0)


def number(x_lo, z, core, y, x_hi):
    return ((x_lo * 16 + z) * 2 + core) * SP + y * 2 + x_hi


def every():
    return [
        (x_lo, z, core, y, x_hi)
        for x_lo in range(2)
        for z in range(16)
        for core in range(2)
        for y in range(4)
        for x_hi in range(2)
    ]


def route(target):
    return [(number(*d), number(*target(*d))) for d in every()]


SWAP_CORE = route(lambda x_lo, z, core, y, x_hi: (x_lo, z, 1 - core, y, x_hi))
SWAP_X_LO = route(lambda x_lo, z, core, y, x_hi: (1 - x_lo, z, core, y, x_hi))
SWAP_X_HI = route(lambda x_lo, z, core, y, x_hi: (x_lo, z, core, y, 1 - x_hi))
FROM_Y = {
    k: route(lambda x_lo, z, core, y, x_hi, k=k: (x_lo, z, core, (y - k) % 4, x_hi))
    for k in (1, 2, 3)
}
TO_Z = {
    k: route(lambda x_lo, z, core, y, x_hi, d=d: (x_lo, (z + d) % 16, core, y, x_hi))
    for k, d in ((4, 4), (8, 8), (12, -4))
}
Z_NEAR_GROUPS = [
    [number(x_lo, 4 * quad + z, core, y, x_hi) for z in range(4)]
    for x_lo in range(2)
    for quad in range(4)
    for core in range(2)
    for y in range(4)
    for x_hi in range(2)
]
Z_CORE_GROUPS = [
    [number(x_lo, z, core, y, x_hi) for z in range(16) for core in range(2)]
    for x_lo in range(2)
    for y in range(4)
    for x_hi in range(2)
]


def send(x, pairs):
    return lax.ppermute(x, AXES, pairs)


def dequant(values, scales):
    return (values.astype(jnp.float32) * jnp.repeat(scales, HD, axis=1)).astype(jnp.bfloat16)


def plus(a, b):
    return a.astype(jnp.float32) + b.astype(jnp.float32)


def dot(a, b):
    return jnp.dot(a, b, preferred_element_type=jnp.float32)


def dot_last(a, b):
    return lax.dot_general(a, b, (((1,), (1,)), ((), ())), preferred_element_type=jnp.float32)


def transposed(x):
    return x.astype(jnp.float32).T


def load_qkv(x_ref, joint, sems):
    copies = []
    for r in range(SP):
        copies.append(
            pltpu.make_async_copy(
                x_ref.at[r, :, pl.ds(0, TXT), :],
                joint.at[:, pl.ds(r * TXT, TXT), :],
                sems.at[2 * r],
            )
        )
        copies.append(
            pltpu.make_async_copy(
                x_ref.at[r, :, pl.ds(TXT, IMG), :],
                joint.at[:, pl.ds(ALL_TXT + r * IMG, IMG), :],
                sems.at[2 * r + 1],
            )
        )
    for copy in copies:
        copy.start()
    return copies


def forward_kernel(x_ref, att_ref, probs_ref, joint, sems):
    for copy in load_qkv(x_ref, joint, sems):
        copy.wait()
    for head in range(HEADS):
        window = slice(head * HD, (head + 1) * HD)
        keys = joint[1, :, window]
        values_t = transposed(joint[2, :, window]).astype(jnp.bfloat16)
        for chunk in range(LENGTH // CHUNK):
            rows = slice(chunk * CHUNK, (chunk + 1) * CHUNK)
            scores = dot_last(keys, joint[0, rows, window])
            highest = jnp.max(scores, axis=0, keepdims=True)
            weights = jnp.exp2((scores - highest) * SCALE2)
            share = 1.0 / jnp.sum(weights, axis=0, keepdims=True)
            probs = (weights * share).astype(jnp.bfloat16)
            probs_ref[head, :, rows] = probs
            att_ref[rows, window] = dot(values_t, probs).T.astype(jnp.bfloat16)


def forward(x):
    return pl.pallas_call(
        forward_kernel,
        out_shape=(
            jax.ShapeDtypeStruct((LENGTH, COLS), jnp.bfloat16),
            jax.ShapeDtypeStruct((HEADS, LENGTH, LENGTH), jnp.bfloat16),
        ),
        in_specs=[pl.BlockSpec(memory_space=pl.ANY)],
        out_specs=(
            pl.BlockSpec(memory_space=pltpu.VMEM),
            pl.BlockSpec(memory_space=pltpu.VMEM),
        ),
        scratch_shapes=[
            pltpu.VMEM((3, LENGTH, COLS), jnp.bfloat16),
            pltpu.SemaphoreType.DMA((2 * SP,)),
        ],
        compiler_params=pltpu.CompilerParams(vmem_limit_bytes=VMEM_LIMIT),
        cost_estimate=LIGHT,
        name="attention_forward",
    )(x)


def slots(sp):
    y, x_hi = sp // 2, sp % 2
    return [((y + k) % 4) * 2 + x_hi for k in range(4)] + [
        ((y + k) % 4) * 2 + 1 - x_hi for k in range(4)
    ]


def load_dy(place_ref, pieces, text, image, sems):
    copies = []
    parts = [(image, TXT, IMG)] + ([(text, 0, TXT)] if text is not None else [])
    for part, (target, row, size) in enumerate(parts):
        for n, piece in enumerate(pieces):
            first = pl.multiple_of(place_ref[n] * size, TXT)
            copies.append(
                pltpu.make_async_copy(
                    piece.at[pl.ds(row, size), :],
                    target.at[pl.ds(first, size), :],
                    sems.at[part * SP + n],
                )
            )
    for copy in copies:
        copy.start()
    return copies


BAND = 8 * 2 * ROWS


def term_kernel(place_ref, *refs):
    pieces, (att_ref, keep_ref, give_ref, image, sems) = refs[:SP], refs[SP:]
    copies = load_dy(place_ref, pieces, None, image, sems)
    att_t = transposed(att_ref[ALL_TXT:, :]).astype(jnp.bfloat16)
    for copy in copies:
        copy.wait()
    core, x_lo = place_ref[SP], place_ref[SP + 1]
    for band in range(D // BAND):
        term = dot(att_t, image[:, band * BAND : (band + 1) * BAND]).T.astype(jnp.bfloat16)
        far = (x_lo + band // 2) % 2
        for j in range(8):
            z = (band % 2) * 8 + j
            low = term[(2 * j) * ROWS : (2 * j + 1) * ROWS]
            high = term[(2 * j + 1) * ROWS : (2 * j + 2) * ROWS]
            keep_ref[far, z % 4, z // 4] = jnp.where(core == 0, low, high)
            give_ref[far, z % 4, z // 4] = jnp.where(core == 0, high, low)


def weight_term(place, pieces, att):
    half = jax.ShapeDtypeStruct((2, 4, 4, ROWS, COLS), jnp.bfloat16)
    return pl.pallas_call(
        term_kernel,
        out_shape=(half, half),
        in_specs=[pl.BlockSpec(memory_space=pltpu.SMEM)]
        + [pl.BlockSpec(memory_space=pl.ANY)] * SP
        + [pl.BlockSpec(memory_space=pltpu.VMEM)],
        out_specs=(
            pl.BlockSpec(memory_space=pltpu.VMEM),
            pl.BlockSpec(memory_space=pltpu.VMEM),
        ),
        scratch_shapes=[
            pltpu.VMEM((SP * IMG, D), jnp.bfloat16),
            pltpu.SemaphoreType.DMA((SP,)),
        ],
        compiler_params=pltpu.CompilerParams(vmem_limit_bytes=VMEM_LIMIT),
        cost_estimate=LIGHT,
        name="weight_term",
    )(place, *pieces, att)


def head_backward(window, joint, grad, att, probs, slopes, out_ref, out_window):
    keys, values = joint[1, :, window], joint[2, :, window]
    keys_t = transposed(keys).astype(jnp.bfloat16)

    def put(member, first, block):
        for r in range(SP):
            lo, hi = r * TXT - first, (r + 1) * TXT - first
            if 0 <= lo < block.shape[0]:
                out_ref[r, member, :TXT, out_window] = block[lo:hi]
            lo, hi = ALL_TXT + r * IMG - first, ALL_TXT + (r + 1) * IMG - first
            start, stop = max(lo, 0), min(hi, block.shape[0])
            if start < stop:
                rows = slice(TXT + start - lo, TXT + stop - lo)
                out_ref[r, member, rows, out_window] = block[start:stop]

    for chunk in range(LENGTH // CHUNK):
        rows = slice(chunk * CHUNK, (chunk + 1) * CHUNK)
        out_grad = grad[rows]
        product = out_grad.astype(jnp.float32) * att[rows].astype(jnp.float32)
        delta = jnp.sum(product.T, axis=0, keepdims=True)
        change = dot_last(values, out_grad) - delta
        slope = (probs[:, rows].astype(jnp.float32) * change).astype(jnp.bfloat16)
        slopes[:, rows] = slope
        put(0, chunk * CHUNK, (dot(keys_t, slope) * FACTOR).T.astype(jnp.bfloat16))
    put(1, 0, (dot(slopes[...], joint[0, :, window]) * FACTOR).astype(jnp.bfloat16))
    put(2, 0, dot(probs[...], grad[...]).astype(jnp.bfloat16))


def first_kernel(place_ref, *refs):
    pieces, rest = refs[:SP], refs[SP:]
    w_ref, x_ref, probs_ref, att, out_ref, other_ref = rest[:6]
    grad, text, image, weight, joint, probs, slopes, sems, dy_sems, qkv_sems = rest[6:]
    copies = [
        pltpu.make_async_copy(
            w_ref.at[:, x_lo, stream], weight.at[stream, x_lo], sems.at[2 * stream + x_lo]
        )
        for stream in range(2)
        for x_lo in range(2)
    ]
    for copy in copies[2:]:
        copy.start()
    dy_copies = load_dy(place_ref, pieces, text, image, dy_sems)
    for copy in copies[:2]:
        copy.start()
    late = load_qkv(x_ref, joint, qkv_sems)
    late.append(pltpu.make_async_copy(probs_ref.at[0], probs, sems.at[4]))
    late[-1].start()
    for copy in copies[2:] + dy_copies[:SP]:
        copy.wait()
    both = dot(image[...], weight[1].reshape(D, COLS)).astype(jnp.bfloat16)
    grad[ALL_TXT:, :] = both[:, :HD]
    other_ref[ALL_TXT:, :] = both[:, HD:]
    for copy in copies[:2] + dy_copies[SP:]:
        copy.wait()
    both = dot(text[...], weight[0].reshape(D, COLS)).astype(jnp.bfloat16)
    grad[:ALL_TXT, :] = both[:, :HD]
    other_ref[:ALL_TXT, :] = both[:, HD:]
    for copy in late:
        copy.wait()
    head_backward(slice(0, HD), joint, grad, att[:, :HD], probs, slopes, out_ref, slice(0, HD))


def second_kernel(x_ref, probs_ref, first_ref, grad, att, out_ref, *rest):
    joint, probs, slopes, sems, qkv_sems = rest
    copies = load_qkv(x_ref, joint, qkv_sems)
    copies.append(pltpu.make_async_copy(probs_ref.at[1], probs, sems.at[0]))
    copies[-1].start()
    out_ref[:, :, :, :HD] = first_ref[...]
    for copy in copies:
        copy.wait()
    window = slice(HD, COLS)
    head_backward(window, joint, grad, att[:, HD:], probs, slopes, out_ref, window)


ANY = pl.BlockSpec(memory_space=pl.ANY)
VMEM = pl.BlockSpec(memory_space=pltpu.VMEM)


def backward_first(place, pieces, w, x, probs, att):
    return pl.pallas_call(
        first_kernel,
        out_shape=(
            jax.ShapeDtypeStruct((SP, 3, TOK, HD), jnp.bfloat16),
            jax.ShapeDtypeStruct((LENGTH, HD), jnp.bfloat16),
        ),
        in_specs=[pl.BlockSpec(memory_space=pltpu.SMEM)] + [ANY] * (SP + 3) + [VMEM],
        out_specs=(VMEM, VMEM),
        scratch_shapes=[
            pltpu.VMEM((LENGTH, HD), jnp.bfloat16),
            pltpu.VMEM((ALL_TXT, D), jnp.bfloat16),
            pltpu.VMEM((ALL_IMG, D), jnp.bfloat16),
            pltpu.VMEM((2, 2, 32, ROWS, COLS), jnp.bfloat16),
            pltpu.VMEM((3, LENGTH, COLS), jnp.bfloat16),
            pltpu.VMEM((LENGTH, LENGTH), jnp.bfloat16),
            pltpu.VMEM((LENGTH, LENGTH), jnp.bfloat16),
            pltpu.SemaphoreType.DMA((5,)),
            pltpu.SemaphoreType.DMA((2 * SP,)),
            pltpu.SemaphoreType.DMA((2 * SP,)),
        ],
        compiler_params=pltpu.CompilerParams(vmem_limit_bytes=VMEM_LIMIT),
        cost_estimate=LIGHT,
        name="project_and_backward_first_head",
    )(place, *pieces, w, x, probs, att)


def backward_second(x, probs, first, grad, att):
    return pl.pallas_call(
        second_kernel,
        out_shape=jax.ShapeDtypeStruct((SP, 3, TOK, COLS), jnp.bfloat16),
        in_specs=[ANY] * 2 + [VMEM] * 3,
        out_specs=VMEM,
        scratch_shapes=[
            pltpu.VMEM((3, LENGTH, COLS), jnp.bfloat16),
            pltpu.VMEM((LENGTH, LENGTH), jnp.bfloat16),
            pltpu.VMEM((LENGTH, LENGTH), jnp.bfloat16),
            pltpu.SemaphoreType.DMA((1,)),
            pltpu.SemaphoreType.DMA((2 * SP,)),
        ],
        compiler_params=pltpu.CompilerParams(vmem_limit_bytes=VMEM_LIMIT),
        cost_estimate=LIGHT,
        name="backward_second_head",
    )(x, probs, first, grad, att)


def spread_kernel(back_ref, txt_ref, img_ref):
    for r in range(SP):
        columns = slice(r * COLS, (r + 1) * COLS)
        txt_ref[0, :, :, columns] = back_ref[r, :, :TXT, :]
        img_ref[0, :, :, columns] = back_ref[r, :, TXT:, :]


def spread(back):
    return pl.pallas_call(
        spread_kernel,
        out_shape=(
            jax.ShapeDtypeStruct((1, 3, TXT, SP * COLS), jnp.bfloat16),
            jax.ShapeDtypeStruct((1, 3, IMG, SP * COLS), jnp.bfloat16),
        ),
        in_specs=[VMEM],
        out_specs=(VMEM, VMEM),
        compiler_params=pltpu.CompilerParams(vmem_limit_bytes=VMEM_LIMIT),
        cost_estimate=LIGHT,
        name="spread_features",
    )(back)


def gather_weights(wv_txt, sc_txt, wv_img, sc_img, x_lo):
    own = jnp.stack([dequant(wv_txt, sc_txt), dequant(wv_img, sc_img)])
    other = send(own, SWAP_X_LO)
    pair = jnp.where(x_lo == 0, jnp.stack([own, other]), jnp.stack([other, own]))
    return lax.all_gather(pair, AXES, axis=0, axis_index_groups=Z_CORE_GROUPS)


def local(qkv_txt, qkv_img, dy_txt, dy_img, wv_txt, sc_txt, wv_img, sc_img):
    fsdp, sp = lax.axis_index("fsdp"), lax.axis_index("sp")
    core, x_lo, z = fsdp % 2, fsdp // 32, (fsdp // 2) % 16
    place = jnp.stack(slots(sp) + [core, x_lo]).astype(jnp.int32)

    own = jnp.concatenate([dy_txt[0], dy_img[0]], axis=0)
    by_y = {k: send(own, FROM_Y[k]) for k in (1, 2, 3)}
    across = send(own, SWAP_X_HI)

    x = jnp.concatenate(
        [qkv_txt[0].reshape(3, TXT, SP, COLS), qkv_img[0].reshape(3, IMG, SP, COLS)], axis=1
    ).transpose(2, 0, 1, 3)
    x, wv_txt, wv_img = lax.optimization_barrier((x, wv_txt, wv_img))
    w = gather_weights(wv_txt, sc_txt, wv_img, sc_img, x_lo)
    x = lax.all_to_all(x, "sp", 0, 0, tiled=True)
    att, probs = forward(x)

    pieces = [own, by_y[1], by_y[2], by_y[3]] + [
        across,
        send(across, FROM_Y[1]),
        send(by_y[2], SWAP_X_HI),
        send(across, FROM_Y[3]),
    ]
    keep, give = weight_term(place, pieces, att)

    other = send(give, SWAP_CORE)
    other, att = lax.optimization_barrier((other, att))
    far = send(plus(keep[1], other[1]).astype(jnp.bfloat16), SWAP_X_LO)
    first, grad = backward_first(place, pieces, w, x, probs, att)
    first, far = lax.optimization_barrier((first, far))
    part = plus(plus(keep[0], other[0]), far).astype(jnp.bfloat16)
    quads = lax.all_to_all(part, AXES, 0, 0, axis_index_groups=Z_NEAR_GROUPS, tiled=True)
    quads = jnp.sum(quads.astype(jnp.float32), axis=0).astype(jnp.bfloat16)
    back = backward_second(x, probs, first, grad, att)
    back, quads = lax.optimization_barrier((back, quads))
    back = lax.all_to_all(back, "sp", 0, 0, tiled=True)

    def quad(step):
        return lax.dynamic_index_in_dim(quads, (z // 4 + step) % 4, 0, keepdims=False)

    weight_grad = quad(0).astype(jnp.float32)
    for step in (1, 3, 2):
        weight_grad = weight_grad + send(quad(step), TO_Z[4 * step]).astype(jnp.float32)
    return (*spread(back), weight_grad * (1.0 / 64))


def solution(mesh):
    placed = (
        P("fsdp", None, "sp", None),
        P("fsdp", None, "sp", None),
        P("fsdp", "sp", None),
        P("fsdp", "sp", None),
        P("fsdp", "sp"),
        P("fsdp", "sp"),
        P("fsdp", "sp"),
        P("fsdp", "sp"),
    )
    return jax.shard_map(
        local,
        mesh=mesh,
        in_specs=placed,
        out_specs=(P("fsdp", None, "sp", None), P("fsdp", None, "sp", None), P("fsdp", "sp")),
        check_vma=False,
    )
```

time: 229 us -> 181 us (0.79)
  the two profiles are of different devices: /device:TPU:32 before, /device:TPU:4 now
where the time goes in v2:
time: 181 us
  starting transfers between devices  78 us (43%)
  waiting for transfers between devices  47.1 us (26%)
  Pallas kernels  31.6 us (17%)
  between operations  14.5 us (8%)
  local copies, waits for them, and re-layouts  4.67 us (3%)
  other arithmetic  4.58 us (3%)
    ppermute x13, starting transfers between devices, send(): return lax.ppermute(x, AXES, pairs)  57.9 us
    ppermute x13, waiting for transfers between devices, send(): return lax.ppermute(x, AXES, pairs)  35.7 us
    pallas_call x1, Pallas kernels, backward_first(): pl.pallas_call(first_kernel, out_shape=(jax.ShapeDtypeStruct((SP, 3, TOK,...  10 us
    pallas_call x1, Pallas kernels, forward(): pl.pallas_call(forward_kernel, out_shape=(jax.ShapeDtypeStruct((LENGTH, C...  9.25 us
    all_to_all x1, starting transfers between devices, local(): x = lax.all_to_all(x, 'sp', 0, 0, tiled=True)  7.77 us
    all_to_all x1, starting transfers between devices, local(): back = lax.all_to_all(back, 'sp', 0, 0, tiled=True)  7.04 us
    pallas_call x1, Pallas kernels, backward_second(): pl.pallas_call(second_kernel, out_shape=jax.ShapeDtypeStruct((SP, 3, TOK,...  6.57 us
    all_to_all x1, waiting for transfers between devices, local(): x = lax.all_to_all(x, 'sp', 0, 0, tiled=True)  6.22 us
  transfers between devices with their start and end apart: 17, of which 11 were waited for; matrix products, arithmetic and copies ran while one was open for 1% of the time, Pallas kernels for 17%

profile of v2, /device:TPU:4, one launch (start us, length us, event | category | flops | bytes accessed | tf_op | source)
XLA Modules:
  0.0 180.5 jit_solution(12860242700866006150)
XLA Ops:
  7.2 0.9 copy.19
  8.1 0.8 copy.20
  8.8 1.1 copy.21
  9.9 0.1 copy.17
  10.0 0.4 copy.22
  10.4 0.3 copy.18
  10.7 1.3 maximum_bitcast_fusion
  12.0 0.1 broadcast_in_dim.6
  12.1 0.1 broadcast_in_dim.7
  12.3 3.1 %collective-permute-start.7 = (bf16[2,48,256]{2,1,0:T(8,128)(2,1)S(1)}, bf16[2,48,256]{2,1,0:T(8,128)(2,1)S(1)}, u32[]{:S(2)}, u32[]{:S(2)}) collective-permute-start(bf16[2,48,256]{2,1,0:T(8,128)(2,1)S(1)} %get-tuple-element.41), channel_id=1, source_target_pairs={{0,256},{1,257},{2,258},{3,259},{4,260},{5,261},{6,262},{7,263},{8... | collective-permute-start | bytes 147464 | tf_op jit(solution)/shard_map/ppermute | solution.py:79
  15.4 2.9 %collective-permute-done.7 = bf16[2,48,256]{2,1,0:T(8,128)(2,1)S(1)} collective-permute-done((bf16[2,48,256]{2,1,0:T(8,128)(2,1)S(1)}, bf16[2,48,256]{2,1,0:T(8,128)(2,1)S(1)}, u32[]{:S(2)}, u32[]{:S(2)}) %collective-permute-start.7) | collective-permute-done | bytes 49184 | tf_op jit(solution)/shard_map/ppermute | solution.py:79
  18.3 0.7 maximum_select_fusion
  19.0 7.8 %collective-permute-start.3 = (bf16[128,3072]{1,0:T(8,128)(2,1)S(1)}, bf16[128,3072]{1,0:T(8,128)(2,1)}, u32[]{:S(2)}, u32[]{:S(2)}) collective-permute-start(bf16[128,3072]{1,0:T(8,128)(2,1)S(1)} %pad_maximum_fusion.refs_0_), channel_id=1, source_target_pairs={{0,1},{1,0},{2,3},{3,2},{4,5},{5,4},{6,7},{7,6},{8,9},{9,8},{10,11... | collective-permute-start | bytes 2359304 | tf_op jit(solution)/shard_map/ppermute | solution.py:79
  26.8 1.9 %collective-permute-start.1 = (bf16[128,3072]{1,0:T(8,128)(2,1)S(1)}, bf16[128,3072]{1,0:T(8,128)(2,1)}, u32[]{:S(2)}, u32[]{:S(2)}) collective-permute-start(bf16[128,3072]{1,0:T(8,128)(2,1)S(1)} %pad_maximum_fusion.refs_0_), channel_id=1, source_target_pairs={{0,4},{1,5},{2,6},{3,7},{4,0},{5,1},{6,2},{7,3},{8,12},{9,13},{10,... | collective-permute-start | bytes 2359304 | tf_op jit(solution)/shard_map/ppermute | solution.py:79
  28.7 7.8 %all-to-all-start = ((bf16[8,3,128,256]{3,2,1,0:T(8,128)(2,1)}), bf16[8,3,128,256]{3,2,1,0:T(8,128)(2,1)S(1)}, u32[]{:S(2)}, u32[]{:S(2)}) async-start(bf16[8,3,128,256]{3,2,1,0:T(8,128)(2,1)} %maximum_bitcast_fusion), calls=%async_computation | async-start | bytes 3145728 | tf_op jit(solution)/shard_map/all_to_all | solution.py:399
  36.5 3.4 %collective-permute-start.2 = (bf16[128,3072]{1,0:T(8,128)(2,1)S(1)}, bf16[128,3072]{1,0:T(8,128)(2,1)}, u32[]{:S(2)}, u32[]{:S(2)}) collective-permute-start(bf16[128,3072]{1,0:T(8,128)(2,1)S(1)} %pad_maximum_fusion.refs_0_), channel_id=1, source_target_pairs={{0,2},{1,3},{2,4},{3,5},{4,6},{5,7},{6,0},{7,1},{8,10},{9,11},{10,... | collective-permute-start | bytes 2359304 | tf_op jit(solution)/shard_map/ppermute | solution.py:79
  39.9 3.7 %collective-permute-start = (bf16[128,3072]{1,0:T(8,128)(2,1)S(1)}, bf16[128,3072]{1,0:T(8,128)(2,1)}, u32[]{:S(2)}, u32[]{:S(2)}) collective-permute-start(bf16[128,3072]{1,0:T(8,128)(2,1)S(1)} %pad_maximum_fusion.refs_0_), channel_id=1, source_target_pairs={{0,6},{1,7},{2,0},{3,1},{4,2},{5,3},{6,4},{7,5},{8,14},{9,15},{10,... | collective-permute-start | bytes 2359304 | tf_op jit(solution)/shard_map/ppermute | solution.py:79
  43.6 1.8 collective-permute-done.3.refs_4_
  45.4 1.9 %collective-permute-start.6 = (bf16[128,3072]{1,0:T(8,128)(2,1)}, bf16[128,3072]{1,0:T(8,128)(2,1)}, u32[]{:S(2)}, u32[]{:S(2)}) collective-permute-start(bf16[128,3072]{1,0:T(8,128)(2,1)} %collective-permute-done.3.refs_4_), channel_id=1, source_target_pairs={{0,2},{1,3},{2,4},{3,5},{4,6},{5,7},{6,0},{7,1},{8,10},{9,11},{10,... | collective-permute-start | bytes 2359304 | tf_op jit(solution)/shard_map/ppermute | solution.py:79
  47.3 5.1 %collective-permute-start.4 = (bf16[128,3072]{1,0:T(8,128)(2,1)}, bf16[128,3072]{1,0:T(8,128)(2,1)}, u32[]{:S(2)}, u32[]{:S(2)}) collective-permute-start(bf16[128,3072]{1,0:T(8,128)(2,1)} %collective-permute-done.3.refs_4_), channel_id=1, source_target_pairs={{0,6},{1,7},{2,0},{3,1},{4,2},{5,3},{6,4},{7,5},{8,14},{9,15},{10,... | collective-permute-start | bytes 2359304 | tf_op jit(solution)/shard_map/ppermute | solution.py:79
  52.4 6.4 %collective-permute-done.1.refs_2_ = bf16[128,3072]{1,0:T(8,128)(2,1)} collective-permute-done((bf16[128,3072]{1,0:T(8,128)(2,1)S(1)}, bf16[128,3072]{1,0:T(8,128)(2,1)}, u32[]{:S(2)}, u32[]{:S(2)}) %collective-permute-start.1) | collective-permute-done | bytes 786464 | tf_op jit(solution)/shard_map/ppermute | solution.py:79
  58.8 1.9 %collective-permute-start.5 = (bf16[128,3072]{1,0:T(8,128)(2,1)}, bf16[128,3072]{1,0:T(8,128)(2,1)}, u32[]{:S(2)}, u32[]{:S(2)}) collective-permute-start(bf16[128,3072]{1,0:T(8,128)(2,1)} %collective-permute-done.1.refs_2_), channel_id=1, source_target_pairs={{0,1},{1,0},{2,3},{3,2},{4,5},{5,4},{6,7},{7,6},{8,9},{9,8},{10,11... | collective-permute-start | bytes 2359304 | tf_op jit(solution)/shard_map/ppermute | solution.py:79
  60.9 0.1 stack.66.place_ref
  60.9 6.2 %all-to-all-done.x_ref.refs_9_ = bf16[8,3,128,256]{3,2,1,0:T(8,128)(2,1)S(1)} async-done(((bf16[8,3,128,256]{3,2,1,0:T(8,128)(2,1)}), bf16[8,3,128,256]{3,2,1,0:T(8,128)(2,1)S(1)}, u32[]{:S(2)}, u32[]{:S(2)}) %all-to-all-start) | async-done | bytes 1572896 | tf_op jit(solution)/shard_map/all_to_all | solution.py:399
  67.2 9.3 %attention_forward.1 = (bf16[1024,256]{1,0:T(8,128)(2,1)S(1)}, bf16[2,1024,1024]{2,1,0:T(8,128)(2,1)}) custom-call(bf16[8,3,128,256]{3,2,1,0:T(8,128)(2,1)S(1)} %all-to-all-done.x_ref.refs_9_), custom_call_target="tpu_custom_call" | custom-call | flops 1000 | bytes 1000 | tf_op jit(solution)/shard_map/attention_forward/pallas_call | solution.py:143
  76.4 5.5 %collective-permute-done.2.refs_3_ = bf16[128,3072]{1,0:T(8,128)(2,1)} collective-permute-done((bf16[128,3072]{1,0:T(8,128)(2,1)S(1)}, bf16[128,3072]{1,0:T(8,128)(2,1)}, u32[]{:S(2)}, u32[]{:S(2)}) %collective-permute-start.2) | collective-permute-done | bytes 786464 | tf_op jit(solution)/shard_map/ppermute | solution.py:79
  81.9 12.1 %collective-permute-done.6.refs_7_ = bf16[128,3072]{1,0:T(8,128)(2,1)} collective-permute-done((bf16[128,3072]{1,0:T(8,128)(2,1)}, bf16[128,3072]{1,0:T(8,128)(2,1)}, u32[]{:S(2)}, u32[]{:S(2)}) %collective-permute-start.6) | collective-permute-done | bytes 786464 | tf_op jit(solution)/shard_map/ppermute | solution.py:79
  94.1 0.6 collective-permute-done.4.refs_5_
  94.7 4.4 %weight_term.1 = (bf16[2,4,4,48,256]{4,3,2,1,0:T(8,128)(2,1)S(1)}, bf16[2,4,4,48,256]{4,3,2,1,0:T(8,128)(2,1)S(1)}) custom-call(s32[10]{0:T(128)S(1)} %stack.66.place_ref, bf16[128,3072]{1,0:T(8,128)(2,1)S(1)} %pad_maximum_fusion.refs_0_, bf16[128,3072]{1,0:T(8,128)(2,1)} %collective-permute-done.refs_1_, bf16[128,3072]{1,0:T(8,128)(2,1)} %collective-permute-done.1.refs_2_, ...), custom_call_target="tpu_custom_call" | custom-call | flops 1000 | bytes 1000 | tf_op jit(solution)/shard_map/weight_term/pallas_call | solution.py:212
  99.1 1.9 %collective-permute-start.8 = (bf16[2,4,4,48,256]{4,3,2,1,0:T(8,128)(2,1)S(1)}, bf16[2,4,4,48,256]{4,3,2,1,0:T(8,128)(2,1)S(1)}, u32[]{:S(2)}, u32[]{:S(2)}) collective-permute-start(bf16[2,4,4,48,256]{4,3,2,1,0:T(8,128)(2,1)S(1)} %get-tuple-element.25), channel_id=1, source_target_pairs={{0,8},{1,9},{2,10},{3,11},{4,12},{5,13},{6,14},{7,15},{8,0},{9,1},... | collective-permute-start | bytes 2359304 | tf_op jit(solution)/shard_map/ppermute | solution.py:79
  101.0 2.3 %collective-permute-done.8 = bf16[2,4,4,48,256]{4,3,2,1,0:T(8,128)(2,1)S(1)} collective-permute-done((bf16[2,4,4,48,256]{4,3,2,1,0:T(8,128)(2,1)S(1)}, bf16[2,4,4,48,256]{4,3,2,1,0:T(8,128)(2,1)S(1)}, u32[]{:S(2)}, u32[]{:S(2)}) %collective-permute-start.8) | collective-permute-done | bytes 786464 | tf_op jit(solution)/shard_map/ppermute | solution.py:79
  103.3 0.9 fusion.1
  104.2 0.1 copy-done.7
  104.3 3.9 %collective-permute-start.9 = (bf16[4,4,48,256]{3,2,1,0:T(8,128)(2,1)}, bf16[4,4,48,256]{3,2,1,0:T(8,128)(2,1)S(1)}, u32[]{:S(2)}, u32[]{:S(2)}) collective-permute-start(bf16[4,4,48,256]{3,2,1,0:T(8,128)(2,1)} %fusion.1), channel_id=1, source_target_pairs={{0,256},{1,257},{2,258},{3,259},{4,260},{5,261},{6,262},{7,263},{8... | collective-permute-start | bytes 1179656 | tf_op jit(solution)/shard_map/ppermute | solution.py:79
  108.3 10.0 %project_and_backward_first_head.1 = (bf16[8,3,128,128]{3,2,1,0:T(8,128)(2,1)S(1)}, bf16[1024,128]{1,0:T(8,128)(2,1)S(1)}) custom-call(s32[10]{0:T(128)S(1)} %stack.66.place_ref, bf16[128,3072]{1,0:T(8,128)(2,1)S(1)} %pad_maximum_fusion.refs_0_, bf16[128,3072]{1,0:T(8,128)(2,1)} %collective-permute-done.refs_1_, ...), custom_call_target="tpu_custom_call" | custom-call | flops 1000 | bytes 1000 | tf_op jit(solution)/shard_map/project_and_backward_first_head/pallas_call | solution.py:311
  118.3 0.9 copy-done.2
  119.2 0.9 fusion
  120.1 5.3 %all-to-all-start.1 = ((bf16[4,4,48,256]{3,2,1,0:T(8,128)(2,1)}), bf16[4,4,48,256]{3,2,1,0:T(8,128)(2,1)S(1)}, u32[]{:S(2)}, u32[]{:S(2)}) async-start(bf16[4,4,48,256]{3,2,1,0:T(8,128)(2,1)} %fusion), calls=%async_computation.1 | async-start | bytes 786432 | tf_op jit(solution)/shard_map/all_to_all | solution.py:416
  125.4 6.6 %backward_second_head.1 = bf16[8,3,128,256]{3,2,1,0:T(8,128)(2,1)} custom-call(bf16[8,3,128,256]{3,2,1,0:T(8,128)(2,1)S(1)} %copy-done.1, bf16[2,1024,1024]{2,1,0:T(8,128)(2,1)} %get-tuple-element.21.refs_10_.probs_ref, bf16[8,3,128,128]{3,2,1,0:T(8,128)(2,1)S(1)} %copy-done.3, bf16[1024,128]{1,0:T(8,128)(2,1)S(1)} %get-tuple-element.31.grad, ...), custom_call_target="tpu_custom_call" | custom-call | flops 1000 | bytes 1000 | tf_op jit(solution)/shard_map/backward_second_head/pallas_call | solution.py:338
  132.0 5.1 %all-to-all-done.1 = bf16[4,4,48,256]{3,2,1,0:T(8,128)(2,1)S(1)} async-done(((bf16[4,4,48,256]{3,2,1,0:T(8,128)(2,1)}), bf16[4,4,48,256]{3,2,1,0:T(8,128)(2,1)S(1)}, u32[]{:S(2)}, u32[]{:S(2)}) %all-to-all-start.1) | async-done | bytes 393248 | tf_op jit(solution)/shard_map/all_to_all | solution.py:416
  137.2 7.0 %all-to-all-start.2 = ((bf16[8,3,128,256]{3,2,1,0:T(8,128)(2,1)}), bf16[8,3,128,256]{3,2,1,0:T(8,128)(2,1)S(1)}, u32[]{:S(2)}, u32[]{:S(2)}) async-start(bf16[8,3,128,256]{3,2,1,0:T(8,128)(2,1)} %backward_second_head.1), calls=%async_computation.2 | async-start | bytes 3145728 | tf_op jit(solution)/shard_map/all_to_all | solution.py:420
  144.2 9.1 %collective-permute-start.10 = (bf16[48,256]{1,0:T(8,128)(2,1)S(1)}, bf16[48,256]{1,0:T(8,128)(2,1)S(1)}, u32[]{:S(2)}, u32[]{:S(2)}) collective-permute-start(bf16[48,256]{1,0:T(8,128)(2,1)S(1)} %get-tuple-element.37), channel_id=1, source_target_pairs={{0,64},{1,65},{2,66},{3,67},{4,68},{5,69},{6,70},{7,71},{8,72},{9,... | collective-permute-start | bytes 73736 | tf_op jit(solution)/shard_map/ppermute | solution.py:79
  153.3 8.7 %collective-permute-start.12 = (bf16[48,256]{1,0:T(8,128)(2,1)S(1)}, bf16[48,256]{1,0:T(8,128)(2,1)S(1)}, u32[]{:S(2)}, u32[]{:S(2)}) collective-permute-start(bf16[48,256]{1,0:T(8,128)(2,1)S(1)} %get-tuple-element.38), channel_id=1, source_target_pairs={{0,128},{1,129},{2,130},{3,131},{4,132},{5,133},{6,134},{7,135},{8... | collective-permute-start | bytes 73736 | tf_op jit(solution)/shard_map/ppermute | solution.py:79
  162.1 5.5 %collective-permute-start.11 = (bf16[48,256]{1,0:T(8,128)(2,1)S(1)}, bf16[48,256]{1,0:T(8,128)(2,1)S(1)}, u32[]{:S(2)}, u32[]{:S(2)}) collective-permute-start(bf16[48,256]{1,0:T(8,128)(2,1)S(1)} %get-tuple-element.39), channel_id=1, source_target_pairs={{0,192},{1,193},{2,194},{3,195},{4,196},{5,197},{6,198},{7,199},{8... | collective-permute-start | bytes 73736 | tf_op jit(solution)/shard_map/ppermute | solution.py:79
  167.6 0.2 collective-permute-done.12
  167.8 3.9 %collective-permute-done.11 = bf16[48,256]{1,0:T(8,128)(2,1)S(1)} collective-permute-done((bf16[48,256]{1,0:T(8,128)(2,1)S(1)}, bf16[48,256]{1,0:T(8,128)(2,1)S(1)}, u32[]{:S(2)}, u32[]{:S(2)}) %collective-permute-start.11) | collective-permute-done | bytes 24608 | tf_op jit(solution)/shard_map/ppermute | solution.py:79
  171.7 0.6 fusion.6
  172.3 1.3 spread_features.1
  (37 shorter events, 0.3 us)
Async XLA Ops:
  7.2 2.8 %copy-start.6 = (bf16[1,3,96,2048]{3,2,1,0:T(8,128)(2,1)S(1)}, bf16[1,3,96,2048]{3,2,1,0:T(8,128)(2,1)}, u32[]{:S(2)}) copy-start(bf16[1,3,96,2048]{3,2,1,0:T(8,128)(2,1)} %param.9) | copy-start | bytes 3538948
  7.2 101.1 %all-gather.2.cloned.1.call-start = ((), (), s32[]{:S(2)}) async-start(), calls=%async_computation.3 | async-start | bytes 3244032 | tf_op jit(solution)/shard_map/all_gather | solution.py:382
  10.6 1.6 copy-start.11
  10.6 1.6 copy-start.12
  10.7 8.3 %copy-start.9 = (bf16[1,96,3072]{2,1,0:T(8,128)(2,1)S(1)}, bf16[1,96,3072]{2,1,0:T(8,128)(2,1)}, u32[]{:S(2)}) copy-start(bf16[1,96,3072]{2,1,0:T(8,128)(2,1)} %param.11) | copy-start | bytes 1769476
  10.7 8.3 %copy-start.10 = (bf16[1,32,3072]{2,1,0:T(8,128)(2,1)S(1)}, bf16[1,32,3072]{2,1,0:T(8,128)(2,1)}, u32[]{:S(2)}) copy-start(bf16[1,32,3072]{2,1,0:T(8,128)(2,1)} %param.10) | copy-start | bytes 589828
  12.3 6.0 %collective-permute-start.7 = (bf16[2,48,256]{2,1,0:T(8,128)(2,1)S(1)}, bf16[2,48,256]{2,1,0:T(8,128)(2,1)S(1)}, u32[]{:S(2)}, u32[]{:S(2)}) collective-permute-start(bf16[2,48,256]{2,1,0:T(8,128)(2,1)S(1)} %get-tuple-element.41), channel_id=1, source_target_pairs={{0,256},{1,257},{2,258},{3,259},{4,260},{5,261},{6,262},{7,263},{8... | collective-permute-start | bytes 147464 | tf_op jit(solution)/shard_map/ppermute | solution.py:79
  19.0 26.3 %collective-permute-start.3 = (bf16[128,3072]{1,0:T(8,128)(2,1)S(1)}, bf16[128,3072]{1,0:T(8,128)(2,1)}, u32[]{:S(2)}, u32[]{:S(2)}) collective-permute-start(bf16[128,3072]{1,0:T(8,128)(2,1)S(1)} %pad_maximum_fusion.refs_0_), channel_id=1, source_target_pairs={{0,1},{1,0},{2,3},{3,2},{4,5},{5,4},{6,7},{7,6},{8,9},{9,8},{10,11... | collective-permute-start | bytes 2359304 | tf_op jit(solution)/shard_map/ppermute | solution.py:79
  26.8 32.0 %collective-permute-start.1 = (bf16[128,3072]{1,0:T(8,128)(2,1)S(1)}, bf16[128,3072]{1,0:T(8,128)(2,1)}, u32[]{:S(2)}, u32[]{:S(2)}) collective-permute-start(bf16[128,3072]{1,0:T(8,128)(2,1)S(1)} %pad_maximum_fusion.refs_0_), channel_id=1, source_target_pairs={{0,4},{1,5},{2,6},{3,7},{4,0},{5,1},{6,2},{7,3},{8,12},{9,13},{10,... | collective-permute-start | bytes 2359304 | tf_op jit(solution)/shard_map/ppermute | solution.py:79
  28.7 38.4 %all-to-all-start = ((bf16[8,3,128,256]{3,2,1,0:T(8,128)(2,1)}), bf16[8,3,128,256]{3,2,1,0:T(8,128)(2,1)S(1)}, u32[]{:S(2)}, u32[]{:S(2)}) async-start(bf16[8,3,128,256]{3,2,1,0:T(8,128)(2,1)} %maximum_bitcast_fusion), calls=%async_computation | async-start | bytes 3145728 | tf_op jit(solution)/shard_map/all_to_all | solution.py:399
  36.5 45.4 %collective-permute-start.2 = (bf16[128,3072]{1,0:T(8,128)(2,1)S(1)}, bf16[128,3072]{1,0:T(8,128)(2,1)}, u32[]{:S(2)}, u32[]{:S(2)}) collective-permute-start(bf16[128,3072]{1,0:T(8,128)(2,1)S(1)} %pad_maximum_fusion.refs_0_), channel_id=1, source_target_pairs={{0,2},{1,3},{2,4},{3,5},{4,6},{5,7},{6,0},{7,1},{8,10},{9,11},{10,... | collective-permute-start | bytes 2359304 | tf_op jit(solution)/shard_map/ppermute | solution.py:79
  39.9 42.1 %collective-permute-start = (bf16[128,3072]{1,0:T(8,128)(2,1)S(1)}, bf16[128,3072]{1,0:T(8,128)(2,1)}, u32[]{:S(2)}, u32[]{:S(2)}) collective-permute-start(bf16[128,3072]{1,0:T(8,128)(2,1)S(1)} %pad_maximum_fusion.refs_0_), channel_id=1, source_target_pairs={{0,6},{1,7},{2,0},{3,1},{4,2},{5,3},{6,4},{7,5},{8,14},{9,15},{10,... | collective-permute-start | bytes 2359304 | tf_op jit(solution)/shard_map/ppermute | solution.py:79
  45.4 48.7 %collective-permute-start.6 = (bf16[128,3072]{1,0:T(8,128)(2,1)}, bf16[128,3072]{1,0:T(8,128)(2,1)}, u32[]{:S(2)}, u32[]{:S(2)}) collective-permute-start(bf16[128,3072]{1,0:T(8,128)(2,1)} %collective-permute-done.3.refs_4_), channel_id=1, source_target_pairs={{0,2},{1,3},{2,4},{3,5},{4,6},{5,7},{6,0},{7,1},{8,10},{9,11},{10,... | collective-permute-start | bytes 2359304 | tf_op jit(solution)/shard_map/ppermute | solution.py:79
  47.3 47.4 %collective-permute-start.4 = (bf16[128,3072]{1,0:T(8,128)(2,1)}, bf16[128,3072]{1,0:T(8,128)(2,1)}, u32[]{:S(2)}, u32[]{:S(2)}) collective-permute-start(bf16[128,3072]{1,0:T(8,128)(2,1)} %collective-permute-done.3.refs_4_), channel_id=1, source_target_pairs={{0,6},{1,7},{2,0},{3,1},{4,2},{5,3},{6,4},{7,5},{8,14},{9,15},{10,... | collective-permute-start | bytes 2359304 | tf_op jit(solution)/shard_map/ppermute | solution.py:79
  58.8 35.8 %collective-permute-start.5 = (bf16[128,3072]{1,0:T(8,128)(2,1)}, bf16[128,3072]{1,0:T(8,128)(2,1)}, u32[]{:S(2)}, u32[]{:S(2)}) collective-permute-start(bf16[128,3072]{1,0:T(8,128)(2,1)} %collective-permute-done.1.refs_2_), channel_id=1, source_target_pairs={{0,1},{1,0},{2,3},{3,2},{4,5},{5,4},{6,7},{7,6},{8,9},{9,8},{10,11... | collective-permute-start | bytes 2359304 | tf_op jit(solution)/shard_map/ppermute | solution.py:79
  67.2 31.9 %copy-start = (bf16[8,3,128,256]{3,2,1,0:T(8,128)(2,1)}, bf16[8,3,128,256]{3,2,1,0:T(8,128)(2,1)S(1)}, u32[]{:S(2)}) copy-start(bf16[8,3,128,256]{3,2,1,0:T(8,128)(2,1)S(1)} %all-to-all-done.x_ref.refs_9_) | copy-start | bytes 4718596
  99.1 4.2 %copy-start.4 = (bf16[2,4,4,48,256]{4,3,2,1,0:T(8,128)(2,1)}, bf16[2,4,4,48,256]{4,3,2,1,0:T(8,128)(2,1)S(1)}, u32[]{:S(2)}) copy-start(bf16[2,4,4,48,256]{4,3,2,1,0:T(8,128)(2,1)S(1)} %get-tuple-element.28) | copy-start | bytes 2359300
  99.1 4.2 %collective-permute-start.8 = (bf16[2,4,4,48,256]{4,3,2,1,0:T(8,128)(2,1)S(1)}, bf16[2,4,4,48,256]{4,3,2,1,0:T(8,128)(2,1)S(1)}, u32[]{:S(2)}, u32[]{:S(2)}) collective-permute-start(bf16[2,4,4,48,256]{4,3,2,1,0:T(8,128)(2,1)S(1)} %get-tuple-element.25), channel_id=1, source_target_pairs={{0,8},{1,9},{2,10},{3,11},{4,12},{5,13},{6,14},{7,15},{8,0},{9,1},... | collective-permute-start | bytes 2359304 | tf_op jit(solution)/shard_map/ppermute | solution.py:79
  103.3 1.0 copy-start.7
  104.3 14.9 %collective-permute-start.9 = (bf16[4,4,48,256]{3,2,1,0:T(8,128)(2,1)}, bf16[4,4,48,256]{3,2,1,0:T(8,128)(2,1)S(1)}, u32[]{:S(2)}, u32[]{:S(2)}) collective-permute-start(bf16[4,4,48,256]{3,2,1,0:T(8,128)(2,1)} %fusion.1), channel_id=1, source_target_pairs={{0,256},{1,257},{2,258},{3,259},{4,260},{5,261},{6,262},{7,263},{8... | collective-permute-start | bytes 1179656 | tf_op jit(solution)/shard_map/ppermute | solution.py:79
  108.3 11.0 %copy-start.5 = (bf16[2,4,4,48,256]{4,3,2,1,0:T(8,128)(2,1)S(1)}, bf16[2,4,4,48,256]{4,3,2,1,0:T(8,128)(2,1)}, u32[]{:S(2)}) copy-start(bf16[2,4,4,48,256]{4,3,2,1,0:T(8,128)(2,1)} %copy-done.4) | copy-start | bytes 2359300
  108.3 11.0 %copy-start.8 = (bf16[2,4,4,48,256]{4,3,2,1,0:T(8,128)(2,1)S(1)}, bf16[2,4,4,48,256]{4,3,2,1,0:T(8,128)(2,1)}, u32[]{:S(2)}) copy-start(bf16[2,4,4,48,256]{4,3,2,1,0:T(8,128)(2,1)} %copy-done.7) | copy-start | bytes 2359300
  118.3 0.9 copy-start.2
  119.2 6.2 %copy-start.1 = (bf16[8,3,128,256]{3,2,1,0:T(8,128)(2,1)S(1)}, bf16[8,3,128,256]{3,2,1,0:T(8,128)(2,1)}, u32[]{:S(2)}) copy-start(bf16[8,3,128,256]{3,2,1,0:T(8,128)(2,1)} %copy-done) | copy-start | bytes 4718596
  119.2 6.2 %copy-start.3 = (bf16[8,3,128,128]{3,2,1,0:T(8,128)(2,1)S(1)}, bf16[8,3,128,128]{3,2,1,0:T(8,128)(2,1)}, u32[]{:S(2)}) copy-start(bf16[8,3,128,128]{3,2,1,0:T(8,128)(2,1)} %copy-done.2) | copy-start | bytes 2359300
  120.1 17.0 %all-to-all-start.1 = ((bf16[4,4,48,256]{3,2,1,0:T(8,128)(2,1)}), bf16[4,4,48,256]{3,2,1,0:T(8,128)(2,1)S(1)}, u32[]{:S(2)}, u32[]{:S(2)}) async-start(bf16[4,4,48,256]{3,2,1,0:T(8,128)(2,1)} %fusion), calls=%async_computation.1 | async-start | bytes 786432 | tf_op jit(solution)/shard_map/all_to_all | solution.py:416
  137.2 35.2 %all-to-all-start.2 = ((bf16[8,3,128,256]{3,2,1,0:T(8,128)(2,1)}), bf16[8,3,128,256]{3,2,1,0:T(8,128)(2,1)S(1)}, u32[]{:S(2)}, u32[]{:S(2)}) async-start(bf16[8,3,128,256]{3,2,1,0:T(8,128)(2,1)} %backward_second_head.1), calls=%async_computation.2 | async-start | bytes 3145728 | tf_op jit(solution)/shard_map/all_to_all | solution.py:420
  144.2 23.3 %collective-permute-start.10 = (bf16[48,256]{1,0:T(8,128)(2,1)S(1)}, bf16[48,256]{1,0:T(8,128)(2,1)S(1)}, u32[]{:S(2)}, u32[]{:S(2)}) collective-permute-start(bf16[48,256]{1,0:T(8,128)(2,1)S(1)} %get-tuple-element.37), channel_id=1, source_target_pairs={{0,64},{1,65},{2,66},{3,67},{4,68},{5,69},{6,70},{7,71},{8,72},{9,... | collective-permute-start | bytes 73736 | tf_op jit(solution)/shard_map/ppermute | solution.py:79
  153.3 14.4 %collective-permute-start.12 = (bf16[48,256]{1,0:T(8,128)(2,1)S(1)}, bf16[48,256]{1,0:T(8,128)(2,1)S(1)}, u32[]{:S(2)}, u32[]{:S(2)}) collective-permute-start(bf16[48,256]{1,0:T(8,128)(2,1)S(1)} %get-tuple-element.38), channel_id=1, source_target_pairs={{0,128},{1,129},{2,130},{3,131},{4,132},{5,133},{6,134},{7,135},{8... | collective-permute-start | bytes 73736 | tf_op jit(solution)/shard_map/ppermute | solution.py:79
  162.1 9.6 %collective-permute-start.11 = (bf16[48,256]{1,0:T(8,128)(2,1)S(1)}, bf16[48,256]{1,0:T(8,128)(2,1)S(1)}, u32[]{:S(2)}, u32[]{:S(2)}) collective-permute-start(bf16[48,256]{1,0:T(8,128)(2,1)S(1)} %get-tuple-element.39), channel_id=1, source_target_pairs={{0,192},{1,193},{2,194},{3,195},{4,196},{5,197},{6,198},{7,199},{8... | collective-permute-start | bytes 73736 | tf_op jit(solution)/shard_map/ppermute | solution.py:79
Sparse Core Ops, SparseCore 0:
  19.1 77.4 all-gather.1

commit v3 on v2

--- a/solution.py
+++ b/solution.py
@@ -18,6 +18,7 @@
 LENGTH = SP * TOK
 COLS = 256
 D = 3072
+HALF = D // 2
 ROWS = 48
 HEADS = COLS // HD
 CHUNK = 256
@@ -53,15 +54,14 @@
 SWAP_X_HI = route(lambda x_lo, z, core, y, x_hi: (x_lo, z, core, y, 1 - x_hi))
 FROM_Y = {
     k: route(lambda x_lo, z, core, y, x_hi, k=k: (x_lo, z, core, (y - k) % 4, x_hi))
-    for k in (1, 2, 3)
+    for k in (1, 3)
 }
 TO_Z = {
     k: route(lambda x_lo, z, core, y, x_hi, d=d: (x_lo, (z + d) % 16, core, y, x_hi))
     for k, d in ((4, 4), (8, 8), (12, -4))
 }
-Z_NEAR_GROUPS = [
-    [number(x_lo, 4 * quad + z, core, y, x_hi) for z in range(4)]
-    for x_lo in range(2)
+NEAR_GROUPS = [
+    [number(x_lo, 4 * quad + z, core, y, x_hi) for x_lo in range(2) for z in range(4)]
     for quad in range(4)
     for core in range(2)
     for y in range(4)
@@ -170,17 +170,18 @@
 
 def load_dy(place_ref, pieces, text, image, sems):
     copies = []
-    parts = [(image, TXT, IMG)] + ([(text, 0, TXT)] if text is not None else [])
-    for part, (target, row, size) in enumerate(parts):
+    for target, row, size in [(image, TXT, IMG)] + ([(text, 0, TXT)] if text is not None else []):
         for n, piece in enumerate(pieces):
-            first = pl.multiple_of(place_ref[n] * size, TXT)
-            copies.append(
-                pltpu.make_async_copy(
-                    piece.at[pl.ds(row, size), :],
-                    target.at[pl.ds(first, size), :],
-                    sems.at[part * SP + n],
-                )
-            )
+            rows = pl.ds(pl.multiple_of(place_ref[n] * size, TXT), size)
+            if n % 4 == 2:
+                ends = [
+                    (piece.at[half, pl.ds(row, size), :], target.at[rows, pl.ds(half * HALF, HALF)])
+                    for half in range(2)
+                ]
+            else:
+                ends = [(piece.at[pl.ds(row, size), :], target.at[rows, :])]
+            for source, place in ends:
+                copies.append(pltpu.make_async_copy(source, place, sems.at[len(copies)]))
     for copy in copies:
         copy.start()
     return copies
@@ -195,20 +196,19 @@
     att_t = transposed(att_ref[ALL_TXT:, :]).astype(jnp.bfloat16)
     for copy in copies:
         copy.wait()
-    core, x_lo = place_ref[SP], place_ref[SP + 1]
+    core = place_ref[SP]
     for band in range(D // BAND):
         term = dot(att_t, image[:, band * BAND : (band + 1) * BAND]).T.astype(jnp.bfloat16)
-        far = (x_lo + band // 2) % 2
         for j in range(8):
             z = (band % 2) * 8 + j
             low = term[(2 * j) * ROWS : (2 * j + 1) * ROWS]
             high = term[(2 * j + 1) * ROWS : (2 * j + 2) * ROWS]
-            keep_ref[far, z % 4, z // 4] = jnp.where(core == 0, low, high)
-            give_ref[far, z % 4, z // 4] = jnp.where(core == 0, high, low)
+            keep_ref[4 * (band // 2) + z % 4, z // 4] = jnp.where(core == 0, low, high)
+            give_ref[4 * (band // 2) + z % 4, z // 4] = jnp.where(core == 0, high, low)
 
 
 def weight_term(place, pieces, att):
-    half = jax.ShapeDtypeStruct((2, 4, 4, ROWS, COLS), jnp.bfloat16)
+    half = jax.ShapeDtypeStruct((8, 4, ROWS, COLS), jnp.bfloat16)
     return pl.pallas_call(
         term_kernel,
         out_shape=(half, half),
@@ -221,7 +221,7 @@
         ),
         scratch_shapes=[
             pltpu.VMEM((SP * IMG, D), jnp.bfloat16),
-            pltpu.SemaphoreType.DMA((SP,)),
+            pltpu.SemaphoreType.DMA((SP + 2,)),
         ],
         compiler_params=pltpu.CompilerParams(vmem_limit_bytes=VMEM_LIMIT),
         cost_estimate=LIGHT,
@@ -257,10 +257,10 @@
     put(2, 0, dot(probs[...], grad[...]).astype(jnp.bfloat16))
 
 
-def first_kernel(place_ref, *refs):
+def backward_kernel(place_ref, *refs):
     pieces, rest = refs[:SP], refs[SP:]
-    w_ref, x_ref, probs_ref, att, out_ref, other_ref = rest[:6]
-    grad, text, image, weight, joint, probs, slopes, sems, dy_sems, qkv_sems = rest[6:]
+    w_ref, x_ref, probs_ref, att, out_ref = rest[:5]
+    grad, text, image, weight, joint, probs, slopes, sems, dy_sems, qkv_sems = rest[5:]
     copies = [
         pltpu.make_async_copy(
             w_ref.at[:, x_lo, stream], weight.at[stream, x_lo], sems.at[2 * stream + x_lo]
@@ -274,83 +274,58 @@
     for copy in copies[:2]:
         copy.start()
     late = load_qkv(x_ref, joint, qkv_sems)
-    late.append(pltpu.make_async_copy(probs_ref.at[0], probs, sems.at[4]))
-    late[-1].start()
-    for copy in copies[2:] + dy_copies[:SP]:
+    probs_copies = [
+        pltpu.make_async_copy(probs_ref.at[head], probs.at[head], sems.at[4 + head])
+        for head in range(HEADS)
+    ]
+    for copy in probs_copies:
+        copy.start()
+    for copy in copies[2:] + dy_copies[: SP + 2]:
         copy.wait()
-    both = dot(image[...], weight[1].reshape(D, COLS)).astype(jnp.bfloat16)
-    grad[ALL_TXT:, :] = both[:, :HD]
-    other_ref[ALL_TXT:, :] = both[:, HD:]
-    for copy in copies[:2] + dy_copies[SP:]:
+    grad[ALL_TXT:, :] = dot(image[...], weight[1].reshape(D, COLS)).astype(jnp.bfloat16)
+    for copy in copies[:2] + dy_copies[SP + 2 :]:
         copy.wait()
-    both = dot(text[...], weight[0].reshape(D, COLS)).astype(jnp.bfloat16)
-    grad[:ALL_TXT, :] = both[:, :HD]
-    other_ref[:ALL_TXT, :] = both[:, HD:]
+    grad[:ALL_TXT, :] = dot(text[...], weight[0].reshape(D, COLS)).astype(jnp.bfloat16)
     for copy in late:
         copy.wait()
-    head_backward(slice(0, HD), joint, grad, att[:, :HD], probs, slopes, out_ref, slice(0, HD))
-
-
-def second_kernel(x_ref, probs_ref, first_ref, grad, att, out_ref, *rest):
-    joint, probs, slopes, sems, qkv_sems = rest
-    copies = load_qkv(x_ref, joint, qkv_sems)
-    copies.append(pltpu.make_async_copy(probs_ref.at[1], probs, sems.at[0]))
-    copies[-1].start()
-    out_ref[:, :, :, :HD] = first_ref[...]
-    for copy in copies:
-        copy.wait()
-    window = slice(HD, COLS)
-    head_backward(window, joint, grad, att[:, HD:], probs, slopes, out_ref, window)
+    for head in range(HEADS):
+        window = slice(head * HD, (head + 1) * HD)
+        probs_copies[head].wait()
+        head_backward(
+            window, joint, grad[:, window], att[:, window], probs[head], slopes, out_ref, window
+        )
 
 
 ANY = pl.BlockSpec(memory_space=pl.ANY)
 VMEM = pl.BlockSpec(memory_space=pltpu.VMEM)
 
 
-def backward_first(place, pieces, w, x, probs, att):
+def backward(place, pieces, w, x, probs, att):
     return pl.pallas_call(
-        first_kernel,
-        out_shape=(
-            jax.ShapeDtypeStruct((SP, 3, TOK, HD), jnp.bfloat16),
-            jax.ShapeDtypeStruct((LENGTH, HD), jnp.bfloat16),
-        ),
+        backward_kernel,
+        out_shape=jax.ShapeDtypeStruct((SP, 3, TOK, COLS), jnp.bfloat16),
         in_specs=[pl.BlockSpec(memory_space=pltpu.SMEM)] + [ANY] * (SP + 3) + [VMEM],
-        out_specs=(VMEM, VMEM),
+        out_specs=VMEM,
         scratch_shapes=[
-            pltpu.VMEM((LENGTH, HD), jnp.bfloat16),
+            pltpu.VMEM((LENGTH, COLS), jnp.bfloat16),
             pltpu.VMEM((ALL_TXT, D), jnp.bfloat16),
             pltpu.VMEM((ALL_IMG, D), jnp.bfloat16),
             pltpu.VMEM((2, 2, 32, ROWS, COLS), jnp.bfloat16),
             pltpu.VMEM((3, LENGTH, COLS), jnp.bfloat16),
+            pltpu.VMEM((HEADS, LENGTH, LENGTH), jnp.bfloat16),
             pltpu.VMEM((LENGTH, LENGTH), jnp.bfloat16),
-            pltpu.VMEM((LENGTH, LENGTH), jnp.bfloat16),
-            pltpu.SemaphoreType.DMA((5,)),
-            pltpu.SemaphoreType.DMA((2 * SP,)),
+            pltpu.SemaphoreType.DMA((6,)),
+            pltpu.SemaphoreType.DMA((2 * SP + 4,)),
             pltpu.SemaphoreType.DMA((2 * SP,)),
         ],
         compiler_params=pltpu.CompilerParams(vmem_limit_bytes=VMEM_LIMIT),
-        cost_estimate=LIGHT,
-        name="project_and_backward_first_head",
+        cost_estimate=pl.CostEstimate(
+            flops=HEADS * 8 * LENGTH * LENGTH * HD + 2 * LENGTH * D * COLS,
+            bytes_accessed=LENGTH * D * 2 + 2 * D * COLS * 2 + 24 * LENGTH * LENGTH,
+            transcendentals=0,
+        ),
+        name="project_and_backward",
     )(place, *pieces, w, x, probs, att)
-
-
-def backward_second(x, probs, first, grad, att):
-    return pl.pallas_call(
-        second_kernel,
-        out_shape=jax.ShapeDtypeStruct((SP, 3, TOK, COLS), jnp.bfloat16),
-        in_specs=[ANY] * 2 + [VMEM] * 3,
-        out_specs=VMEM,
-        scratch_shapes=[
-            pltpu.VMEM((3, LENGTH, COLS), jnp.bfloat16),
-            pltpu.VMEM((LENGTH, LENGTH), jnp.bfloat16),
-            pltpu.VMEM((LENGTH, LENGTH), jnp.bfloat16),
-            pltpu.SemaphoreType.DMA((1,)),
-            pltpu.SemaphoreType.DMA((2 * SP,)),
-        ],
-        compiler_params=pltpu.CompilerParams(vmem_limit_bytes=VMEM_LIMIT),
-        cost_estimate=LIGHT,
-        name="backward_second_head",
-    )(x, probs, first, grad, att)
 
 
 def spread_kernel(back_ref, txt_ref, img_ref):
@@ -385,10 +360,10 @@
 def local(qkv_txt, qkv_img, dy_txt, dy_img, wv_txt, sc_txt, wv_img, sc_img):
     fsdp, sp = lax.axis_index("fsdp"), lax.axis_index("sp")
     core, x_lo, z = fsdp % 2, fsdp // 32, (fsdp // 2) % 16
-    place = jnp.stack(slots(sp) + [core, x_lo]).astype(jnp.int32)
+    place = jnp.stack(slots(sp) + [core]).astype(jnp.int32)
 
     own = jnp.concatenate([dy_txt[0], dy_img[0]], axis=0)
-    by_y = {k: send(own, FROM_Y[k]) for k in (1, 2, 3)}
+    by_y = {k: send(own, FROM_Y[k]) for k in (1, 3)}
     across = send(own, SWAP_X_HI)
 
     x = jnp.concatenate(
@@ -399,24 +374,23 @@
     x = lax.all_to_all(x, "sp", 0, 0, tiled=True)
     att, probs = forward(x)
 
-    pieces = [own, by_y[1], by_y[2], by_y[3]] + [
+    far = jnp.stack(
+        [send(by_y[1][:, :HALF], FROM_Y[1]), send(by_y[3][:, HALF:], FROM_Y[3])]
+    )
+    pieces = [own, by_y[1], far, by_y[3]] + [
         across,
         send(across, FROM_Y[1]),
-        send(by_y[2], SWAP_X_HI),
+        send(far, SWAP_X_HI),
         send(across, FROM_Y[3]),
     ]
     keep, give = weight_term(place, pieces, att)
 
-    other = send(give, SWAP_CORE)
-    other, att = lax.optimization_barrier((other, att))
-    far = send(plus(keep[1], other[1]).astype(jnp.bfloat16), SWAP_X_LO)
-    first, grad = backward_first(place, pieces, w, x, probs, att)
-    first, far = lax.optimization_barrier((first, far))
-    part = plus(plus(keep[0], other[0]), far).astype(jnp.bfloat16)
-    quads = lax.all_to_all(part, AXES, 0, 0, axis_index_groups=Z_NEAR_GROUPS, tiled=True)
+    total = plus(keep, send(give, SWAP_CORE)).astype(jnp.bfloat16)
+    total, att = lax.optimization_barrier((total, att))
+    quads = lax.all_to_all(total, AXES, 0, 0, axis_index_groups=NEAR_GROUPS, tiled=True)
+    back = backward(place, pieces, w, x, probs, att)
+    back, quads = lax.optimization_barrier((back, quads))
     quads = jnp.sum(quads.astype(jnp.float32), axis=0).astype(jnp.bfloat16)
-    back = backward_second(x, probs, first, grad, att)
-    back, quads = lax.optimization_barrier((back, quads))
     back = lax.all_to_all(back, "sp", 0, 0, tiled=True)
 
     def quad(step):

time: 181 us -> 171 us (0.945)
  waiting for transfers between devices: 47.1 us -> 39.2 us
  Pallas kernels: 31.6 us -> 28.6 us
    ppermute x13, waiting for transfers between devices: 35.7 us -> 25.3 us  [send(): return lax.ppermute(x, AXES, pairs)]
    pallas_call x2 -> x1, Pallas kernels: 16.6 us -> 13.8 us  [backward(): pl.pallas_call(backward_kernel, out_shape=jax.ShapeDtypeStruct((SP, 3, TO...]
    all_to_all x1, starting transfers between devices: 7.04 us -> 4.8 us  [local(): back = lax.all_to_all(back, 'sp', 0, 0, tiled=True)]
    unnamed x30 -> x36, local copies, waits for them, and re-layouts: 4.03 us -> 4.54 us
  transfers between devices with their start and end apart: 17 -> 17, of which waited for: 11 -> 9; matrix products, arithmetic and copies ran while one was open for 1% -> 2% of each run, Pallas kernels for 17% -> 16%
where the time goes in v3:
time: 171 us; the launch traced here: 170 us
  starting transfers between devices  76.8 us (45%)
  waiting for transfers between devices  39.2 us (23%)
  Pallas kernels  28.6 us (17%)
  between operations  14.6 us (9%)
  other arithmetic  6.06 us (4%)
  local copies, waits for them, and re-layouts  5.24 us (3%)
    ppermute x13, starting transfers between devices, send(): return lax.ppermute(x, AXES, pairs)  57.8 us
    ppermute x13, waiting for transfers between devices, send(): return lax.ppermute(x, AXES, pairs)  25.3 us
    pallas_call x1, Pallas kernels, backward(): pl.pallas_call(backward_kernel, out_shape=jax.ShapeDtypeStruct((SP, 3, TO...  13.8 us
    pallas_call x1, Pallas kernels, forward(): pl.pallas_call(forward_kernel, out_shape=(jax.ShapeDtypeStruct((LENGTH, C...  9.25 us
    all_to_all x1, starting transfers between devices, local(): x = lax.all_to_all(x, 'sp', 0, 0, tiled=True)  7.47 us
    all_to_all x1, waiting for transfers between devices, local(): x = lax.all_to_all(x, 'sp', 0, 0, tiled=True)  7.35 us
    all_to_all x1, starting transfers between devices, local(): lax.all_to_all(total, AXES, 0, 0, axis_index_groups=NEAR_GROUPS, tiled=True)  6.61 us
    all_to_all x1, waiting for transfers between devices, local(): lax.all_to_all(total, AXES, 0, 0, axis_index_groups=NEAR_GROUPS, tiled=True)  6.56 us
  transfers between devices with their start and end apart: 17, of which 9 were waited for; matrix products, arithmetic and copies ran while one was open for 2% of the time, Pallas kernels for 16%

profile of v3, /device:TPU:4, one launch (start us, length us, event | category | flops | bytes accessed | tf_op | source)
XLA Modules:
  0.0 170.5 jit_solution(2240096425761172181)
XLA Ops:
  7.2 1.6 copy.22
  8.8 0.3 copy.18
  9.1 0.7 copy-done.10
  9.8 0.1 copy.21
  9.9 0.1 copy.17
  10.1 1.3 maximum_bitcast_fusion
  11.4 0.1 copy.19
  11.5 0.1 copy.20
  11.6 0.1 broadcast_in_dim.6
  11.7 0.1 broadcast_in_dim.7
  11.8 3.1 %collective-permute-start.8 = (bf16[2,48,256]{2,1,0:T(8,128)(2,1)S(1)}, bf16[2,48,256]{2,1,0:T(8,128)(2,1)S(1)}, u32[]{:S(2)}, u32[]{:S(2)}) collective-permute-start(bf16[2,48,256]{2,1,0:T(8,128)(2,1)S(1)} %get-tuple-element.33), channel_id=1, source_target_pairs={{0,256},{1,257},{2,258},{3,259},{4,260},{5,261},{6,262},{7,263},{8... | collective-permute-start | bytes 147464 | tf_op jit(solution)/shard_map/ppermute | solution.py:79
  15.0 2.9 %collective-permute-done.8 = bf16[2,48,256]{2,1,0:T(8,128)(2,1)S(1)} collective-permute-done((bf16[2,48,256]{2,1,0:T(8,128)(2,1)S(1)}, bf16[2,48,256]{2,1,0:T(8,128)(2,1)S(1)}, u32[]{:S(2)}, u32[]{:S(2)}) %collective-permute-start.8) | collective-permute-done | bytes 49184 | tf_op jit(solution)/shard_map/ppermute | solution.py:79
  17.8 0.7 maximum_select_fusion
  18.5 0.1 pad_maximum_fusion.refs_0_
  18.6 4.9 %collective-permute-start = (bf16[128,3072]{1,0:T(8,128)(2,1)S(1)}, bf16[128,3072]{1,0:T(8,128)(2,1)S(1)}, u32[]{:S(2)}, u32[]{:S(2)}) collective-permute-start(bf16[128,3072]{1,0:T(8,128)(2,1)S(1)} %pad_maximum_fusion.refs_0_), channel_id=1, source_target_pairs={{0,6},{1,7},{2,0},{3,1},{4,2},{5,3},{6,4},{7,5},{8,14},{9,15},{10,... | collective-permute-start | bytes 2359304 | tf_op jit(solution)/shard_map/ppermute | solution.py:79
  23.5 1.9 %collective-permute-start.2 = (bf16[128,3072]{1,0:T(8,128)(2,1)S(1)}, bf16[128,3072]{1,0:T(8,128)(2,1)S(1)}, u32[]{:S(2)}, u32[]{:S(2)}) collective-permute-start(bf16[128,3072]{1,0:T(8,128)(2,1)S(1)} %pad_maximum_fusion.refs_0_), channel_id=1, source_target_pairs={{0,2},{1,3},{2,4},{3,5},{4,6},{5,7},{6,0},{7,1},{8,10},{9,11},{10,... | collective-permute-start | bytes 2359304 | tf_op jit(solution)/shard_map/ppermute | solution.py:79
  25.4 6.8 %collective-permute-start.4 = (bf16[128,3072]{1,0:T(8,128)(2,1)S(1)}, bf16[128,3072]{1,0:T(8,128)(2,1)}, u32[]{:S(2)}, u32[]{:S(2)}) collective-permute-start(bf16[128,3072]{1,0:T(8,128)(2,1)S(1)} %pad_maximum_fusion.refs_0_), channel_id=1, source_target_pairs={{0,1},{1,0},{2,3},{3,2},{4,5},{5,4},{6,7},{7,6},{8,9},{9,8},{10,11... | collective-permute-start | bytes 2359304 | tf_op jit(solution)/shard_map/ppermute | solution.py:79
  32.2 6.9 %collective-permute-done.refs_1_ = bf16[128,3072]{1,0:T(8,128)(2,1)S(1)} collective-permute-done((bf16[128,3072]{1,0:T(8,128)(2,1)S(1)}, bf16[128,3072]{1,0:T(8,128)(2,1)S(1)}, u32[]{:S(2)}, u32[]{:S(2)}) %collective-permute-start) | collective-permute-done | bytes 786464 | tf_op jit(solution)/shard_map/ppermute | solution.py:79
  39.2 5.6 %collective-permute-start.1 = (bf16[128,1536]{1,0:T(8,128)(2,1)S(1)}, bf16[128,1536]{1,0:T(8,128)(2,1)S(1)}, u32[]{:S(2)}, u32[]{:S(2)}) collective-permute-start(bf16[128,1536]{1,0:T(8,128)(2,1)S(1)} %slice.8), channel_id=1, source_target_pairs={{0,6},{1,7},{2,0},{3,1},{4,2},{5,3},{6,4},{7,5},{8,14},{9,15},{10,... | collective-permute-start | bytes 1179656 | tf_op jit(solution)/shard_map/ppermute | solution.py:79
  44.8 0.8 copy-done.4
  45.7 1.9 %collective-permute-start.3 = (bf16[128,1536]{1,0:T(8,128)(2,1)S(1)}, bf16[128,1536]{1,0:T(8,128)(2,1)}, u32[]{:S(2)}, u32[]{:S(2)}) collective-permute-start(bf16[128,1536]{1,0:T(8,128)(2,1)S(1)} %slice.9), channel_id=1, source_target_pairs={{0,2},{1,3},{2,4},{3,5},{4,6},{5,7},{6,0},{7,1},{8,10},{9,11},{10,... | collective-permute-start | bytes 1179656 | tf_op jit(solution)/shard_map/ppermute | solution.py:79
  47.6 7.5 %all-to-all-start = ((bf16[8,3,128,256]{3,2,1,0:T(8,128)(2,1)}), bf16[8,3,128,256]{3,2,1,0:T(8,128)(2,1)S(1)}, u32[]{:S(2)}, u32[]{:S(2)}) async-start(bf16[8,3,128,256]{3,2,1,0:T(8,128)(2,1)} %maximum_bitcast_fusion), calls=%async_computation | async-start | bytes 3145728 | tf_op jit(solution)/shard_map/all_to_all | solution.py:374
  55.1 4.6 %collective-permute-start.5 = (bf16[128,3072]{1,0:T(8,128)(2,1)}, bf16[128,3072]{1,0:T(8,128)(2,1)}, u32[]{:S(2)}, u32[]{:S(2)}) collective-permute-start(bf16[128,3072]{1,0:T(8,128)(2,1)} %collective-permute-done.4.refs_4_), channel_id=1, source_target_pairs={{0,6},{1,7},{2,0},{3,1},{4,2},{5,3},{6,4},{7,5},{8,14},{9,15},{10,... | collective-permute-start | bytes 2359304 | tf_op jit(solution)/shard_map/ppermute | solution.py:79
  59.7 1.9 %collective-permute-start.7 = (bf16[128,3072]{1,0:T(8,128)(2,1)}, bf16[128,3072]{1,0:T(8,128)(2,1)}, u32[]{:S(2)}, u32[]{:S(2)}) collective-permute-start(bf16[128,3072]{1,0:T(8,128)(2,1)} %collective-permute-done.4.refs_4_), channel_id=1, source_target_pairs={{0,2},{1,3},{2,4},{3,5},{4,6},{5,7},{6,0},{7,1},{8,10},{9,11},{10,... | collective-permute-start | bytes 2359304 | tf_op jit(solution)/shard_map/ppermute | solution.py:79
  61.6 3.7 %collective-permute-done.3 = bf16[128,1536]{1,0:T(8,128)(2,1)} collective-permute-done((bf16[128,1536]{1,0:T(8,128)(2,1)S(1)}, bf16[128,1536]{1,0:T(8,128)(2,1)}, u32[]{:S(2)}, u32[]{:S(2)}) %collective-permute-start.3) | collective-permute-done | bytes 393248 | tf_op jit(solution)/shard_map/ppermute | solution.py:79
  65.4 1.1 pad_maximum_fusion.1.refs_2_
  66.4 1.9 %collective-permute-start.6 = (bf16[2,128,1536]{2,1,0:T(8,128)(2,1)S(1)}, bf16[2,128,1536]{2,1,0:T(8,128)(2,1)}, u32[]{:S(2)}, u32[]{:S(2)}) collective-permute-start(bf16[2,128,1536]{2,1,0:T(8,128)(2,1)S(1)} %pad_maximum_fusion.1.refs_2_), channel_id=1, source_target_pairs={{0,1},{1,0},{2,3},{3,2},{4,5},{5,4},{6,7},{7,6},{8,9},{9,8},{10,11... | collective-permute-start | bytes 2359304 | tf_op jit(solution)/shard_map/ppermute | solution.py:79
  68.5 0.1 stack.71.place_ref
  68.5 7.4 %all-to-all-done.x_ref.refs_9_ = bf16[8,3,128,256]{3,2,1,0:T(8,128)(2,1)S(1)} async-done(((bf16[8,3,128,256]{3,2,1,0:T(8,128)(2,1)}), bf16[8,3,128,256]{3,2,1,0:T(8,128)(2,1)S(1)}, u32[]{:S(2)}, u32[]{:S(2)}) %all-to-all-start) | async-done | bytes 1572896 | tf_op jit(solution)/shard_map/all_to_all | solution.py:374
  75.9 9.2 %attention_forward.1 = (bf16[1024,256]{1,0:T(8,128)(2,1)S(1)}, bf16[2,1024,1024]{2,1,0:T(8,128)(2,1)}) custom-call(bf16[8,3,128,256]{3,2,1,0:T(8,128)(2,1)S(1)} %all-to-all-done.x_ref.refs_9_), custom_call_target="tpu_custom_call" | custom-call | flops 1000 | bytes 1000 | tf_op jit(solution)/shard_map/attention_forward/pallas_call | solution.py:143
  85.2 2.9 %collective-permute-done.5.refs_5_ = bf16[128,3072]{1,0:T(8,128)(2,1)} collective-permute-done((bf16[128,3072]{1,0:T(8,128)(2,1)}, bf16[128,3072]{1,0:T(8,128)(2,1)}, u32[]{:S(2)}, u32[]{:S(2)}) %collective-permute-start.5) | collective-permute-done | bytes 786464 | tf_op jit(solution)/shard_map/ppermute | solution.py:79
  88.0 3.0 %collective-permute-done.7.refs_7_ = bf16[128,3072]{1,0:T(8,128)(2,1)} collective-permute-done((bf16[128,3072]{1,0:T(8,128)(2,1)}, bf16[128,3072]{1,0:T(8,128)(2,1)}, u32[]{:S(2)}, u32[]{:S(2)}) %collective-permute-start.7) | collective-permute-done | bytes 786464 | tf_op jit(solution)/shard_map/ppermute | solution.py:79
  91.1 4.3 %weight_term.1 = (bf16[8,4,48,256]{3,2,1,0:T(8,128)(2,1)S(1)}, bf16[8,4,48,256]{3,2,1,0:T(8,128)(2,1)S(1)}) custom-call(s32[9]{0:T(128)S(1)} %stack.71.place_ref, bf16[128,3072]{1,0:T(8,128)(2,1)S(1)} %pad_maximum_fusion.refs_0_, bf16[128,3072]{1,0:T(8,128)(2,1)S(1)} %copy-done.2, bf16[2,128,1536]{2,1,0:T(8,128)(2,1)S(1)} %pad_maximum_fusion.1.refs_2_, ...), custom_call_target="tpu_custom_call" | custom-call | flops 1000 | bytes 1000 | tf_op jit(solution)/shard_map/weight_term/pallas_call | solution.py:212
  95.4 1.9 %collective-permute-start.9 = (bf16[8,4,48,256]{3,2,1,0:T(8,128)(2,1)S(1)}, bf16[8,4,48,256]{3,2,1,0:T(8,128)(2,1)S(1)}, u32[]{:S(2)}, u32[]{:S(2)}) collective-permute-start(bf16[8,4,48,256]{3,2,1,0:T(8,128)(2,1)S(1)} %get-tuple-element.22), channel_id=1, source_target_pairs={{0,8},{1,9},{2,10},{3,11},{4,12},{5,13},{6,14},{7,15},{8,0},{9,1},... | collective-permute-start | bytes 2359304 | tf_op jit(solution)/shard_map/ppermute | solution.py:79
  97.3 2.3 %collective-permute-done.9 = bf16[8,4,48,256]{3,2,1,0:T(8,128)(2,1)S(1)} collective-permute-done((bf16[8,4,48,256]{3,2,1,0:T(8,128)(2,1)S(1)}, bf16[8,4,48,256]{3,2,1,0:T(8,128)(2,1)S(1)}, u32[]{:S(2)}, u32[]{:S(2)}) %collective-permute-start.9) | collective-permute-done | bytes 786464 | tf_op jit(solution)/shard_map/ppermute | solution.py:79
  99.6 1.1 add_convert_fusion
  100.7 6.6 %all-to-all-start.1 = ((bf16[8,4,48,256]{3,2,1,0:T(8,128)(2,1)}), bf16[8,4,48,256]{3,2,1,0:T(8,128)(2,1)}, u32[]{:S(2)}, u32[]{:S(2)}) async-start(bf16[8,4,48,256]{3,2,1,0:T(8,128)(2,1)} %add_convert_fusion), calls=%async_computation.1 | async-start | bytes 1572864 | tf_op jit(solution)/shard_map/all_to_all | solution.py:390
  107.3 1.0 copy-done.8
  108.4 13.8 %project_and_backward.1 = bf16[8,3,128,256]{3,2,1,0:T(8,128)(2,1)} custom-call(s32[9]{0:T(128)S(1)} %stack.71.place_ref, bf16[128,3072]{1,0:T(8,128)(2,1)S(1)} %pad_maximum_fusion.refs_0_, bf16[128,3072]{1,0:T(8,128)(2,1)S(1)} %copy-done.3, bf16[2,128,1536]{2,1,0:T(8,128)(2,1)S(1)} %pad_maximum_fusion.1.refs_2_, bf16[128,3072]{1,0:T(8,128)(2,1)S(1)} %copy-done.6, ...), custom_call_target="tpu_custom_call" | custom-call | flops 3758096384 | bytes 34603008 | tf_op jit(solution)/shard_map/project_and_backward/pallas_call | solution.py:304
  122.1 6.6 %all-to-all-done.1 = bf16[8,4,48,256]{3,2,1,0:T(8,128)(2,1)} async-done(((bf16[8,4,48,256]{3,2,1,0:T(8,128)(2,1)}), bf16[8,4,48,256]{3,2,1,0:T(8,128)(2,1)}, u32[]{:S(2)}, u32[]{:S(2)}) %all-to-all-start.1) | async-done | bytes 786464 | tf_op jit(solution)/shard_map/all_to_all | solution.py:390
  128.7 4.8 %all-to-all-start.2 = ((bf16[8,3,128,256]{3,2,1,0:T(8,128)(2,1)}), bf16[8,3,128,256]{3,2,1,0:T(8,128)(2,1)S(1)}, u32[]{:S(2)}, u32[]{:S(2)}) async-start(bf16[8,3,128,256]{3,2,1,0:T(8,128)(2,1)} %project_and_backward.1), calls=%async_computation.2 | async-start | bytes 3145728 | tf_op jit(solution)/shard_map/all_to_all | solution.py:394
  133.5 1.2 reduce_sum.12
  134.8 9.1 %collective-permute-start.10 = (bf16[48,256]{1,0:T(8,128)(2,1)S(1)}, bf16[48,256]{1,0:T(8,128)(2,1)S(1)}, u32[]{:S(2)}, u32[]{:S(2)}) collective-permute-start(bf16[48,256]{1,0:T(8,128)(2,1)S(1)} %get-tuple-element.29), channel_id=1, source_target_pairs={{0,64},{1,65},{2,66},{3,67},{4,68},{5,69},{6,70},{7,71},{8,72},{9,... | collective-permute-start | bytes 73736 | tf_op jit(solution)/shard_map/ppermute | solution.py:79
  143.9 3.3 %collective-permute-start.11 = (bf16[48,256]{1,0:T(8,128)(2,1)S(1)}, bf16[48,256]{1,0:T(8,128)(2,1)S(1)}, u32[]{:S(2)}, u32[]{:S(2)}) collective-permute-start(bf16[48,256]{1,0:T(8,128)(2,1)S(1)} %get-tuple-element.31), channel_id=1, source_target_pairs={{0,192},{1,193},{2,194},{3,195},{4,196},{5,197},{6,198},{7,199},{8... | collective-permute-start | bytes 73736 | tf_op jit(solution)/shard_map/ppermute | solution.py:79
  147.2 10.8 %collective-permute-start.12 = (bf16[48,256]{1,0:T(8,128)(2,1)S(1)}, bf16[48,256]{1,0:T(8,128)(2,1)S(1)}, u32[]{:S(2)}, u32[]{:S(2)}) collective-permute-start(bf16[48,256]{1,0:T(8,128)(2,1)S(1)} %get-tuple-element.30), channel_id=1, source_target_pairs={{0,128},{1,129},{2,130},{3,131},{4,132},{5,133},{6,134},{7,135},{8... | collective-permute-start | bytes 73736 | tf_op jit(solution)/shard_map/ppermute | solution.py:79
  158.1 3.6 %collective-permute-done.12 = bf16[48,256]{1,0:T(8,128)(2,1)S(1)} collective-permute-done((bf16[48,256]{1,0:T(8,128)(2,1)S(1)}, bf16[48,256]{1,0:T(8,128)(2,1)S(1)}, u32[]{:S(2)}, u32[]{:S(2)}) %collective-permute-start.12) | collective-permute-done | bytes 24608 | tf_op jit(solution)/shard_map/ppermute | solution.py:79
  161.6 0.6 fusion.4
  162.3 1.3 spread_features.1
  (44 shorter events, 0.3 us)
Async XLA Ops:
  7.2 100.1 %all-gather.2.cloned.1.call-start = ((), (), s32[]{:S(2)}) async-start(), calls=%async_computation.3 | async-start | bytes 3244032 | tf_op jit(solution)/shard_map/all_gather | solution.py:357
  8.8 1.0 copy-start.10
  10.0 1.4 copy-start.14
  10.0 1.4 copy-start.15
  10.0 1.8 %copy-start.12 = (bf16[48,256]{1,0:T(8,128)(2,1)S(1)}, bf16[48,256]{1,0:T(8,128)(2,1)}, u32[]{:S(2)}) copy-start(bf16[48,256]{1,0:T(8,128)(2,1)} %param.12) | copy-start | bytes 73732
  10.0 1.8 %copy-start.13 = (bf16[48,256]{1,0:T(8,128)(2,1)S(1)}, bf16[48,256]{1,0:T(8,128)(2,1)}, u32[]{:S(2)}) copy-start(bf16[48,256]{1,0:T(8,128)(2,1)} %param.14) | copy-start | bytes 73732
  10.1 8.5 %copy-start.9 = (bf16[1,96,3072]{2,1,0:T(8,128)(2,1)S(1)}, bf16[1,96,3072]{2,1,0:T(8,128)(2,1)}, u32[]{:S(2)}) copy-start(bf16[1,96,3072]{2,1,0:T(8,128)(2,1)} %param.11) | copy-start | bytes 1769476
  10.1 8.5 %copy-start.11 = (bf16[1,32,3072]{2,1,0:T(8,128)(2,1)S(1)}, bf16[1,32,3072]{2,1,0:T(8,128)(2,1)}, u32[]{:S(2)}) copy-start(bf16[1,32,3072]{2,1,0:T(8,128)(2,1)} %param.10) | copy-start | bytes 589828
  11.8 6.0 %collective-permute-start.8 = (bf16[2,48,256]{2,1,0:T(8,128)(2,1)S(1)}, bf16[2,48,256]{2,1,0:T(8,128)(2,1)S(1)}, u32[]{:S(2)}, u32[]{:S(2)}) collective-permute-start(bf16[2,48,256]{2,1,0:T(8,128)(2,1)S(1)} %get-tuple-element.33), channel_id=1, source_target_pairs={{0,256},{1,257},{2,258},{3,259},{4,260},{5,261},{6,262},{7,263},{8... | collective-permute-start | bytes 147464 | tf_op jit(solution)/shard_map/ppermute | solution.py:79
  18.6 20.6 %collective-permute-start = (bf16[128,3072]{1,0:T(8,128)(2,1)S(1)}, bf16[128,3072]{1,0:T(8,128)(2,1)S(1)}, u32[]{:S(2)}, u32[]{:S(2)}) collective-permute-start(bf16[128,3072]{1,0:T(8,128)(2,1)S(1)} %pad_maximum_fusion.refs_0_), channel_id=1, source_target_pairs={{0,6},{1,7},{2,0},{3,1},{4,2},{5,3},{6,4},{7,5},{8,14},{9,15},{10,... | collective-permute-start | bytes 2359304 | tf_op jit(solution)/shard_map/ppermute | solution.py:79
  23.5 21.3 %collective-permute-start.2 = (bf16[128,3072]{1,0:T(8,128)(2,1)S(1)}, bf16[128,3072]{1,0:T(8,128)(2,1)S(1)}, u32[]{:S(2)}, u32[]{:S(2)}) collective-permute-start(bf16[128,3072]{1,0:T(8,128)(2,1)S(1)} %pad_maximum_fusion.refs_0_), channel_id=1, source_target_pairs={{0,2},{1,3},{2,4},{3,5},{4,6},{5,7},{6,0},{7,1},{8,10},{9,11},{10,... | collective-permute-start | bytes 2359304 | tf_op jit(solution)/shard_map/ppermute | solution.py:79
  25.4 29.6 %collective-permute-start.4 = (bf16[128,3072]{1,0:T(8,128)(2,1)S(1)}, bf16[128,3072]{1,0:T(8,128)(2,1)}, u32[]{:S(2)}, u32[]{:S(2)}) collective-permute-start(bf16[128,3072]{1,0:T(8,128)(2,1)S(1)} %pad_maximum_fusion.refs_0_), channel_id=1, source_target_pairs={{0,1},{1,0},{2,3},{3,2},{4,5},{5,4},{6,7},{7,6},{8,9},{9,8},{10,11... | collective-permute-start | bytes 2359304 | tf_op jit(solution)/shard_map/ppermute | solution.py:79
  39.1 5.7 %copy-start.1 = (bf16[128,3072]{1,0:T(8,128)(2,1)}, bf16[128,3072]{1,0:T(8,128)(2,1)S(1)}, u32[]{:S(2)}) copy-start(bf16[128,3072]{1,0:T(8,128)(2,1)S(1)} %collective-permute-done.refs_1_) | copy-start | bytes 2359300
  39.2 22.4 %collective-permute-start.1 = (bf16[128,1536]{1,0:T(8,128)(2,1)S(1)}, bf16[128,1536]{1,0:T(8,128)(2,1)S(1)}, u32[]{:S(2)}, u32[]{:S(2)}) collective-permute-start(bf16[128,1536]{1,0:T(8,128)(2,1)S(1)} %slice.8), channel_id=1, source_target_pairs={{0,6},{1,7},{2,0},{3,1},{4,2},{5,3},{6,4},{7,5},{8,14},{9,15},{10,... | collective-permute-start | bytes 1179656 | tf_op jit(solution)/shard_map/ppermute | solution.py:79
  44.8 0.9 copy-start.4
  45.7 19.7 %collective-permute-start.3 = (bf16[128,1536]{1,0:T(8,128)(2,1)S(1)}, bf16[128,1536]{1,0:T(8,128)(2,1)}, u32[]{:S(2)}, u32[]{:S(2)}) collective-permute-start(bf16[128,1536]{1,0:T(8,128)(2,1)S(1)} %slice.9), channel_id=1, source_target_pairs={{0,2},{1,3},{2,4},{3,5},{4,6},{5,7},{6,0},{7,1},{8,10},{9,11},{10,... | collective-permute-start | bytes 1179656 | tf_op jit(solution)/shard_map/ppermute | solution.py:79
  47.6 28.3 %all-to-all-start = ((bf16[8,3,128,256]{3,2,1,0:T(8,128)(2,1)}), bf16[8,3,128,256]{3,2,1,0:T(8,128)(2,1)S(1)}, u32[]{:S(2)}, u32[]{:S(2)}) async-start(bf16[8,3,128,256]{3,2,1,0:T(8,128)(2,1)} %maximum_bitcast_fusion), calls=%async_computation | async-start | bytes 3145728 | tf_op jit(solution)/shard_map/all_to_all | solution.py:374
  55.1 33.0 %collective-permute-start.5 = (bf16[128,3072]{1,0:T(8,128)(2,1)}, bf16[128,3072]{1,0:T(8,128)(2,1)}, u32[]{:S(2)}, u32[]{:S(2)}) collective-permute-start(bf16[128,3072]{1,0:T(8,128)(2,1)} %collective-permute-done.4.refs_4_), channel_id=1, source_target_pairs={{0,6},{1,7},{2,0},{3,1},{4,2},{5,3},{6,4},{7,5},{8,14},{9,15},{10,... | collective-permute-start | bytes 2359304 | tf_op jit(solution)/shard_map/ppermute | solution.py:79
  59.7 31.4 %collective-permute-start.7 = (bf16[128,3072]{1,0:T(8,128)(2,1)}, bf16[128,3072]{1,0:T(8,128)(2,1)}, u32[]{:S(2)}, u32[]{:S(2)}) collective-permute-start(bf16[128,3072]{1,0:T(8,128)(2,1)} %collective-permute-done.4.refs_4_), channel_id=1, source_target_pairs={{0,2},{1,3},{2,4},{3,5},{4,6},{5,7},{6,0},{7,1},{8,10},{9,11},{10,... | collective-permute-start | bytes 2359304 | tf_op jit(solution)/shard_map/ppermute | solution.py:79
  66.4 24.7 %collective-permute-start.6 = (bf16[2,128,1536]{2,1,0:T(8,128)(2,1)S(1)}, bf16[2,128,1536]{2,1,0:T(8,128)(2,1)}, u32[]{:S(2)}, u32[]{:S(2)}) collective-permute-start(bf16[2,128,1536]{2,1,0:T(8,128)(2,1)S(1)} %pad_maximum_fusion.1.refs_2_), channel_id=1, source_target_pairs={{0,1},{1,0},{2,3},{3,2},{4,5},{5,4},{6,7},{7,6},{8,9},{9,8},{10,11... | collective-permute-start | bytes 2359304 | tf_op jit(solution)/shard_map/ppermute | solution.py:79
  75.9 19.5 %copy-start = (bf16[8,3,128,256]{3,2,1,0:T(8,128)(2,1)}, bf16[8,3,128,256]{3,2,1,0:T(8,128)(2,1)S(1)}, u32[]{:S(2)}) copy-start(bf16[8,3,128,256]{3,2,1,0:T(8,128)(2,1)S(1)} %all-to-all-done.x_ref.refs_9_) | copy-start | bytes 4718596
  75.9 15.2 %copy-start.2 = (bf16[128,3072]{1,0:T(8,128)(2,1)S(1)}, bf16[128,3072]{1,0:T(8,128)(2,1)}, u32[]{:S(2)}) copy-start(bf16[128,3072]{1,0:T(8,128)(2,1)} %copy-done.1) | copy-start | bytes 2359300
  75.9 15.2 %copy-start.5 = (bf16[128,3072]{1,0:T(8,128)(2,1)S(1)}, bf16[128,3072]{1,0:T(8,128)(2,1)}, u32[]{:S(2)}) copy-start(bf16[128,3072]{1,0:T(8,128)(2,1)} %copy-done.4) | copy-start | bytes 2359300
  85.2 10.2 %copy-start.7 = (bf16[1024,256]{1,0:T(8,128)(2,1)}, bf16[1024,256]{1,0:T(8,128)(2,1)S(1)}, u32[]{:S(2)}) copy-start(bf16[1024,256]{1,0:T(8,128)(2,1)S(1)} %get-tuple-element.23.refs_8_.refs_11_) | copy-start | bytes 1572868
  95.4 4.2 %collective-permute-start.9 = (bf16[8,4,48,256]{3,2,1,0:T(8,128)(2,1)S(1)}, bf16[8,4,48,256]{3,2,1,0:T(8,128)(2,1)S(1)}, u32[]{:S(2)}, u32[]{:S(2)}) collective-permute-start(bf16[8,4,48,256]{3,2,1,0:T(8,128)(2,1)S(1)} %get-tuple-element.22), channel_id=1, source_target_pairs={{0,8},{1,9},{2,10},{3,11},{4,12},{5,13},{6,14},{7,15},{8,0},{9,1},... | collective-permute-start | bytes 2359304 | tf_op jit(solution)/shard_map/ppermute | solution.py:79
  99.6 7.7 %copy-start.3 = (bf16[128,3072]{1,0:T(8,128)(2,1)S(1)}, bf16[128,3072]{1,0:T(8,128)(2,1)}, u32[]{:S(2)}) copy-start(bf16[128,3072]{1,0:T(8,128)(2,1)} %copy-done.1) | copy-start | bytes 2359300
  99.6 7.7 %copy-start.6 = (bf16[128,3072]{1,0:T(8,128)(2,1)S(1)}, bf16[128,3072]{1,0:T(8,128)(2,1)}, u32[]{:S(2)}) copy-start(bf16[128,3072]{1,0:T(8,128)(2,1)} %copy-done.4) | copy-start | bytes 2359300
  100.7 28.0 %all-to-all-start.1 = ((bf16[8,4,48,256]{3,2,1,0:T(8,128)(2,1)}), bf16[8,4,48,256]{3,2,1,0:T(8,128)(2,1)}, u32[]{:S(2)}, u32[]{:S(2)}) async-start(bf16[8,4,48,256]{3,2,1,0:T(8,128)(2,1)} %add_convert_fusion), calls=%async_computation.1 | async-start | bytes 1572864 | tf_op jit(solution)/shard_map/all_to_all | solution.py:390
  107.3 1.0 copy-start.8
  128.7 33.6 %all-to-all-start.2 = ((bf16[8,3,128,256]{3,2,1,0:T(8,128)(2,1)}), bf16[8,3,128,256]{3,2,1,0:T(8,128)(2,1)S(1)}, u32[]{:S(2)}, u32[]{:S(2)}) async-start(bf16[8,3,128,256]{3,2,1,0:T(8,128)(2,1)} %project_and_backward.1), calls=%async_computation.2 | async-start | bytes 3145728 | tf_op jit(solution)/shard_map/all_to_all | solution.py:394
  134.8 23.3 %collective-permute-start.10 = (bf16[48,256]{1,0:T(8,128)(2,1)S(1)}, bf16[48,256]{1,0:T(8,128)(2,1)S(1)}, u32[]{:S(2)}, u32[]{:S(2)}) collective-permute-start(bf16[48,256]{1,0:T(8,128)(2,1)S(1)} %get-tuple-element.29), channel_id=1, source_target_pairs={{0,64},{1,65},{2,66},{3,67},{4,68},{5,69},{6,70},{7,71},{8,72},{9,... | collective-permute-start | bytes 73736 | tf_op jit(solution)/shard_map/ppermute | solution.py:79
  143.9 14.2 %collective-permute-start.11 = (bf16[48,256]{1,0:T(8,128)(2,1)S(1)}, bf16[48,256]{1,0:T(8,128)(2,1)S(1)}, u32[]{:S(2)}, u32[]{:S(2)}) collective-permute-start(bf16[48,256]{1,0:T(8,128)(2,1)S(1)} %get-tuple-element.31), channel_id=1, source_target_pairs={{0,192},{1,193},{2,194},{3,195},{4,196},{5,197},{6,198},{7,199},{8... | collective-permute-start | bytes 73736 | tf_op jit(solution)/shard_map/ppermute | solution.py:79
  147.2 14.4 %collective-permute-start.12 = (bf16[48,256]{1,0:T(8,128)(2,1)S(1)}, bf16[48,256]{1,0:T(8,128)(2,1)S(1)}, u32[]{:S(2)}, u32[]{:S(2)}) collective-permute-start(bf16[48,256]{1,0:T(8,128)(2,1)S(1)} %get-tuple-element.30), channel_id=1, source_target_pairs={{0,128},{1,129},{2,130},{3,131},{4,132},{5,133},{6,134},{7,135},{8... | collective-permute-start | bytes 73736 | tf_op jit(solution)/shard_map/ppermute | solution.py:79
Sparse Core Ops, SparseCore 0:
  18.6 77.3 all-gather.1

commit v4 on v3

--- a/solution.py
+++ b/solution.py
@@ -56,9 +56,8 @@
     k: route(lambda x_lo, z, core, y, x_hi, k=k: (x_lo, z, core, (y - k) % 4, x_hi))
     for k in (1, 3)
 }
-TO_Z = {
-    k: route(lambda x_lo, z, core, y, x_hi, d=d: (x_lo, (z + d) % 16, core, y, x_hi))
-    for k, d in ((4, 4), (8, 8), (12, -4))
+SWAP_Z = {
+    k: route(lambda x_lo, z, core, y, x_hi, k=k: (x_lo, z ^ k, core, y, x_hi)) for k in (4, 8)
 }
 NEAR_GROUPS = [
     [number(x_lo, 4 * quad + z, core, y, x_hi) for x_lo in range(2) for z in range(4)]
@@ -369,7 +368,6 @@
     x = jnp.concatenate(
         [qkv_txt[0].reshape(3, TXT, SP, COLS), qkv_img[0].reshape(3, IMG, SP, COLS)], axis=1
     ).transpose(2, 0, 1, 3)
-    x, wv_txt, wv_img = lax.optimization_barrier((x, wv_txt, wv_img))
     w = gather_weights(wv_txt, sc_txt, wv_img, sc_img, x_lo)
     x = lax.all_to_all(x, "sp", 0, 0, tiled=True)
     att, probs = forward(x)
@@ -393,13 +391,16 @@
     quads = jnp.sum(quads.astype(jnp.float32), axis=0).astype(jnp.bfloat16)
     back = lax.all_to_all(back, "sp", 0, 0, tiled=True)
 
-    def quad(step):
-        return lax.dynamic_index_in_dim(quads, (z // 4 + step) % 4, 0, keepdims=False)
-
-    weight_grad = quad(0).astype(jnp.float32)
-    for step in (1, 3, 2):
-        weight_grad = weight_grad + send(quad(step), TO_Z[4 * step]).astype(jnp.float32)
-    return (*spread(back), weight_grad * (1.0 / 64))
+    half, row = z // 8, (z // 4) % 2
+    quads = quads.reshape(2, 2, ROWS, COLS)
+    give = lax.dynamic_index_in_dim(quads, 1 - half, 0, keepdims=False)
+    keep = lax.dynamic_index_in_dim(quads, half, 0, keepdims=False)
+    pair = plus(keep, send(give, SWAP_Z[8]))
+    give = lax.dynamic_index_in_dim(pair, 1 - row, 0, keepdims=False).astype(jnp.bfloat16)
+    last = send(give, SWAP_Z[4])
+    outs, last = lax.optimization_barrier((spread(back), last))
+    keep = lax.dynamic_index_in_dim(pair, row, 0, keepdims=False)
+    return (*outs, plus(keep, last) * (1.0 / 64))
 
 
 def solution(mesh):

time: 171 us -> 169 us (0.988)
  waiting for transfers between devices: 39.2 us -> 34.9 us
  other arithmetic: 6.06 us -> 7.95 us
    ppermute x13 -> x12, waiting for transfers between devices: 25.3 us -> 18.7 us  [send(): return lax.ppermute(x, AXES, pairs)]
    all_to_all x1, waiting for transfers between devices: 7.35 us -> 9.56 us  [local(): x = lax.all_to_all(x, 'sp', 0, 0, tiled=True)]
    ppermute x13 -> x12, starting transfers between devices: 57.8 us -> 57 us  [send(): return lax.ppermute(x, AXES, pairs)]
    unnamed x36 -> x26, local copies, waits for them, and re-layouts: 4.54 us -> 4.67 us
  transfers between devices with their start and end apart: 17 -> 16, of which waited for: 9 -> 9; matrix products, arithmetic and copies ran while one was open for 2% -> 4% of each run, Pallas kernels for 16% -> 17%
where the time goes in v4:
time: 169 us; the launch traced here: 168 us
  starting transfers between devices  76.3 us (45%)
  waiting for transfers between devices  34.9 us (21%)
  Pallas kernels  28.6 us (17%)
  between operations  14.6 us (9%)
  other arithmetic  7.95 us (5%)
  local copies, waits for them, and re-layouts  5.39 us (3%)
    ppermute x12, starting transfers between devices, send(): return lax.ppermute(x, AXES, pairs)  57 us
    ppermute x12, waiting for transfers between devices, send(): return lax.ppermute(x, AXES, pairs)  18.7 us
    pallas_call x1, Pallas kernels, backward(): pl.pallas_call(backward_kernel, out_shape=jax.ShapeDtypeStruct((SP, 3, TO...  13.8 us
    all_to_all x1, waiting for transfers between devices, local(): x = lax.all_to_all(x, 'sp', 0, 0, tiled=True)  9.56 us
    pallas_call x1, Pallas kernels, forward(): pl.pallas_call(forward_kernel, out_shape=(jax.ShapeDtypeStruct((LENGTH, C...  9.24 us
    all_to_all x1, starting transfers between devices, local(): x = lax.all_to_all(x, 'sp', 0, 0, tiled=True)  7.46 us
    all_to_all x1, starting transfers between devices, local(): lax.all_to_all(total, AXES, 0, 0, axis_index_groups=NEAR_GROUPS, tiled=True)  6.63 us
    all_to_all x1, waiting for transfers between devices, local(): lax.all_to_all(total, AXES, 0, 0, axis_index_groups=NEAR_GROUPS, tiled=True)  6.54 us
  transfers between devices with their start and end apart: 16, of which 9 were waited for; matrix products, arithmetic and copies ran while one was open for 4% of the time, Pallas kernels for 17%

profile of v4, /device:TPU:4, one launch (start us, length us, event | category | flops | bytes accessed | tf_op | source)
XLA Modules:
  0.0 167.6 jit_solution(4094644951309399376)
XLA Ops:
  7.2 0.9 copy.17
  8.1 0.8 copy.18
  8.8 0.1 broadcast_in_dim.6
  8.9 0.1 broadcast_in_dim.7
  9.1 0.8 fusion.4
  9.9 3.1 %collective-permute-start.8 = (bf16[2,48,256]{2,1,0:T(8,128)(2,1)S(1)}, bf16[2,48,256]{2,1,0:T(8,128)(2,1)S(1)}, u32[]{:S(2)}, u32[]{:S(2)}) collective-permute-start(bf16[2,48,256]{2,1,0:T(8,128)(2,1)S(1)} %get-tuple-element.30), channel_id=1, source_target_pairs={{0,256},{1,257},{2,258},{3,259},{4,260},{5,261},{6,262},{7,263},{8... | collective-permute-start | bytes 147464 | tf_op jit(solution)/shard_map/ppermute | solution.py:78
  13.0 2.9 %collective-permute-done.8 = bf16[2,48,256]{2,1,0:T(8,128)(2,1)S(1)} collective-permute-done((bf16[2,48,256]{2,1,0:T(8,128)(2,1)S(1)}, bf16[2,48,256]{2,1,0:T(8,128)(2,1)S(1)}, u32[]{:S(2)}, u32[]{:S(2)}) %collective-permute-start.8) | collective-permute-done | bytes 49184 | tf_op jit(solution)/shard_map/ppermute | solution.py:78
  15.8 0.7 maximum_select_fusion
  16.5 1.2 pad_maximum_fusion.refs_0_
  17.7 4.9 %collective-permute-start = (bf16[128,3072]{1,0:T(8,128)(2,1)S(1)}, bf16[128,3072]{1,0:T(8,128)(2,1)S(1)}, u32[]{:S(2)}, u32[]{:S(2)}) collective-permute-start(bf16[128,3072]{1,0:T(8,128)(2,1)S(1)} %pad_maximum_fusion.refs_0_), channel_id=1, source_target_pairs={{0,6},{1,7},{2,0},{3,1},{4,2},{5,3},{6,4},{7,5},{8,14},{9,15},{10,... | collective-permute-start | bytes 2359304 | tf_op jit(solution)/shard_map/ppermute | solution.py:78
  22.6 1.9 %collective-permute-start.2 = (bf16[128,3072]{1,0:T(8,128)(2,1)S(1)}, bf16[128,3072]{1,0:T(8,128)(2,1)S(1)}, u32[]{:S(2)}, u32[]{:S(2)}) collective-permute-start(bf16[128,3072]{1,0:T(8,128)(2,1)S(1)} %pad_maximum_fusion.refs_0_), channel_id=1, source_target_pairs={{0,2},{1,3},{2,4},{3,5},{4,6},{5,7},{6,0},{7,1},{8,10},{9,11},{10,... | collective-permute-start | bytes 2359304 | tf_op jit(solution)/shard_map/ppermute | solution.py:78
  24.5 6.8 %collective-permute-start.4 = (bf16[128,3072]{1,0:T(8,128)(2,1)S(1)}, bf16[128,3072]{1,0:T(8,128)(2,1)}, u32[]{:S(2)}, u32[]{:S(2)}) collective-permute-start(bf16[128,3072]{1,0:T(8,128)(2,1)S(1)} %pad_maximum_fusion.refs_0_), channel_id=1, source_target_pairs={{0,1},{1,0},{2,3},{3,2},{4,5},{5,4},{6,7},{7,6},{8,9},{9,8},{10,11... | collective-permute-start | bytes 2359304 | tf_op jit(solution)/shard_map/ppermute | solution.py:78
  31.3 0.4 copy.24
  31.7 0.3 copy.20
  32.0 0.7 copy-done.10
  32.7 0.1 copy.23
  32.8 0.1 copy.19
  32.9 5.4 %collective-permute-done.refs_1_ = bf16[128,3072]{1,0:T(8,128)(2,1)S(1)} collective-permute-done((bf16[128,3072]{1,0:T(8,128)(2,1)S(1)}, bf16[128,3072]{1,0:T(8,128)(2,1)S(1)}, u32[]{:S(2)}, u32[]{:S(2)}) %collective-permute-start) | collective-permute-done | bytes 786464 | tf_op jit(solution)/shard_map/ppermute | solution.py:78
  38.3 5.6 %collective-permute-start.1 = (bf16[128,1536]{1,0:T(8,128)(2,1)S(1)}, bf16[128,1536]{1,0:T(8,128)(2,1)S(1)}, u32[]{:S(2)}, u32[]{:S(2)}) collective-permute-start(bf16[128,1536]{1,0:T(8,128)(2,1)S(1)} %slice.8), channel_id=1, source_target_pairs={{0,6},{1,7},{2,0},{3,1},{4,2},{5,3},{6,4},{7,5},{8,14},{9,15},{10,... | collective-permute-start | bytes 1179656 | tf_op jit(solution)/shard_map/ppermute | solution.py:78
  43.9 0.8 copy-done.4
  44.8 1.9 %collective-permute-start.3 = (bf16[128,1536]{1,0:T(8,128)(2,1)S(1)}, bf16[128,1536]{1,0:T(8,128)(2,1)}, u32[]{:S(2)}, u32[]{:S(2)}) collective-permute-start(bf16[128,1536]{1,0:T(8,128)(2,1)S(1)} %slice.9), channel_id=1, source_target_pairs={{0,2},{1,3},{2,4},{3,5},{4,6},{5,7},{6,0},{7,1},{8,10},{9,11},{10,... | collective-permute-start | bytes 1179656 | tf_op jit(solution)/shard_map/ppermute | solution.py:78
  46.7 1.3 maximum_bitcast_fusion
  48.0 7.5 %all-to-all-start = ((bf16[8,3,128,256]{3,2,1,0:T(8,128)(2,1)}), bf16[8,3,128,256]{3,2,1,0:T(8,128)(2,1)S(1)}, u32[]{:S(2)}, u32[]{:S(2)}) async-start(bf16[8,3,128,256]{3,2,1,0:T(8,128)(2,1)} %maximum_bitcast_fusion), calls=%async_computation | async-start | bytes 3145728 | tf_op jit(solution)/shard_map/all_to_all | solution.py:372
  55.5 4.6 %collective-permute-start.5 = (bf16[128,3072]{1,0:T(8,128)(2,1)}, bf16[128,3072]{1,0:T(8,128)(2,1)}, u32[]{:S(2)}, u32[]{:S(2)}) collective-permute-start(bf16[128,3072]{1,0:T(8,128)(2,1)} %collective-permute-done.4.refs_4_), channel_id=1, source_target_pairs={{0,6},{1,7},{2,0},{3,1},{4,2},{5,3},{6,4},{7,5},{8,14},{9,15},{10,... | collective-permute-start | bytes 2359304 | tf_op jit(solution)/shard_map/ppermute | solution.py:78
  60.0 1.9 %collective-permute-start.7 = (bf16[128,3072]{1,0:T(8,128)(2,1)}, bf16[128,3072]{1,0:T(8,128)(2,1)}, u32[]{:S(2)}, u32[]{:S(2)}) collective-permute-start(bf16[128,3072]{1,0:T(8,128)(2,1)} %collective-permute-done.4.refs_4_), channel_id=1, source_target_pairs={{0,2},{1,3},{2,4},{3,5},{4,6},{5,7},{6,0},{7,1},{8,10},{9,11},{10,... | collective-permute-start | bytes 2359304 | tf_op jit(solution)/shard_map/ppermute | solution.py:78
  62.0 1.1 pad_maximum_fusion.1.refs_2_
  63.1 2.5 %collective-permute-start.6 = (bf16[2,128,1536]{2,1,0:T(8,128)(2,1)S(1)}, bf16[2,128,1536]{2,1,0:T(8,128)(2,1)}, u32[]{:S(2)}, u32[]{:S(2)}) collective-permute-start(bf16[2,128,1536]{2,1,0:T(8,128)(2,1)S(1)} %pad_maximum_fusion.1.refs_2_), channel_id=1, source_target_pairs={{0,1},{1,0},{2,3},{3,2},{4,5},{5,4},{6,7},{7,6},{8,9},{9,8},{10,11... | collective-permute-start | bytes 2359304 | tf_op jit(solution)/shard_map/ppermute | solution.py:78
  65.6 0.1 stack.71.place_ref
  65.7 9.6 %all-to-all-done.x_ref.refs_9_ = bf16[8,3,128,256]{3,2,1,0:T(8,128)(2,1)S(1)} async-done(((bf16[8,3,128,256]{3,2,1,0:T(8,128)(2,1)}), bf16[8,3,128,256]{3,2,1,0:T(8,128)(2,1)S(1)}, u32[]{:S(2)}, u32[]{:S(2)}) %all-to-all-start) | async-done | bytes 1572896 | tf_op jit(solution)/shard_map/all_to_all | solution.py:372
  75.3 9.2 %attention_forward.1 = (bf16[1024,256]{1,0:T(8,128)(2,1)S(1)}, bf16[2,1024,1024]{2,1,0:T(8,128)(2,1)}) custom-call(bf16[8,3,128,256]{3,2,1,0:T(8,128)(2,1)S(1)} %all-to-all-done.x_ref.refs_9_), custom_call_target="tpu_custom_call" | custom-call | flops 1000 | bytes 1000 | tf_op jit(solution)/shard_map/attention_forward/pallas_call | solution.py:142
  84.5 3.9 %collective-permute-done.5.refs_5_ = bf16[128,3072]{1,0:T(8,128)(2,1)} collective-permute-done((bf16[128,3072]{1,0:T(8,128)(2,1)}, bf16[128,3072]{1,0:T(8,128)(2,1)}, u32[]{:S(2)}, u32[]{:S(2)}) %collective-permute-start.5) | collective-permute-done | bytes 786464 | tf_op jit(solution)/shard_map/ppermute | solution.py:78
  88.4 1.8 %collective-permute-done.7.refs_7_ = bf16[128,3072]{1,0:T(8,128)(2,1)} collective-permute-done((bf16[128,3072]{1,0:T(8,128)(2,1)}, bf16[128,3072]{1,0:T(8,128)(2,1)}, u32[]{:S(2)}, u32[]{:S(2)}) %collective-permute-start.7) | collective-permute-done | bytes 786464 | tf_op jit(solution)/shard_map/ppermute | solution.py:78
  90.2 4.2 %weight_term.1 = (bf16[8,4,48,256]{3,2,1,0:T(8,128)(2,1)S(1)}, bf16[8,4,48,256]{3,2,1,0:T(8,128)(2,1)S(1)}) custom-call(s32[9]{0:T(128)S(1)} %stack.71.place_ref, bf16[128,3072]{1,0:T(8,128)(2,1)S(1)} %pad_maximum_fusion.refs_0_, bf16[128,3072]{1,0:T(8,128)(2,1)S(1)} %copy-done.2, bf16[2,128,1536]{2,1,0:T(8,128)(2,1)S(1)} %pad_maximum_fusion.1.refs_2_, ...), custom_call_target="tpu_custom_call" | custom-call | flops 1000 | bytes 1000 | tf_op jit(solution)/shard_map/weight_term/pallas_call | solution.py:211
  94.5 1.9 %collective-permute-start.9 = (bf16[8,4,48,256]{3,2,1,0:T(8,128)(2,1)S(1)}, bf16[8,4,48,256]{3,2,1,0:T(8,128)(2,1)S(1)}, u32[]{:S(2)}, u32[]{:S(2)}) collective-permute-start(bf16[8,4,48,256]{3,2,1,0:T(8,128)(2,1)S(1)} %get-tuple-element.19), channel_id=1, source_target_pairs={{0,8},{1,9},{2,10},{3,11},{4,12},{5,13},{6,14},{7,15},{8,0},{9,1},... | collective-permute-start | bytes 2359304 | tf_op jit(solution)/shard_map/ppermute | solution.py:78
  96.4 2.3 %collective-permute-done.9 = bf16[8,4,48,256]{3,2,1,0:T(8,128)(2,1)S(1)} collective-permute-done((bf16[8,4,48,256]{3,2,1,0:T(8,128)(2,1)S(1)}, bf16[8,4,48,256]{3,2,1,0:T(8,128)(2,1)S(1)}, u32[]{:S(2)}, u32[]{:S(2)}) %collective-permute-start.9) | collective-permute-done | bytes 786464 | tf_op jit(solution)/shard_map/ppermute | solution.py:78
  98.7 1.1 add_convert_fusion
  99.8 6.6 %all-to-all-start.1 = ((bf16[8,4,48,256]{3,2,1,0:T(8,128)(2,1)}), bf16[8,4,48,256]{3,2,1,0:T(8,128)(2,1)}, u32[]{:S(2)}, u32[]{:S(2)}) async-start(bf16[8,4,48,256]{3,2,1,0:T(8,128)(2,1)} %add_convert_fusion), calls=%async_computation.1 | async-start | bytes 1572864 | tf_op jit(solution)/shard_map/all_to_all | solution.py:388
  106.5 1.0 copy-done.8
  107.5 13.8 %project_and_backward.1 = bf16[8,3,128,256]{3,2,1,0:T(8,128)(2,1)} custom-call(s32[9]{0:T(128)S(1)} %stack.71.place_ref, bf16[128,3072]{1,0:T(8,128)(2,1)S(1)} %pad_maximum_fusion.refs_0_, bf16[128,3072]{1,0:T(8,128)(2,1)S(1)} %copy-done.3, bf16[2,128,1536]{2,1,0:T(8,128)(2,1)S(1)} %pad_maximum_fusion.1.refs_2_, bf16[128,3072]{1,0:T(8,128)(2,1)S(1)} %copy-done.6, ...), custom_call_target="tpu_custom_call" | custom-call | flops 3758096384 | bytes 34603008 | tf_op jit(solution)/shard_map/project_and_backward/pallas_call | solution.py:303
  121.3 6.5 %all-to-all-done.1 = bf16[8,4,48,256]{3,2,1,0:T(8,128)(2,1)} async-done(((bf16[8,4,48,256]{3,2,1,0:T(8,128)(2,1)}), bf16[8,4,48,256]{3,2,1,0:T(8,128)(2,1)}, u32[]{:S(2)}, u32[]{:S(2)}) %all-to-all-start.1) | async-done | bytes 786464 | tf_op jit(solution)/shard_map/all_to_all | solution.py:388
  127.8 5.2 %all-to-all-start.2 = ((bf16[8,3,128,256]{3,2,1,0:T(8,128)(2,1)}), bf16[8,3,128,256]{3,2,1,0:T(8,128)(2,1)S(1)}, u32[]{:S(2)}, u32[]{:S(2)}) async-start(bf16[8,3,128,256]{3,2,1,0:T(8,128)(2,1)} %project_and_backward.1), calls=%async_computation.2 | async-start | bytes 3145728 | tf_op jit(solution)/shard_map/all_to_all | solution.py:392
  133.0 1.2 reduce_sum.12
  134.2 13.5 %collective-permute-start.10 = (bf16[2,48,256]{2,1,0:T(8,128)(2,1)S(1)}, bf16[2,48,256]{2,1,0:T(8,128)(2,1)S(1)}, u32[]{:S(2)}, u32[]{:S(2)}) collective-permute-start(bf16[2,48,256]{2,1,0:T(8,128)(2,1)S(1)} %dynamic-slice_bitcast_fusion), channel_id=1, source_target_pairs={{0,128},{1,129},{2,130},{3,131},{4,132},{5,133},{6,134},{7,135},{8... | collective-permute-start | bytes 147464 | tf_op jit(solution)/shard_map/ppermute | solution.py:78
  147.8 2.0 %collective-permute-done.10 = bf16[2,48,256]{2,1,0:T(8,128)(2,1)S(1)} collective-permute-done((bf16[2,48,256]{2,1,0:T(8,128)(2,1)S(1)}, bf16[2,48,256]{2,1,0:T(8,128)(2,1)S(1)}, u32[]{:S(2)}, u32[]{:S(2)}) %collective-permute-start.10) | collective-permute-done | bytes 49184 | tf_op jit(solution)/shard_map/ppermute | solution.py:78
  149.8 8.3 %collective-permute-start.11 = (bf16[48,256]{1,0:T(8,128)(2,1)S(1)}, bf16[48,256]{1,0:T(8,128)(2,1)S(1)}, u32[]{:S(2)}, u32[]{:S(2)}) collective-permute-start(bf16[48,256]{1,0:T(8,128)(2,1)S(1)} %fusion.3), channel_id=1, source_target_pairs={{0,64},{1,65},{2,66},{3,67},{4,68},{5,69},{6,70},{7,71},{8,72},{9,... | collective-permute-start | bytes 73736 | tf_op jit(solution)/shard_map/ppermute | solution.py:78
  158.2 1.3 spread_features.1
  159.5 0.6 collective-permute-done.11
  160.2 0.6 fusion.2
  (34 shorter events, 0.2 us)
Async XLA Ops:
  7.2 24.2 %copy-start.9 = (bf16[1,3,96,2048]{3,2,1,0:T(8,128)(2,1)S(1)}, bf16[1,3,96,2048]{3,2,1,0:T(8,128)(2,1)}, u32[]{:S(2)}) copy-start(bf16[1,3,96,2048]{3,2,1,0:T(8,128)(2,1)} %param.9) | copy-start | bytes 3538948
  7.2 99.2 %all-gather.2.cloned.1.call-start = ((), (), s32[]{:S(2)}) async-start(), calls=%async_computation.3 | async-start | bytes 3244032 | tf_op jit(solution)/shard_map/all_gather | solution.py:356
  9.9 6.0 %collective-permute-start.8 = (bf16[2,48,256]{2,1,0:T(8,128)(2,1)S(1)}, bf16[2,48,256]{2,1,0:T(8,128)(2,1)S(1)}, u32[]{:S(2)}, u32[]{:S(2)}) collective-permute-start(bf16[2,48,256]{2,1,0:T(8,128)(2,1)S(1)} %get-tuple-element.30), channel_id=1, source_target_pairs={{0,256},{1,257},{2,258},{3,259},{4,260},{5,261},{6,262},{7,263},{8... | collective-permute-start | bytes 147464 | tf_op jit(solution)/shard_map/ppermute | solution.py:78
  17.7 20.6 %collective-permute-start = (bf16[128,3072]{1,0:T(8,128)(2,1)S(1)}, bf16[128,3072]{1,0:T(8,128)(2,1)S(1)}, u32[]{:S(2)}, u32[]{:S(2)}) collective-permute-start(bf16[128,3072]{1,0:T(8,128)(2,1)S(1)} %pad_maximum_fusion.refs_0_), channel_id=1, source_target_pairs={{0,6},{1,7},{2,0},{3,1},{4,2},{5,3},{6,4},{7,5},{8,14},{9,15},{10,... | collective-permute-start | bytes 2359304 | tf_op jit(solution)/shard_map/ppermute | solution.py:78
  22.6 21.3 %collective-permute-start.2 = (bf16[128,3072]{1,0:T(8,128)(2,1)S(1)}, bf16[128,3072]{1,0:T(8,128)(2,1)S(1)}, u32[]{:S(2)}, u32[]{:S(2)}) collective-permute-start(bf16[128,3072]{1,0:T(8,128)(2,1)S(1)} %pad_maximum_fusion.refs_0_), channel_id=1, source_target_pairs={{0,2},{1,3},{2,4},{3,5},{4,6},{5,7},{6,0},{7,1},{8,10},{9,11},{10,... | collective-permute-start | bytes 2359304 | tf_op jit(solution)/shard_map/ppermute | solution.py:78
  24.5 30.9 %collective-permute-start.4 = (bf16[128,3072]{1,0:T(8,128)(2,1)S(1)}, bf16[128,3072]{1,0:T(8,128)(2,1)}, u32[]{:S(2)}, u32[]{:S(2)}) collective-permute-start(bf16[128,3072]{1,0:T(8,128)(2,1)S(1)} %pad_maximum_fusion.refs_0_), channel_id=1, source_target_pairs={{0,1},{1,0},{2,3},{3,2},{4,5},{5,4},{6,7},{7,6},{8,9},{9,8},{10,11... | collective-permute-start | bytes 2359304 | tf_op jit(solution)/shard_map/ppermute | solution.py:78
  31.7 1.0 copy-start.10
  38.2 5.7 %copy-start.1 = (bf16[128,3072]{1,0:T(8,128)(2,1)}, bf16[128,3072]{1,0:T(8,128)(2,1)S(1)}, u32[]{:S(2)}) copy-start(bf16[128,3072]{1,0:T(8,128)(2,1)S(1)} %collective-permute-done.refs_1_) | copy-start | bytes 2359300
  38.3 23.7 %collective-permute-start.1 = (bf16[128,1536]{1,0:T(8,128)(2,1)S(1)}, bf16[128,1536]{1,0:T(8,128)(2,1)S(1)}, u32[]{:S(2)}, u32[]{:S(2)}) collective-permute-start(bf16[128,1536]{1,0:T(8,128)(2,1)S(1)} %slice.8), channel_id=1, source_target_pairs={{0,6},{1,7},{2,0},{3,1},{4,2},{5,3},{6,4},{7,5},{8,14},{9,15},{10,... | collective-permute-start | bytes 1179656 | tf_op jit(solution)/shard_map/ppermute | solution.py:78
  43.9 0.9 copy-start.4
  44.8 17.2 %collective-permute-start.3 = (bf16[128,1536]{1,0:T(8,128)(2,1)S(1)}, bf16[128,1536]{1,0:T(8,128)(2,1)}, u32[]{:S(2)}, u32[]{:S(2)}) collective-permute-start(bf16[128,1536]{1,0:T(8,128)(2,1)S(1)} %slice.9), channel_id=1, source_target_pairs={{0,2},{1,3},{2,4},{3,5},{4,6},{5,7},{6,0},{7,1},{8,10},{9,11},{10,... | collective-permute-start | bytes 1179656 | tf_op jit(solution)/shard_map/ppermute | solution.py:78
  48.0 27.3 %all-to-all-start = ((bf16[8,3,128,256]{3,2,1,0:T(8,128)(2,1)}), bf16[8,3,128,256]{3,2,1,0:T(8,128)(2,1)S(1)}, u32[]{:S(2)}, u32[]{:S(2)}) async-start(bf16[8,3,128,256]{3,2,1,0:T(8,128)(2,1)} %maximum_bitcast_fusion), calls=%async_computation | async-start | bytes 3145728 | tf_op jit(solution)/shard_map/all_to_all | solution.py:372
  55.5 33.0 %collective-permute-start.5 = (bf16[128,3072]{1,0:T(8,128)(2,1)}, bf16[128,3072]{1,0:T(8,128)(2,1)}, u32[]{:S(2)}, u32[]{:S(2)}) collective-permute-start(bf16[128,3072]{1,0:T(8,128)(2,1)} %collective-permute-done.4.refs_4_), channel_id=1, source_target_pairs={{0,6},{1,7},{2,0},{3,1},{4,2},{5,3},{6,4},{7,5},{8,14},{9,15},{10,... | collective-permute-start | bytes 2359304 | tf_op jit(solution)/shard_map/ppermute | solution.py:78
  60.0 30.2 %collective-permute-start.7 = (bf16[128,3072]{1,0:T(8,128)(2,1)}, bf16[128,3072]{1,0:T(8,128)(2,1)}, u32[]{:S(2)}, u32[]{:S(2)}) collective-permute-start(bf16[128,3072]{1,0:T(8,128)(2,1)} %collective-permute-done.4.refs_4_), channel_id=1, source_target_pairs={{0,2},{1,3},{2,4},{3,5},{4,6},{5,7},{6,0},{7,1},{8,10},{9,11},{10,... | collective-permute-start | bytes 2359304 | tf_op jit(solution)/shard_map/ppermute | solution.py:78
  63.1 27.1 %collective-permute-start.6 = (bf16[2,128,1536]{2,1,0:T(8,128)(2,1)S(1)}, bf16[2,128,1536]{2,1,0:T(8,128)(2,1)}, u32[]{:S(2)}, u32[]{:S(2)}) collective-permute-start(bf16[2,128,1536]{2,1,0:T(8,128)(2,1)S(1)} %pad_maximum_fusion.1.refs_2_), channel_id=1, source_target_pairs={{0,1},{1,0},{2,3},{3,2},{4,5},{5,4},{6,7},{7,6},{8,9},{9,8},{10,11... | collective-permute-start | bytes 2359304 | tf_op jit(solution)/shard_map/ppermute | solution.py:78
  75.3 19.2 %copy-start = (bf16[8,3,128,256]{3,2,1,0:T(8,128)(2,1)}, bf16[8,3,128,256]{3,2,1,0:T(8,128)(2,1)S(1)}, u32[]{:S(2)}) copy-start(bf16[8,3,128,256]{3,2,1,0:T(8,128)(2,1)S(1)} %all-to-all-done.x_ref.refs_9_) | copy-start | bytes 4718596
  75.3 14.9 %copy-start.2 = (bf16[128,3072]{1,0:T(8,128)(2,1)S(1)}, bf16[128,3072]{1,0:T(8,128)(2,1)}, u32[]{:S(2)}) copy-start(bf16[128,3072]{1,0:T(8,128)(2,1)} %copy-done.1) | copy-start | bytes 2359300
  75.3 14.9 %copy-start.5 = (bf16[128,3072]{1,0:T(8,128)(2,1)S(1)}, bf16[128,3072]{1,0:T(8,128)(2,1)}, u32[]{:S(2)}) copy-start(bf16[128,3072]{1,0:T(8,128)(2,1)} %copy-done.4) | copy-start | bytes 2359300
  84.5 9.9 %copy-start.7 = (bf16[1024,256]{1,0:T(8,128)(2,1)}, bf16[1024,256]{1,0:T(8,128)(2,1)S(1)}, u32[]{:S(2)}) copy-start(bf16[1024,256]{1,0:T(8,128)(2,1)S(1)} %get-tuple-element.20.refs_8_.refs_11_) | copy-start | bytes 1572868
  94.5 4.2 %collective-permute-start.9 = (bf16[8,4,48,256]{3,2,1,0:T(8,128)(2,1)S(1)}, bf16[8,4,48,256]{3,2,1,0:T(8,128)(2,1)S(1)}, u32[]{:S(2)}, u32[]{:S(2)}) collective-permute-start(bf16[8,4,48,256]{3,2,1,0:T(8,128)(2,1)S(1)} %get-tuple-element.19), channel_id=1, source_target_pairs={{0,8},{1,9},{2,10},{3,11},{4,12},{5,13},{6,14},{7,15},{8,0},{9,1},... | collective-permute-start | bytes 2359304 | tf_op jit(solution)/shard_map/ppermute | solution.py:78
  98.7 7.8 %copy-start.3 = (bf16[128,3072]{1,0:T(8,128)(2,1)S(1)}, bf16[128,3072]{1,0:T(8,128)(2,1)}, u32[]{:S(2)}) copy-start(bf16[128,3072]{1,0:T(8,128)(2,1)} %copy-done.1) | copy-start | bytes 2359300
  98.7 7.8 %copy-start.6 = (bf16[128,3072]{1,0:T(8,128)(2,1)S(1)}, bf16[128,3072]{1,0:T(8,128)(2,1)}, u32[]{:S(2)}) copy-start(bf16[128,3072]{1,0:T(8,128)(2,1)} %copy-done.4) | copy-start | bytes 2359300
  99.8 28.0 %all-to-all-start.1 = ((bf16[8,4,48,256]{3,2,1,0:T(8,128)(2,1)}), bf16[8,4,48,256]{3,2,1,0:T(8,128)(2,1)}, u32[]{:S(2)}, u32[]{:S(2)}) async-start(bf16[8,4,48,256]{3,2,1,0:T(8,128)(2,1)} %add_convert_fusion), calls=%async_computation.1 | async-start | bytes 1572864 | tf_op jit(solution)/shard_map/all_to_all | solution.py:388
  106.4 1.0 copy-start.8
  127.8 30.4 %all-to-all-start.2 = ((bf16[8,3,128,256]{3,2,1,0:T(8,128)(2,1)}), bf16[8,3,128,256]{3,2,1,0:T(8,128)(2,1)S(1)}, u32[]{:S(2)}, u32[]{:S(2)}) async-start(bf16[8,3,128,256]{3,2,1,0:T(8,128)(2,1)} %project_and_backward.1), calls=%async_computation.2 | async-start | bytes 3145728 | tf_op jit(solution)/shard_map/all_to_all | solution.py:392
  134.2 15.6 %collective-permute-start.10 = (bf16[2,48,256]{2,1,0:T(8,128)(2,1)S(1)}, bf16[2,48,256]{2,1,0:T(8,128)(2,1)S(1)}, u32[]{:S(2)}, u32[]{:S(2)}) collective-permute-start(bf16[2,48,256]{2,1,0:T(8,128)(2,1)S(1)} %dynamic-slice_bitcast_fusion), channel_id=1, source_target_pairs={{0,128},{1,129},{2,130},{3,131},{4,132},{5,133},{6,134},{7,135},{8... | collective-permute-start | bytes 147464 | tf_op jit(solution)/shard_map/ppermute | solution.py:78
  149.8 10.3 %collective-permute-start.11 = (bf16[48,256]{1,0:T(8,128)(2,1)S(1)}, bf16[48,256]{1,0:T(8,128)(2,1)S(1)}, u32[]{:S(2)}, u32[]{:S(2)}) collective-permute-start(bf16[48,256]{1,0:T(8,128)(2,1)S(1)} %fusion.3), channel_id=1, source_target_pairs={{0,64},{1,65},{2,66},{3,67},{4,68},{5,69},{6,70},{7,71},{8,72},{9,... | collective-permute-start | bytes 73736 | tf_op jit(solution)/shard_map/ppermute | solution.py:78
Sparse Core Ops, SparseCore 0:
  16.6 77.4 all-gather.1

commit v5 on v4

--- a/solution.py
+++ b/solution.py
@@ -120,9 +120,10 @@
     return copies
 
 
-def forward_kernel(x_ref, att_ref, probs_ref, joint, sems):
+def forward_kernel(x_ref, att_ref, probs_ref, joint, held, sems, out_sems):
     for copy in load_qkv(x_ref, joint, sems):
         copy.wait()
+    copies = []
     for head in range(HEADS):
         window = slice(head * HD, (head + 1) * HD)
         keys = joint[1, :, window]
@@ -134,8 +135,18 @@
             weights = jnp.exp2((scores - highest) * SCALE2)
             share = 1.0 / jnp.sum(weights, axis=0, keepdims=True)
             probs = (weights * share).astype(jnp.bfloat16)
-            probs_ref[head, :, rows] = probs
+            held[head, :, rows] = probs
+            copies.append(
+                pltpu.make_async_copy(
+                    held.at[head, :, pl.ds(chunk * CHUNK, CHUNK)],
+                    probs_ref.at[head, :, pl.ds(chunk * CHUNK, CHUNK)],
+                    out_sems.at[len(copies)],
+                )
+            )
+            copies[-1].start()
             att_ref[rows, window] = dot(values_t, probs).T.astype(jnp.bfloat16)
+    for copy in copies:
+        copy.wait()
 
 
 def forward(x):
@@ -148,11 +159,13 @@
         in_specs=[pl.BlockSpec(memory_space=pl.ANY)],
         out_specs=(
             pl.BlockSpec(memory_space=pltpu.VMEM),
-            pl.BlockSpec(memory_space=pltpu.VMEM),
+            pl.BlockSpec(memory_space=pl.ANY),
         ),
         scratch_shapes=[
             pltpu.VMEM((3, LENGTH, COLS), jnp.bfloat16),
+            pltpu.VMEM((HEADS, LENGTH, LENGTH), jnp.bfloat16),
             pltpu.SemaphoreType.DMA((2 * SP,)),
+            pltpu.SemaphoreType.DMA((HEADS * LENGTH // CHUNK,)),
         ],
         compiler_params=pltpu.CompilerParams(vmem_limit_bytes=VMEM_LIMIT),
         cost_estimate=LIGHT,

time: 169 us -> 169 us (level)
  transfers between devices with their start and end apart: 16 -> 16, of which waited for: 9 -> 9; matrix products, arithmetic and copies ran while one was open for 4% -> 4% of each run, Pallas kernels for 17% -> 16%
where the time goes in v5:
time: 169 us; the launch traced here: 168 us
  starting transfers between devices  76.3 us (45%)
  waiting for transfers between devices  35.9 us (21%)
  Pallas kernels  27.5 us (16%)
  between operations  14.6 us (9%)
  other arithmetic  7.95 us (5%)
  local copies, waits for them, and re-layouts  5.39 us (3%)
    ppermute x12, starting transfers between devices, send(): return lax.ppermute(x, AXES, pairs)  57 us
    ppermute x12, waiting for transfers between devices, send(): return lax.ppermute(x, AXES, pairs)  19.8 us
    pallas_call x1, Pallas kernels, backward(): pl.pallas_call(backward_kernel, out_shape=jax.ShapeDtypeStruct((SP, 3, TO...  13.8 us
    all_to_all x1, waiting for transfers between devices, local(): x = lax.all_to_all(x, 'sp', 0, 0, tiled=True)  9.56 us
    pallas_call x1, Pallas kernels, forward(): pl.pallas_call(forward_kernel, out_shape=(jax.ShapeDtypeStruct((LENGTH, C...  8.16 us
    all_to_all x1, starting transfers between devices, local(): x = lax.all_to_all(x, 'sp', 0, 0, tiled=True)  7.46 us
    all_to_all x1, starting transfers between devices, local(): lax.all_to_all(total, AXES, 0, 0, axis_index_groups=NEAR_GROUPS, tiled=True)  6.63 us
    all_to_all x1, waiting for transfers between devices, local(): lax.all_to_all(total, AXES, 0, 0, axis_index_groups=NEAR_GROUPS, tiled=True)  6.54 us
  transfers between devices with their start and end apart: 16, of which 9 were waited for; matrix products, arithmetic and copies ran while one was open for 4% of the time, Pallas kernels for 16%

profile of v5, /device:TPU:4, one launch (start us, length us, event | category | flops | bytes accessed | tf_op | source)
XLA Modules:
  0.0 167.6 jit_solution(17722520439224064374)
XLA Ops:
  7.2 0.9 copy.17
  8.1 0.8 copy.18
  8.8 0.1 broadcast_in_dim.6
  8.9 0.1 broadcast_in_dim.7
  9.1 0.8 fusion.4
  9.9 3.1 %collective-permute-start.8 = (bf16[2,48,256]{2,1,0:T(8,128)(2,1)S(1)}, bf16[2,48,256]{2,1,0:T(8,128)(2,1)S(1)}, u32[]{:S(2)}, u32[]{:S(2)}) collective-permute-start(bf16[2,48,256]{2,1,0:T(8,128)(2,1)S(1)} %get-tuple-element.30), channel_id=1, source_target_pairs={{0,256},{1,257},{2,258},{3,259},{4,260},{5,261},{6,262},{7,263},{8... | collective-permute-start | bytes 147464 | tf_op jit(solution)/shard_map/ppermute | solution.py:78
  13.0 2.9 %collective-permute-done.8 = bf16[2,48,256]{2,1,0:T(8,128)(2,1)S(1)} collective-permute-done((bf16[2,48,256]{2,1,0:T(8,128)(2,1)S(1)}, bf16[2,48,256]{2,1,0:T(8,128)(2,1)S(1)}, u32[]{:S(2)}, u32[]{:S(2)}) %collective-permute-start.8) | collective-permute-done | bytes 49184 | tf_op jit(solution)/shard_map/ppermute | solution.py:78
  15.8 0.7 maximum_select_fusion
  16.5 1.2 pad_maximum_fusion.refs_0_
  17.7 4.9 %collective-permute-start = (bf16[128,3072]{1,0:T(8,128)(2,1)S(1)}, bf16[128,3072]{1,0:T(8,128)(2,1)S(1)}, u32[]{:S(2)}, u32[]{:S(2)}) collective-permute-start(bf16[128,3072]{1,0:T(8,128)(2,1)S(1)} %pad_maximum_fusion.refs_0_), channel_id=1, source_target_pairs={{0,6},{1,7},{2,0},{3,1},{4,2},{5,3},{6,4},{7,5},{8,14},{9,15},{10,... | collective-permute-start | bytes 2359304 | tf_op jit(solution)/shard_map/ppermute | solution.py:78
  22.6 1.9 %collective-permute-start.2 = (bf16[128,3072]{1,0:T(8,128)(2,1)S(1)}, bf16[128,3072]{1,0:T(8,128)(2,1)S(1)}, u32[]{:S(2)}, u32[]{:S(2)}) collective-permute-start(bf16[128,3072]{1,0:T(8,128)(2,1)S(1)} %pad_maximum_fusion.refs_0_), channel_id=1, source_target_pairs={{0,2},{1,3},{2,4},{3,5},{4,6},{5,7},{6,0},{7,1},{8,10},{9,11},{10,... | collective-permute-start | bytes 2359304 | tf_op jit(solution)/shard_map/ppermute | solution.py:78
  24.5 6.8 %collective-permute-start.4 = (bf16[128,3072]{1,0:T(8,128)(2,1)S(1)}, bf16[128,3072]{1,0:T(8,128)(2,1)}, u32[]{:S(2)}, u32[]{:S(2)}) collective-permute-start(bf16[128,3072]{1,0:T(8,128)(2,1)S(1)} %pad_maximum_fusion.refs_0_), channel_id=1, source_target_pairs={{0,1},{1,0},{2,3},{3,2},{4,5},{5,4},{6,7},{7,6},{8,9},{9,8},{10,11... | collective-permute-start | bytes 2359304 | tf_op jit(solution)/shard_map/ppermute | solution.py:78
  31.3 0.4 copy.24
  31.7 0.3 copy.20
  32.0 0.7 copy-done.10
  32.7 0.1 copy.23
  32.8 0.1 copy.19
  32.9 5.4 %collective-permute-done.refs_1_ = bf16[128,3072]{1,0:T(8,128)(2,1)S(1)} collective-permute-done((bf16[128,3072]{1,0:T(8,128)(2,1)S(1)}, bf16[128,3072]{1,0:T(8,128)(2,1)S(1)}, u32[]{:S(2)}, u32[]{:S(2)}) %collective-permute-start) | collective-permute-done | bytes 786464 | tf_op jit(solution)/shard_map/ppermute | solution.py:78
  38.3 5.6 %collective-permute-start.1 = (bf16[128,1536]{1,0:T(8,128)(2,1)S(1)}, bf16[128,1536]{1,0:T(8,128)(2,1)S(1)}, u32[]{:S(2)}, u32[]{:S(2)}) collective-permute-start(bf16[128,1536]{1,0:T(8,128)(2,1)S(1)} %slice.8), channel_id=1, source_target_pairs={{0,6},{1,7},{2,0},{3,1},{4,2},{5,3},{6,4},{7,5},{8,14},{9,15},{10,... | collective-permute-start | bytes 1179656 | tf_op jit(solution)/shard_map/ppermute | solution.py:78
  43.9 0.8 copy-done.4
  44.8 1.9 %collective-permute-start.3 = (bf16[128,1536]{1,0:T(8,128)(2,1)S(1)}, bf16[128,1536]{1,0:T(8,128)(2,1)}, u32[]{:S(2)}, u32[]{:S(2)}) collective-permute-start(bf16[128,1536]{1,0:T(8,128)(2,1)S(1)} %slice.9), channel_id=1, source_target_pairs={{0,2},{1,3},{2,4},{3,5},{4,6},{5,7},{6,0},{7,1},{8,10},{9,11},{10,... | collective-permute-start | bytes 1179656 | tf_op jit(solution)/shard_map/ppermute | solution.py:78
  46.7 1.3 maximum_bitcast_fusion
  48.0 7.5 %all-to-all-start = ((bf16[8,3,128,256]{3,2,1,0:T(8,128)(2,1)}), bf16[8,3,128,256]{3,2,1,0:T(8,128)(2,1)S(1)}, u32[]{:S(2)}, u32[]{:S(2)}) async-start(bf16[8,3,128,256]{3,2,1,0:T(8,128)(2,1)} %maximum_bitcast_fusion), calls=%async_computation | async-start | bytes 3145728 | tf_op jit(solution)/shard_map/all_to_all | solution.py:385
  55.5 4.6 %collective-permute-start.5 = (bf16[128,3072]{1,0:T(8,128)(2,1)}, bf16[128,3072]{1,0:T(8,128)(2,1)}, u32[]{:S(2)}, u32[]{:S(2)}) collective-permute-start(bf16[128,3072]{1,0:T(8,128)(2,1)} %collective-permute-done.4.refs_4_), channel_id=1, source_target_pairs={{0,6},{1,7},{2,0},{3,1},{4,2},{5,3},{6,4},{7,5},{8,14},{9,15},{10,... | collective-permute-start | bytes 2359304 | tf_op jit(solution)/shard_map/ppermute | solution.py:78
  60.0 1.9 %collective-permute-start.7 = (bf16[128,3072]{1,0:T(8,128)(2,1)}, bf16[128,3072]{1,0:T(8,128)(2,1)}, u32[]{:S(2)}, u32[]{:S(2)}) collective-permute-start(bf16[128,3072]{1,0:T(8,128)(2,1)} %collective-permute-done.4.refs_4_), channel_id=1, source_target_pairs={{0,2},{1,3},{2,4},{3,5},{4,6},{5,7},{6,0},{7,1},{8,10},{9,11},{10,... | collective-permute-start | bytes 2359304 | tf_op jit(solution)/shard_map/ppermute | solution.py:78
  62.0 1.1 pad_maximum_fusion.1.refs_2_
  63.1 2.5 %collective-permute-start.6 = (bf16[2,128,1536]{2,1,0:T(8,128)(2,1)S(1)}, bf16[2,128,1536]{2,1,0:T(8,128)(2,1)}, u32[]{:S(2)}, u32[]{:S(2)}) collective-permute-start(bf16[2,128,1536]{2,1,0:T(8,128)(2,1)S(1)} %pad_maximum_fusion.1.refs_2_), channel_id=1, source_target_pairs={{0,1},{1,0},{2,3},{3,2},{4,5},{5,4},{6,7},{7,6},{8,9},{9,8},{10,11... | collective-permute-start | bytes 2359304 | tf_op jit(solution)/shard_map/ppermute | solution.py:78
  65.6 0.1 stack.71.place_ref
  65.7 9.6 %all-to-all-done.x_ref.refs_9_ = bf16[8,3,128,256]{3,2,1,0:T(8,128)(2,1)S(1)} async-done(((bf16[8,3,128,256]{3,2,1,0:T(8,128)(2,1)}), bf16[8,3,128,256]{3,2,1,0:T(8,128)(2,1)S(1)}, u32[]{:S(2)}, u32[]{:S(2)}) %all-to-all-start) | async-done | bytes 1572896 | tf_op jit(solution)/shard_map/all_to_all | solution.py:385
  75.3 8.2 %attention_forward.1 = (bf16[1024,256]{1,0:T(8,128)(2,1)S(1)}, bf16[2,1024,1024]{2,1,0:T(8,128)(2,1)}) custom-call(bf16[8,3,128,256]{3,2,1,0:T(8,128)(2,1)S(1)} %all-to-all-done.x_ref.refs_9_), custom_call_target="tpu_custom_call" | custom-call | flops 1000 | bytes 1000 | tf_op jit(solution)/shard_map/attention_forward/pallas_call | solution.py:153
  83.5 5.0 %collective-permute-done.5.refs_5_ = bf16[128,3072]{1,0:T(8,128)(2,1)} collective-permute-done((bf16[128,3072]{1,0:T(8,128)(2,1)}, bf16[128,3072]{1,0:T(8,128)(2,1)}, u32[]{:S(2)}, u32[]{:S(2)}) %collective-permute-start.5) | collective-permute-done | bytes 786464 | tf_op jit(solution)/shard_map/ppermute | solution.py:78
  88.4 1.8 %collective-permute-done.7.refs_7_ = bf16[128,3072]{1,0:T(8,128)(2,1)} collective-permute-done((bf16[128,3072]{1,0:T(8,128)(2,1)}, bf16[128,3072]{1,0:T(8,128)(2,1)}, u32[]{:S(2)}, u32[]{:S(2)}) %collective-permute-start.7) | collective-permute-done | bytes 786464 | tf_op jit(solution)/shard_map/ppermute | solution.py:78
  90.2 4.2 %weight_term.1 = (bf16[8,4,48,256]{3,2,1,0:T(8,128)(2,1)S(1)}, bf16[8,4,48,256]{3,2,1,0:T(8,128)(2,1)S(1)}) custom-call(s32[9]{0:T(128)S(1)} %stack.71.place_ref, bf16[128,3072]{1,0:T(8,128)(2,1)S(1)} %pad_maximum_fusion.refs_0_, bf16[128,3072]{1,0:T(8,128)(2,1)S(1)} %copy-done.2, bf16[2,128,1536]{2,1,0:T(8,128)(2,1)S(1)} %pad_maximum_fusion.1.refs_2_, ...), custom_call_target="tpu_custom_call" | custom-call | flops 1000 | bytes 1000 | tf_op jit(solution)/shard_map/weight_term/pallas_call | solution.py:224
  94.5 1.9 %collective-permute-start.9 = (bf16[8,4,48,256]{3,2,1,0:T(8,128)(2,1)S(1)}, bf16[8,4,48,256]{3,2,1,0:T(8,128)(2,1)S(1)}, u32[]{:S(2)}, u32[]{:S(2)}) collective-permute-start(bf16[8,4,48,256]{3,2,1,0:T(8,128)(2,1)S(1)} %get-tuple-element.19), channel_id=1, source_target_pairs={{0,8},{1,9},{2,10},{3,11},{4,12},{5,13},{6,14},{7,15},{8,0},{9,1},... | collective-permute-start | bytes 2359304 | tf_op jit(solution)/shard_map/ppermute | solution.py:78
  96.4 2.3 %collective-permute-done.9 = bf16[8,4,48,256]{3,2,1,0:T(8,128)(2,1)S(1)} collective-permute-done((bf16[8,4,48,256]{3,2,1,0:T(8,128)(2,1)S(1)}, bf16[8,4,48,256]{3,2,1,0:T(8,128)(2,1)S(1)}, u32[]{:S(2)}, u32[]{:S(2)}) %collective-permute-start.9) | collective-permute-done | bytes 786464 | tf_op jit(solution)/shard_map/ppermute | solution.py:78
  98.7 1.1 add_convert_fusion
  99.8 6.6 %all-to-all-start.1 = ((bf16[8,4,48,256]{3,2,1,0:T(8,128)(2,1)}), bf16[8,4,48,256]{3,2,1,0:T(8,128)(2,1)}, u32[]{:S(2)}, u32[]{:S(2)}) async-start(bf16[8,4,48,256]{3,2,1,0:T(8,128)(2,1)} %add_convert_fusion), calls=%async_computation.1 | async-start | bytes 1572864 | tf_op jit(solution)/shard_map/all_to_all | solution.py:401
  106.5 1.0 copy-done.8
  107.5 13.8 %project_and_backward.1 = bf16[8,3,128,256]{3,2,1,0:T(8,128)(2,1)} custom-call(s32[9]{0:T(128)S(1)} %stack.71.place_ref, bf16[128,3072]{1,0:T(8,128)(2,1)S(1)} %pad_maximum_fusion.refs_0_, bf16[128,3072]{1,0:T(8,128)(2,1)S(1)} %copy-done.3, bf16[2,128,1536]{2,1,0:T(8,128)(2,1)S(1)} %pad_maximum_fusion.1.refs_2_, bf16[128,3072]{1,0:T(8,128)(2,1)S(1)} %copy-done.6, ...), custom_call_target="tpu_custom_call" | custom-call | flops 3758096384 | bytes 34603008 | tf_op jit(solution)/shard_map/project_and_backward/pallas_call | solution.py:316
  121.3 6.5 %all-to-all-done.1 = bf16[8,4,48,256]{3,2,1,0:T(8,128)(2,1)} async-done(((bf16[8,4,48,256]{3,2,1,0:T(8,128)(2,1)}), bf16[8,4,48,256]{3,2,1,0:T(8,128)(2,1)}, u32[]{:S(2)}, u32[]{:S(2)}) %all-to-all-start.1) | async-done | bytes 786464 | tf_op jit(solution)/shard_map/all_to_all | solution.py:401
  127.8 5.2 %all-to-all-start.2 = ((bf16[8,3,128,256]{3,2,1,0:T(8,128)(2,1)}), bf16[8,3,128,256]{3,2,1,0:T(8,128)(2,1)S(1)}, u32[]{:S(2)}, u32[]{:S(2)}) async-start(bf16[8,3,128,256]{3,2,1,0:T(8,128)(2,1)} %project_and_backward.1), calls=%async_computation.2 | async-start | bytes 3145728 | tf_op jit(solution)/shard_map/all_to_all | solution.py:405
  133.0 1.2 reduce_sum.12
  134.2 13.5 %collective-permute-start.10 = (bf16[2,48,256]{2,1,0:T(8,128)(2,1)S(1)}, bf16[2,48,256]{2,1,0:T(8,128)(2,1)S(1)}, u32[]{:S(2)}, u32[]{:S(2)}) collective-permute-start(bf16[2,48,256]{2,1,0:T(8,128)(2,1)S(1)} %dynamic-slice_bitcast_fusion), channel_id=1, source_target_pairs={{0,128},{1,129},{2,130},{3,131},{4,132},{5,133},{6,134},{7,135},{8... | collective-permute-start | bytes 147464 | tf_op jit(solution)/shard_map/ppermute | solution.py:78
  147.8 2.0 %collective-permute-done.10 = bf16[2,48,256]{2,1,0:T(8,128)(2,1)S(1)} collective-permute-done((bf16[2,48,256]{2,1,0:T(8,128)(2,1)S(1)}, bf16[2,48,256]{2,1,0:T(8,128)(2,1)S(1)}, u32[]{:S(2)}, u32[]{:S(2)}) %collective-permute-start.10) | collective-permute-done | bytes 49184 | tf_op jit(solution)/shard_map/ppermute | solution.py:78
  149.8 8.3 %collective-permute-start.11 = (bf16[48,256]{1,0:T(8,128)(2,1)S(1)}, bf16[48,256]{1,0:T(8,128)(2,1)S(1)}, u32[]{:S(2)}, u32[]{:S(2)}) collective-permute-start(bf16[48,256]{1,0:T(8,128)(2,1)S(1)} %fusion.3), channel_id=1, source_target_pairs={{0,64},{1,65},{2,66},{3,67},{4,68},{5,69},{6,70},{7,71},{8,72},{9,... | collective-permute-start | bytes 73736 | tf_op jit(solution)/shard_map/ppermute | solution.py:78
  158.2 1.3 spread_features.1
  159.5 0.6 collective-permute-done.11
  160.2 0.6 fusion.2
  (34 shorter events, 0.2 us)
Async XLA Ops:
  7.2 24.2 %copy-start.9 = (bf16[1,3,96,2048]{3,2,1,0:T(8,128)(2,1)S(1)}, bf16[1,3,96,2048]{3,2,1,0:T(8,128)(2,1)}, u32[]{:S(2)}) copy-start(bf16[1,3,96,2048]{3,2,1,0:T(8,128)(2,1)} %param.9) | copy-start | bytes 3538948
  7.2 99.2 %all-gather.2.cloned.1.call-start = ((), (), s32[]{:S(2)}) async-start(), calls=%async_computation.3 | async-start | bytes 3244032 | tf_op jit(solution)/shard_map/all_gather | solution.py:369
  9.9 6.0 %collective-permute-start.8 = (bf16[2,48,256]{2,1,0:T(8,128)(2,1)S(1)}, bf16[2,48,256]{2,1,0:T(8,128)(2,1)S(1)}, u32[]{:S(2)}, u32[]{:S(2)}) collective-permute-start(bf16[2,48,256]{2,1,0:T(8,128)(2,1)S(1)} %get-tuple-element.30), channel_id=1, source_target_pairs={{0,256},{1,257},{2,258},{3,259},{4,260},{5,261},{6,262},{7,263},{8... | collective-permute-start | bytes 147464 | tf_op jit(solution)/shard_map/ppermute | solution.py:78
  17.7 20.6 %collective-permute-start = (bf16[128,3072]{1,0:T(8,128)(2,1)S(1)}, bf16[128,3072]{1,0:T(8,128)(2,1)S(1)}, u32[]{:S(2)}, u32[]{:S(2)}) collective-permute-start(bf16[128,3072]{1,0:T(8,128)(2,1)S(1)} %pad_maximum_fusion.refs_0_), channel_id=1, source_target_pairs={{0,6},{1,7},{2,0},{3,1},{4,2},{5,3},{6,4},{7,5},{8,14},{9,15},{10,... | collective-permute-start | bytes 2359304 | tf_op jit(solution)/shard_map/ppermute | solution.py:78
  22.6 21.3 %collective-permute-start.2 = (bf16[128,3072]{1,0:T(8,128)(2,1)S(1)}, bf16[128,3072]{1,0:T(8,128)(2,1)S(1)}, u32[]{:S(2)}, u32[]{:S(2)}) collective-permute-start(bf16[128,3072]{1,0:T(8,128)(2,1)S(1)} %pad_maximum_fusion.refs_0_), channel_id=1, source_target_pairs={{0,2},{1,3},{2,4},{3,5},{4,6},{5,7},{6,0},{7,1},{8,10},{9,11},{10,... | collective-permute-start | bytes 2359304 | tf_op jit(solution)/shard_map/ppermute | solution.py:78
  24.5 30.9 %collective-permute-start.4 = (bf16[128,3072]{1,0:T(8,128)(2,1)S(1)}, bf16[128,3072]{1,0:T(8,128)(2,1)}, u32[]{:S(2)}, u32[]{:S(2)}) collective-permute-start(bf16[128,3072]{1,0:T(8,128)(2,1)S(1)} %pad_maximum_fusion.refs_0_), channel_id=1, source_target_pairs={{0,1},{1,0},{2,3},{3,2},{4,5},{5,4},{6,7},{7,6},{8,9},{9,8},{10,11... | collective-permute-start | bytes 2359304 | tf_op jit(solution)/shard_map/ppermute | solution.py:78
  31.7 1.0 copy-start.10
  38.2 5.7 %copy-start.1 = (bf16[128,3072]{1,0:T(8,128)(2,1)}, bf16[128,3072]{1,0:T(8,128)(2,1)S(1)}, u32[]{:S(2)}) copy-start(bf16[128,3072]{1,0:T(8,128)(2,1)S(1)} %collective-permute-done.refs_1_) | copy-start | bytes 2359300
  38.3 23.7 %collective-permute-start.1 = (bf16[128,1536]{1,0:T(8,128)(2,1)S(1)}, bf16[128,1536]{1,0:T(8,128)(2,1)S(1)}, u32[]{:S(2)}, u32[]{:S(2)}) collective-permute-start(bf16[128,1536]{1,0:T(8,128)(2,1)S(1)} %slice.8), channel_id=1, source_target_pairs={{0,6},{1,7},{2,0},{3,1},{4,2},{5,3},{6,4},{7,5},{8,14},{9,15},{10,... | collective-permute-start | bytes 1179656 | tf_op jit(solution)/shard_map/ppermute | solution.py:78
  43.9 0.9 copy-start.4
  44.8 17.2 %collective-permute-start.3 = (bf16[128,1536]{1,0:T(8,128)(2,1)S(1)}, bf16[128,1536]{1,0:T(8,128)(2,1)}, u32[]{:S(2)}, u32[]{:S(2)}) collective-permute-start(bf16[128,1536]{1,0:T(8,128)(2,1)S(1)} %slice.9), channel_id=1, source_target_pairs={{0,2},{1,3},{2,4},{3,5},{4,6},{5,7},{6,0},{7,1},{8,10},{9,11},{10,... | collective-permute-start | bytes 1179656 | tf_op jit(solution)/shard_map/ppermute | solution.py:78
  48.0 27.3 %all-to-all-start = ((bf16[8,3,128,256]{3,2,1,0:T(8,128)(2,1)}), bf16[8,3,128,256]{3,2,1,0:T(8,128)(2,1)S(1)}, u32[]{:S(2)}, u32[]{:S(2)}) async-start(bf16[8,3,128,256]{3,2,1,0:T(8,128)(2,1)} %maximum_bitcast_fusion), calls=%async_computation | async-start | bytes 3145728 | tf_op jit(solution)/shard_map/all_to_all | solution.py:385
  55.5 33.0 %collective-permute-start.5 = (bf16[128,3072]{1,0:T(8,128)(2,1)}, bf16[128,3072]{1,0:T(8,128)(2,1)}, u32[]{:S(2)}, u32[]{:S(2)}) collective-permute-start(bf16[128,3072]{1,0:T(8,128)(2,1)} %collective-permute-done.4.refs_4_), channel_id=1, source_target_pairs={{0,6},{1,7},{2,0},{3,1},{4,2},{5,3},{6,4},{7,5},{8,14},{9,15},{10,... | collective-permute-start | bytes 2359304 | tf_op jit(solution)/shard_map/ppermute | solution.py:78
  60.0 30.2 %collective-permute-start.7 = (bf16[128,3072]{1,0:T(8,128)(2,1)}, bf16[128,3072]{1,0:T(8,128)(2,1)}, u32[]{:S(2)}, u32[]{:S(2)}) collective-permute-start(bf16[128,3072]{1,0:T(8,128)(2,1)} %collective-permute-done.4.refs_4_), channel_id=1, source_target_pairs={{0,2},{1,3},{2,4},{3,5},{4,6},{5,7},{6,0},{7,1},{8,10},{9,11},{10,... | collective-permute-start | bytes 2359304 | tf_op jit(solution)/shard_map/ppermute | solution.py:78
  63.1 27.1 %collective-permute-start.6 = (bf16[2,128,1536]{2,1,0:T(8,128)(2,1)S(1)}, bf16[2,128,1536]{2,1,0:T(8,128)(2,1)}, u32[]{:S(2)}, u32[]{:S(2)}) collective-permute-start(bf16[2,128,1536]{2,1,0:T(8,128)(2,1)S(1)} %pad_maximum_fusion.1.refs_2_), channel_id=1, source_target_pairs={{0,1},{1,0},{2,3},{3,2},{4,5},{5,4},{6,7},{7,6},{8,9},{9,8},{10,11... | collective-permute-start | bytes 2359304 | tf_op jit(solution)/shard_map/ppermute | solution.py:78
  75.3 19.2 %copy-start = (bf16[8,3,128,256]{3,2,1,0:T(8,128)(2,1)}, bf16[8,3,128,256]{3,2,1,0:T(8,128)(2,1)S(1)}, u32[]{:S(2)}) copy-start(bf16[8,3,128,256]{3,2,1,0:T(8,128)(2,1)S(1)} %all-to-all-done.x_ref.refs_9_) | copy-start | bytes 4718596
  75.3 14.9 %copy-start.2 = (bf16[128,3072]{1,0:T(8,128)(2,1)S(1)}, bf16[128,3072]{1,0:T(8,128)(2,1)}, u32[]{:S(2)}) copy-start(bf16[128,3072]{1,0:T(8,128)(2,1)} %copy-done.1) | copy-start | bytes 2359300
  75.3 14.9 %copy-start.5 = (bf16[128,3072]{1,0:T(8,128)(2,1)S(1)}, bf16[128,3072]{1,0:T(8,128)(2,1)}, u32[]{:S(2)}) copy-start(bf16[128,3072]{1,0:T(8,128)(2,1)} %copy-done.4) | copy-start | bytes 2359300
  83.5 11.0 %copy-start.7 = (bf16[1024,256]{1,0:T(8,128)(2,1)}, bf16[1024,256]{1,0:T(8,128)(2,1)S(1)}, u32[]{:S(2)}) copy-start(bf16[1024,256]{1,0:T(8,128)(2,1)S(1)} %get-tuple-element.20.refs_8_.refs_11_) | copy-start | bytes 1572868
  94.5 4.2 %collective-permute-start.9 = (bf16[8,4,48,256]{3,2,1,0:T(8,128)(2,1)S(1)}, bf16[8,4,48,256]{3,2,1,0:T(8,128)(2,1)S(1)}, u32[]{:S(2)}, u32[]{:S(2)}) collective-permute-start(bf16[8,4,48,256]{3,2,1,0:T(8,128)(2,1)S(1)} %get-tuple-element.19), channel_id=1, source_target_pairs={{0,8},{1,9},{2,10},{3,11},{4,12},{5,13},{6,14},{7,15},{8,0},{9,1},... | collective-permute-start | bytes 2359304 | tf_op jit(solution)/shard_map/ppermute | solution.py:78
  98.7 7.8 %copy-start.3 = (bf16[128,3072]{1,0:T(8,128)(2,1)S(1)}, bf16[128,3072]{1,0:T(8,128)(2,1)}, u32[]{:S(2)}) copy-start(bf16[128,3072]{1,0:T(8,128)(2,1)} %copy-done.1) | copy-start | bytes 2359300
  98.7 7.8 %copy-start.6 = (bf16[128,3072]{1,0:T(8,128)(2,1)S(1)}, bf16[128,3072]{1,0:T(8,128)(2,1)}, u32[]{:S(2)}) copy-start(bf16[128,3072]{1,0:T(8,128)(2,1)} %copy-done.4) | copy-start | bytes 2359300
  99.8 28.0 %all-to-all-start.1 = ((bf16[8,4,48,256]{3,2,1,0:T(8,128)(2,1)}), bf16[8,4,48,256]{3,2,1,0:T(8,128)(2,1)}, u32[]{:S(2)}, u32[]{:S(2)}) async-start(bf16[8,4,48,256]{3,2,1,0:T(8,128)(2,1)} %add_convert_fusion), calls=%async_computation.1 | async-start | bytes 1572864 | tf_op jit(solution)/shard_map/all_to_all | solution.py:401
  106.4 1.0 copy-start.8
  127.8 30.4 %all-to-all-start.2 = ((bf16[8,3,128,256]{3,2,1,0:T(8,128)(2,1)}), bf16[8,3,128,256]{3,2,1,0:T(8,128)(2,1)S(1)}, u32[]{:S(2)}, u32[]{:S(2)}) async-start(bf16[8,3,128,256]{3,2,1,0:T(8,128)(2,1)} %project_and_backward.1), calls=%async_computation.2 | async-start | bytes 3145728 | tf_op jit(solution)/shard_map/all_to_all | solution.py:405
  134.2 15.6 %collective-permute-start.10 = (bf16[2,48,256]{2,1,0:T(8,128)(2,1)S(1)}, bf16[2,48,256]{2,1,0:T(8,128)(2,1)S(1)}, u32[]{:S(2)}, u32[]{:S(2)}) collective-permute-start(bf16[2,48,256]{2,1,0:T(8,128)(2,1)S(1)} %dynamic-slice_bitcast_fusion), channel_id=1, source_target_pairs={{0,128},{1,129},{2,130},{3,131},{4,132},{5,133},{6,134},{7,135},{8... | collective-permute-start | bytes 147464 | tf_op jit(solution)/shard_map/ppermute | solution.py:78
  149.8 10.3 %collective-permute-start.11 = (bf16[48,256]{1,0:T(8,128)(2,1)S(1)}, bf16[48,256]{1,0:T(8,128)(2,1)S(1)}, u32[]{:S(2)}, u32[]{:S(2)}) collective-permute-start(bf16[48,256]{1,0:T(8,128)(2,1)S(1)} %fusion.3), channel_id=1, source_target_pairs={{0,64},{1,65},{2,66},{3,67},{4,68},{5,69},{6,70},{7,71},{8,72},{9,... | collective-permute-start | bytes 73736 | tf_op jit(solution)/shard_map/ppermute | solution.py:78
Sparse Core Ops, SparseCore 0:
  16.6 77.4 all-gather.1

commit v6 on v4

--- a/solution.py
+++ b/solution.py
@@ -78,10 +78,6 @@
     return lax.ppermute(x, AXES, pairs)
 
 
-def dequant(values, scales):
-    return (values.astype(jnp.float32) * jnp.repeat(scales, HD, axis=1)).astype(jnp.bfloat16)
-
-
 def plus(a, b):
     return a.astype(jnp.float32) + b.astype(jnp.float32)
 
@@ -260,12 +256,15 @@
     pieces, rest = refs[:SP], refs[SP:]
     w_ref, x_ref, probs_ref, att, out_ref = rest[:5]
     grad, text, image, weight, joint, probs, slopes, sems, dy_sems, qkv_sems = rest[5:]
+    x_lo = place_ref[SP + 1]
     copies = [
         pltpu.make_async_copy(
-            w_ref.at[:, x_lo, stream], weight.at[stream, x_lo], sems.at[2 * stream + x_lo]
+            w_ref.at[:, n, stream],
+            weight.at[stream, (x_lo + n) % 2],
+            sems.at[2 * stream + n],
         )
         for stream in range(2)
-        for x_lo in range(2)
+        for n in range(2)
     ]
     for copy in copies[2:]:
         copy.start()
@@ -349,26 +348,48 @@
     )(back)
 
 
-def gather_weights(wv_txt, sc_txt, wv_img, sc_img, x_lo):
-    own = jnp.stack([dequant(wv_txt, sc_txt), dequant(wv_img, sc_img)])
-    other = send(own, SWAP_X_LO)
-    pair = jnp.where(x_lo == 0, jnp.stack([own, other]), jnp.stack([other, own]))
+def dequant_kernel(txt_ref, txt_scales, img_ref, img_scales, out_ref):
+    for stream, (values, scales) in enumerate(((txt_ref, txt_scales), (img_ref, img_scales))):
+        by_row = scales[...].T
+        for head in range(HEADS):
+            window = slice(head * HD, (head + 1) * HD)
+            scaled = values[:, window].astype(jnp.float32) * by_row[:, head : head + 1]
+            out_ref[stream, :, window] = scaled.astype(jnp.bfloat16)
+
+
+def dequant(wv_txt, sc_txt, wv_img, sc_img):
+    return pl.pallas_call(
+        dequant_kernel,
+        out_shape=jax.ShapeDtypeStruct((2, ROWS, COLS), jnp.bfloat16),
+        in_specs=[VMEM] * 4,
+        out_specs=VMEM,
+        cost_estimate=LIGHT,
+        name="dequantize",
+    )(wv_txt, sc_txt.T, wv_img, sc_img.T)
+
+
+def gather_weights(own, other):
+    pair = jnp.stack([own, other])
     return lax.all_gather(pair, AXES, axis=0, axis_index_groups=Z_CORE_GROUPS)
 
 
 def local(qkv_txt, qkv_img, dy_txt, dy_img, wv_txt, sc_txt, wv_img, sc_img):
     fsdp, sp = lax.axis_index("fsdp"), lax.axis_index("sp")
     core, x_lo, z = fsdp % 2, fsdp // 32, (fsdp // 2) % 16
-    place = jnp.stack(slots(sp) + [core]).astype(jnp.int32)
-
+    place = jnp.stack(slots(sp) + [core, x_lo]).astype(jnp.int32)
+
+    weights = dequant(wv_txt, sc_txt, wv_img, sc_img)
+    other = send(weights, SWAP_X_LO)
     own = jnp.concatenate([dy_txt[0], dy_img[0]], axis=0)
+    other, own = lax.optimization_barrier((other, own))
+    w = gather_weights(weights, other)
     by_y = {k: send(own, FROM_Y[k]) for k in (1, 3)}
     across = send(own, SWAP_X_HI)
 
     x = jnp.concatenate(
         [qkv_txt[0].reshape(3, TXT, SP, COLS), qkv_img[0].reshape(3, IMG, SP, COLS)], axis=1
     ).transpose(2, 0, 1, 3)
-    w = gather_weights(wv_txt, sc_txt, wv_img, sc_img, x_lo)
+    by_y[1], x = lax.optimization_barrier((by_y[1], x))
     x = lax.all_to_all(x, "sp", 0, 0, tiled=True)
     att, probs = forward(x)
 

time: 169 us -> 166 us (0.982)
  local copies, waits for them, and re-layouts: 5.39 us -> 3.57 us
  Pallas kernels: 28.6 us -> 30.3 us
    all_to_all x1, waiting for transfers between devices: 9.56 us -> 7.35 us  [local(): x = lax.all_to_all(x, 'sp', 0, 0, tiled=True)]
    ppermute x12, waiting for transfers between devices: 18.7 us -> 20.6 us  [send(): return lax.ppermute(x, AXES, pairs)]
  transfers between devices with their start and end apart: 16 -> 16, of which waited for: 9 -> 10; matrix products, arithmetic and copies ran while one was open for 4% -> 4% of each run, Pallas kernels for 17% -> 17%
where the time goes in v6:
time: 166 us; the launch traced here: 165 us
  starting transfers between devices  75.5 us (45%)
  waiting for transfers between devices  34.5 us (21%)
  Pallas kernels  30.3 us (18%)
  between operations  14.5 us (9%)
  other arithmetic  7.15 us (4%)
  local copies, waits for them, and re-layouts  3.57 us (2%)
    ppermute x12, starting transfers between devices, send(): return lax.ppermute(x, AXES, pairs)  56.5 us
    ppermute x12, waiting for transfers between devices, send(): return lax.ppermute(x, AXES, pairs)  20.6 us
    pallas_call x1, Pallas kernels, backward(): pl.pallas_call(backward_kernel, out_shape=jax.ShapeDtypeStruct((SP, 3, TO...  13.8 us
    pallas_call x1, Pallas kernels, forward(): pl.pallas_call(forward_kernel, out_shape=(jax.ShapeDtypeStruct((LENGTH, C...  9.23 us
    all_to_all x1, starting transfers between devices, local(): x = lax.all_to_all(x, 'sp', 0, 0, tiled=True)  7.47 us
    all_to_all x1, waiting for transfers between devices, local(): x = lax.all_to_all(x, 'sp', 0, 0, tiled=True)  7.35 us
    all_to_all x1, starting transfers between devices, local(): lax.all_to_all(total, AXES, 0, 0, axis_index_groups=NEAR_GROUPS, tiled=True)  6.62 us
    all_to_all x1, waiting for transfers between devices, local(): lax.all_to_all(total, AXES, 0, 0, axis_index_groups=NEAR_GROUPS, tiled=True)  6.53 us
  transfers between devices with their start and end apart: 16, of which 10 were waited for; matrix products, arithmetic and copies ran while one was open for 4% of the time, Pallas kernels for 17%

profile of v6, /device:TPU:4, one launch (start us, length us, event | category | flops | bytes accessed | tf_op | source)
XLA Modules:
  0.0 165.4 jit_solution(16027964471357682019)
XLA Ops:
  7.2 0.0 all-gather.3.cloned.1.call-start
  7.2 1.6 dequantize.1
  8.9 3.2 %collective-permute-start = (bf16[2,48,256]{2,1,0:T(8,128)(2,1)}, bf16[2,48,256]{2,1,0:T(8,128)(2,1)S(1)}, u32[]{:S(2)}, u32[]{:S(2)}) collective-permute-start(bf16[2,48,256]{2,1,0:T(8,128)(2,1)} %dequantize.1), channel_id=1, source_target_pairs={{0,256},{1,257},{2,258},{3,259},{4,260},{5,261},{6,262},{7,263},{8... | collective-permute-start | bytes 147464 | tf_op jit(solution)/shard_map/ppermute | solution.py:78
  12.1 1.2 pad_maximum_fusion.refs_0_
  13.3 1.9 %collective-permute-done = bf16[2,48,256]{2,1,0:T(8,128)(2,1)S(1)} collective-permute-done((bf16[2,48,256]{2,1,0:T(8,128)(2,1)}, bf16[2,48,256]{2,1,0:T(8,128)(2,1)S(1)}, u32[]{:S(2)}, u32[]{:S(2)}) %collective-permute-start) | collective-permute-done | bytes 49184 | tf_op jit(solution)/shard_map/ppermute | solution.py:78
  15.2 0.7 pad_maximum_fusion.2
  15.8 0.0 all-gather.3.cloned.1.call-update
  15.9 4.9 %collective-permute-start.1 = (bf16[128,3072]{1,0:T(8,128)(2,1)S(1)}, bf16[128,3072]{1,0:T(8,128)(2,1)S(1)}, u32[]{:S(2)}, u32[]{:S(2)}) collective-permute-start(bf16[128,3072]{1,0:T(8,128)(2,1)S(1)} %pad_maximum_fusion.refs_0_), channel_id=1, source_target_pairs={{0,6},{1,7},{2,0},{3,1},{4,2},{5,3},{6,4},{7,5},{8,14},{9,15},{10,... | collective-permute-start | bytes 2359304 | tf_op jit(solution)/shard_map/ppermute | solution.py:78
  20.8 1.9 %collective-permute-start.3 = (bf16[128,3072]{1,0:T(8,128)(2,1)S(1)}, bf16[128,3072]{1,0:T(8,128)(2,1)S(1)}, u32[]{:S(2)}, u32[]{:S(2)}) collective-permute-start(bf16[128,3072]{1,0:T(8,128)(2,1)S(1)} %pad_maximum_fusion.refs_0_), channel_id=1, source_target_pairs={{0,2},{1,3},{2,4},{3,5},{4,6},{5,7},{6,0},{7,1},{8,10},{9,11},{10,... | collective-permute-start | bytes 2359304 | tf_op jit(solution)/shard_map/ppermute | solution.py:78
  22.7 6.8 %collective-permute-start.5 = (bf16[128,3072]{1,0:T(8,128)(2,1)S(1)}, bf16[128,3072]{1,0:T(8,128)(2,1)}, u32[]{:S(2)}, u32[]{:S(2)}) collective-permute-start(bf16[128,3072]{1,0:T(8,128)(2,1)S(1)} %pad_maximum_fusion.refs_0_), channel_id=1, source_target_pairs={{0,1},{1,0},{2,3},{3,2},{4,5},{5,4},{6,7},{7,6},{8,9},{9,8},{10,11... | collective-permute-start | bytes 2359304 | tf_op jit(solution)/shard_map/ppermute | solution.py:78
  29.5 0.4 copy.16
  29.9 0.3 copy.14
  30.2 0.7 copy-done.10
  30.9 0.1 copy.15
  31.0 0.1 copy.13
  31.1 1.3 maximum_bitcast_fusion
  32.3 4.1 %collective-permute-done.1.refs_1_ = bf16[128,3072]{1,0:T(8,128)(2,1)S(1)} collective-permute-done((bf16[128,3072]{1,0:T(8,128)(2,1)S(1)}, bf16[128,3072]{1,0:T(8,128)(2,1)S(1)}, u32[]{:S(2)}, u32[]{:S(2)}) %collective-permute-start.1) | collective-permute-done | bytes 786464 | tf_op jit(solution)/shard_map/ppermute | solution.py:78
  36.5 5.6 %collective-permute-start.2 = (bf16[128,1536]{1,0:T(8,128)(2,1)S(1)}, bf16[128,1536]{1,0:T(8,128)(2,1)S(1)}, u32[]{:S(2)}, u32[]{:S(2)}) collective-permute-start(bf16[128,1536]{1,0:T(8,128)(2,1)S(1)} %slice.6), channel_id=1, source_target_pairs={{0,6},{1,7},{2,0},{3,1},{4,2},{5,3},{6,4},{7,5},{8,14},{9,15},{10,... | collective-permute-start | bytes 1179656 | tf_op jit(solution)/shard_map/ppermute | solution.py:78
  42.1 0.8 copy-done.4
  43.0 1.9 %collective-permute-start.4 = (bf16[128,1536]{1,0:T(8,128)(2,1)S(1)}, bf16[128,1536]{1,0:T(8,128)(2,1)}, u32[]{:S(2)}, u32[]{:S(2)}) collective-permute-start(bf16[128,1536]{1,0:T(8,128)(2,1)S(1)} %slice.8), channel_id=1, source_target_pairs={{0,2},{1,3},{2,4},{3,5},{4,6},{5,7},{6,0},{7,1},{8,10},{9,11},{10,... | collective-permute-start | bytes 1179656 | tf_op jit(solution)/shard_map/ppermute | solution.py:78
  44.9 7.5 %all-to-all-start = ((bf16[8,3,128,256]{3,2,1,0:T(8,128)(2,1)}), bf16[8,3,128,256]{3,2,1,0:T(8,128)(2,1)S(1)}, u32[]{:S(2)}, u32[]{:S(2)}) async-start(bf16[8,3,128,256]{3,2,1,0:T(8,128)(2,1)} %maximum_bitcast_fusion), calls=%async_computation | async-start | bytes 3145728 | tf_op jit(solution)/shard_map/all_to_all | solution.py:393
  52.4 4.6 %collective-permute-start.6 = (bf16[128,3072]{1,0:T(8,128)(2,1)}, bf16[128,3072]{1,0:T(8,128)(2,1)}, u32[]{:S(2)}, u32[]{:S(2)}) collective-permute-start(bf16[128,3072]{1,0:T(8,128)(2,1)} %collective-permute-done.5.refs_4_), channel_id=1, source_target_pairs={{0,6},{1,7},{2,0},{3,1},{4,2},{5,3},{6,4},{7,5},{8,14},{9,15},{10,... | collective-permute-start | bytes 2359304 | tf_op jit(solution)/shard_map/ppermute | solution.py:78
  56.9 1.9 %collective-permute-start.8 = (bf16[128,3072]{1,0:T(8,128)(2,1)}, bf16[128,3072]{1,0:T(8,128)(2,1)}, u32[]{:S(2)}, u32[]{:S(2)}) collective-permute-start(bf16[128,3072]{1,0:T(8,128)(2,1)} %collective-permute-done.5.refs_4_), channel_id=1, source_target_pairs={{0,2},{1,3},{2,4},{3,5},{4,6},{5,7},{6,0},{7,1},{8,10},{9,11},{10,... | collective-permute-start | bytes 2359304 | tf_op jit(solution)/shard_map/ppermute | solution.py:78
  58.9 3.7 %collective-permute-done.4 = bf16[128,1536]{1,0:T(8,128)(2,1)} collective-permute-done((bf16[128,1536]{1,0:T(8,128)(2,1)S(1)}, bf16[128,1536]{1,0:T(8,128)(2,1)}, u32[]{:S(2)}, u32[]{:S(2)}) %collective-permute-start.4) | collective-permute-done | bytes 393248 | tf_op jit(solution)/shard_map/ppermute | solution.py:78
  62.6 1.1 pad_maximum_fusion.1.refs_2_
  63.7 1.9 %collective-permute-start.7 = (bf16[2,128,1536]{2,1,0:T(8,128)(2,1)S(1)}, bf16[2,128,1536]{2,1,0:T(8,128)(2,1)}, u32[]{:S(2)}, u32[]{:S(2)}) collective-permute-start(bf16[2,128,1536]{2,1,0:T(8,128)(2,1)S(1)} %pad_maximum_fusion.1.refs_2_), channel_id=1, source_target_pairs={{0,1},{1,0},{2,3},{3,2},{4,5},{5,4},{6,7},{7,6},{8,9},{9,8},{10,11... | collective-permute-start | bytes 2359304 | tf_op jit(solution)/shard_map/ppermute | solution.py:78
  65.7 0.1 stack.61.place_ref
  65.8 7.3 %all-to-all-done.x_ref.refs_9_ = bf16[8,3,128,256]{3,2,1,0:T(8,128)(2,1)S(1)} async-done(((bf16[8,3,128,256]{3,2,1,0:T(8,128)(2,1)}), bf16[8,3,128,256]{3,2,1,0:T(8,128)(2,1)S(1)}, u32[]{:S(2)}, u32[]{:S(2)}) %all-to-all-start) | async-done | bytes 1572896 | tf_op jit(solution)/shard_map/all_to_all | solution.py:393
  73.2 9.2 %attention_forward.1 = (bf16[1024,256]{1,0:T(8,128)(2,1)S(1)}, bf16[2,1024,1024]{2,1,0:T(8,128)(2,1)}) custom-call(bf16[8,3,128,256]{3,2,1,0:T(8,128)(2,1)S(1)} %all-to-all-done.x_ref.refs_9_), custom_call_target="tpu_custom_call" | custom-call | flops 1000 | bytes 1000 | tf_op jit(solution)/shard_map/attention_forward/pallas_call | solution.py:138
  82.4 2.9 %collective-permute-done.6.refs_5_ = bf16[128,3072]{1,0:T(8,128)(2,1)} collective-permute-done((bf16[128,3072]{1,0:T(8,128)(2,1)}, bf16[128,3072]{1,0:T(8,128)(2,1)}, u32[]{:S(2)}, u32[]{:S(2)}) %collective-permute-start.6) | collective-permute-done | bytes 786464 | tf_op jit(solution)/shard_map/ppermute | solution.py:78
  85.3 3.0 %collective-permute-done.8.refs_7_ = bf16[128,3072]{1,0:T(8,128)(2,1)} collective-permute-done((bf16[128,3072]{1,0:T(8,128)(2,1)}, bf16[128,3072]{1,0:T(8,128)(2,1)}, u32[]{:S(2)}, u32[]{:S(2)}) %collective-permute-start.8) | collective-permute-done | bytes 786464 | tf_op jit(solution)/shard_map/ppermute | solution.py:78
  88.4 4.3 %weight_term.1 = (bf16[8,4,48,256]{3,2,1,0:T(8,128)(2,1)S(1)}, bf16[8,4,48,256]{3,2,1,0:T(8,128)(2,1)S(1)}) custom-call(s32[10]{0:T(128)S(1)} %stack.61.place_ref, bf16[128,3072]{1,0:T(8,128)(2,1)S(1)} %pad_maximum_fusion.refs_0_, bf16[128,3072]{1,0:T(8,128)(2,1)S(1)} %copy-done.2, bf16[2,128,1536]{2,1,0:T(8,128)(2,1)S(1)} %pad_maximum_fusion.1.refs_2_, ...), custom_call_target="tpu_custom_call" | custom-call | flops 1000 | bytes 1000 | tf_op jit(solution)/shard_map/weight_term/pallas_call | solution.py:207
  92.7 1.9 %collective-permute-start.9 = (bf16[8,4,48,256]{3,2,1,0:T(8,128)(2,1)S(1)}, bf16[8,4,48,256]{3,2,1,0:T(8,128)(2,1)S(1)}, u32[]{:S(2)}, u32[]{:S(2)}) collective-permute-start(bf16[8,4,48,256]{3,2,1,0:T(8,128)(2,1)S(1)} %get-tuple-element.27), channel_id=1, source_target_pairs={{0,8},{1,9},{2,10},{3,11},{4,12},{5,13},{6,14},{7,15},{8,0},{9,1},... | collective-permute-start | bytes 2359304 | tf_op jit(solution)/shard_map/ppermute | solution.py:78
  94.6 2.3 %collective-permute-done.9 = bf16[8,4,48,256]{3,2,1,0:T(8,128)(2,1)S(1)} collective-permute-done((bf16[8,4,48,256]{3,2,1,0:T(8,128)(2,1)S(1)}, bf16[8,4,48,256]{3,2,1,0:T(8,128)(2,1)S(1)}, u32[]{:S(2)}, u32[]{:S(2)}) %collective-permute-start.9) | collective-permute-done | bytes 786464 | tf_op jit(solution)/shard_map/ppermute | solution.py:78
  96.9 1.1 add_convert_fusion
  98.0 6.6 %all-to-all-start.1 = ((bf16[8,4,48,256]{3,2,1,0:T(8,128)(2,1)}), bf16[8,4,48,256]{3,2,1,0:T(8,128)(2,1)}, u32[]{:S(2)}, u32[]{:S(2)}) async-start(bf16[8,4,48,256]{3,2,1,0:T(8,128)(2,1)} %add_convert_fusion), calls=%async_computation.1 | async-start | bytes 1572864 | tf_op jit(solution)/shard_map/all_to_all | solution.py:409
  104.6 0.0 all-gather.3.cloned.1.call-done
  104.6 1.0 copy-done.8
  105.7 13.8 %project_and_backward.1 = bf16[8,3,128,256]{3,2,1,0:T(8,128)(2,1)} custom-call(s32[10]{0:T(128)S(1)} %stack.61.place_ref, bf16[128,3072]{1,0:T(8,128)(2,1)S(1)} %pad_maximum_fusion.refs_0_, bf16[128,3072]{1,0:T(8,128)(2,1)S(1)} %copy-done.3, bf16[2,128,1536]{2,1,0:T(8,128)(2,1)S(1)} %pad_maximum_fusion.1.refs_2_, bf16[128,3072]{1,0:T(8,128)(2,1)S(1)} %copy-done.6, ...), custom_call_target="tpu_custom_call" | custom-call | flops 3758096384 | bytes 34603008 | tf_op jit(solution)/shard_map/project_and_backward/pallas_call | solution.py:302
  119.5 6.5 %all-to-all-done.1 = bf16[8,4,48,256]{3,2,1,0:T(8,128)(2,1)} async-done(((bf16[8,4,48,256]{3,2,1,0:T(8,128)(2,1)}), bf16[8,4,48,256]{3,2,1,0:T(8,128)(2,1)}, u32[]{:S(2)}, u32[]{:S(2)}) %all-to-all-start.1) | async-done | bytes 786464 | tf_op jit(solution)/shard_map/all_to_all | solution.py:409
  126.0 4.8 %all-to-all-start.2 = ((bf16[8,3,128,256]{3,2,1,0:T(8,128)(2,1)}), bf16[8,3,128,256]{3,2,1,0:T(8,128)(2,1)S(1)}, u32[]{:S(2)}, u32[]{:S(2)}) async-start(bf16[8,3,128,256]{3,2,1,0:T(8,128)(2,1)} %project_and_backward.1), calls=%async_computation.2 | async-start | bytes 3145728 | tf_op jit(solution)/shard_map/all_to_all | solution.py:413
  130.8 1.2 reduce_sum.12
  132.1 13.5 %collective-permute-start.10 = (bf16[2,48,256]{2,1,0:T(8,128)(2,1)S(1)}, bf16[2,48,256]{2,1,0:T(8,128)(2,1)S(1)}, u32[]{:S(2)}, u32[]{:S(2)}) collective-permute-start(bf16[2,48,256]{2,1,0:T(8,128)(2,1)S(1)} %dynamic-slice_bitcast_fusion), channel_id=1, source_target_pairs={{0,128},{1,129},{2,130},{3,131},{4,132},{5,133},{6,134},{7,135},{8... | collective-permute-start | bytes 147464 | tf_op jit(solution)/shard_map/ppermute | solution.py:78
  145.6 2.0 %collective-permute-done.10 = bf16[2,48,256]{2,1,0:T(8,128)(2,1)S(1)} collective-permute-done((bf16[2,48,256]{2,1,0:T(8,128)(2,1)S(1)}, bf16[2,48,256]{2,1,0:T(8,128)(2,1)S(1)}, u32[]{:S(2)}, u32[]{:S(2)}) %collective-permute-start.10) | collective-permute-done | bytes 49184 | tf_op jit(solution)/shard_map/ppermute | solution.py:78
  147.6 8.3 %collective-permute-start.11 = (bf16[48,256]{1,0:T(8,128)(2,1)S(1)}, bf16[48,256]{1,0:T(8,128)(2,1)S(1)}, u32[]{:S(2)}, u32[]{:S(2)}) collective-permute-start(bf16[48,256]{1,0:T(8,128)(2,1)S(1)} %fusion.1), channel_id=1, source_target_pairs={{0,64},{1,65},{2,66},{3,67},{4,68},{5,69},{6,70},{7,71},{8,72},{9,... | collective-permute-start | bytes 73736 | tf_op jit(solution)/shard_map/ppermute | solution.py:78
  156.0 1.3 spread_features.1
  157.4 0.6 collective-permute-done.11
  158.0 0.6 fusion
  (31 shorter events, 0.1 us)
Async XLA Ops:
  7.2 22.4 %copy-start.9 = (bf16[1,3,96,2048]{3,2,1,0:T(8,128)(2,1)S(1)}, bf16[1,3,96,2048]{3,2,1,0:T(8,128)(2,1)}, u32[]{:S(2)}) copy-start(bf16[1,3,96,2048]{3,2,1,0:T(8,128)(2,1)} %param.9) | copy-start | bytes 3538948
  7.2 97.4 %all-gather.3.cloned.1.call-start = ((), (), s32[]{:S(2)}) async-start(), calls=%async_computation.3 | async-start | bytes 3244032 | tf_op jit(solution)/shard_map/all_gather | solution.py:373
  8.9 6.3 %copy-start.11 = (bf16[2,48,256]{2,1,0:T(8,128)(2,1)S(1)}, bf16[2,48,256]{2,1,0:T(8,128)(2,1)}, u32[]{:S(2)}) copy-start(bf16[2,48,256]{2,1,0:T(8,128)(2,1)} %dequantize.1) | copy-start | bytes 147460
  8.9 6.3 %collective-permute-start = (bf16[2,48,256]{2,1,0:T(8,128)(2,1)}, bf16[2,48,256]{2,1,0:T(8,128)(2,1)S(1)}, u32[]{:S(2)}, u32[]{:S(2)}) collective-permute-start(bf16[2,48,256]{2,1,0:T(8,128)(2,1)} %dequantize.1), channel_id=1, source_target_pairs={{0,256},{1,257},{2,258},{3,259},{4,260},{5,261},{6,262},{7,263},{8... | collective-permute-start | bytes 147464 | tf_op jit(solution)/shard_map/ppermute | solution.py:78
  15.9 20.6 %collective-permute-start.1 = (bf16[128,3072]{1,0:T(8,128)(2,1)S(1)}, bf16[128,3072]{1,0:T(8,128)(2,1)S(1)}, u32[]{:S(2)}, u32[]{:S(2)}) collective-permute-start(bf16[128,3072]{1,0:T(8,128)(2,1)S(1)} %pad_maximum_fusion.refs_0_), channel_id=1, source_target_pairs={{0,6},{1,7},{2,0},{3,1},{4,2},{5,3},{6,4},{7,5},{8,14},{9,15},{10,... | collective-permute-start | bytes 2359304 | tf_op jit(solution)/shard_map/ppermute | solution.py:78
  20.8 21.3 %collective-permute-start.3 = (bf16[128,3072]{1,0:T(8,128)(2,1)S(1)}, bf16[128,3072]{1,0:T(8,128)(2,1)S(1)}, u32[]{:S(2)}, u32[]{:S(2)}) collective-permute-start(bf16[128,3072]{1,0:T(8,128)(2,1)S(1)} %pad_maximum_fusion.refs_0_), channel_id=1, source_target_pairs={{0,2},{1,3},{2,4},{3,5},{4,6},{5,7},{6,0},{7,1},{8,10},{9,11},{10,... | collective-permute-start | bytes 2359304 | tf_op jit(solution)/shard_map/ppermute | solution.py:78
  22.7 29.6 %collective-permute-start.5 = (bf16[128,3072]{1,0:T(8,128)(2,1)S(1)}, bf16[128,3072]{1,0:T(8,128)(2,1)}, u32[]{:S(2)}, u32[]{:S(2)}) collective-permute-start(bf16[128,3072]{1,0:T(8,128)(2,1)S(1)} %pad_maximum_fusion.refs_0_), channel_id=1, source_target_pairs={{0,1},{1,0},{2,3},{3,2},{4,5},{5,4},{6,7},{7,6},{8,9},{9,8},{10,11... | collective-permute-start | bytes 2359304 | tf_op jit(solution)/shard_map/ppermute | solution.py:78
  29.9 1.0 copy-start.10
  36.4 5.7 %copy-start.1 = (bf16[128,3072]{1,0:T(8,128)(2,1)}, bf16[128,3072]{1,0:T(8,128)(2,1)S(1)}, u32[]{:S(2)}) copy-start(bf16[128,3072]{1,0:T(8,128)(2,1)S(1)} %collective-permute-done.1.refs_1_) | copy-start | bytes 2359300
  36.5 22.4 %collective-permute-start.2 = (bf16[128,1536]{1,0:T(8,128)(2,1)S(1)}, bf16[128,1536]{1,0:T(8,128)(2,1)S(1)}, u32[]{:S(2)}, u32[]{:S(2)}) collective-permute-start(bf16[128,1536]{1,0:T(8,128)(2,1)S(1)} %slice.6), channel_id=1, source_target_pairs={{0,6},{1,7},{2,0},{3,1},{4,2},{5,3},{6,4},{7,5},{8,14},{9,15},{10,... | collective-permute-start | bytes 1179656 | tf_op jit(solution)/shard_map/ppermute | solution.py:78
  42.1 0.9 copy-start.4
  43.0 19.7 %collective-permute-start.4 = (bf16[128,1536]{1,0:T(8,128)(2,1)S(1)}, bf16[128,1536]{1,0:T(8,128)(2,1)}, u32[]{:S(2)}, u32[]{:S(2)}) collective-permute-start(bf16[128,1536]{1,0:T(8,128)(2,1)S(1)} %slice.8), channel_id=1, source_target_pairs={{0,2},{1,3},{2,4},{3,5},{4,6},{5,7},{6,0},{7,1},{8,10},{9,11},{10,... | collective-permute-start | bytes 1179656 | tf_op jit(solution)/shard_map/ppermute | solution.py:78
  44.9 28.3 %all-to-all-start = ((bf16[8,3,128,256]{3,2,1,0:T(8,128)(2,1)}), bf16[8,3,128,256]{3,2,1,0:T(8,128)(2,1)S(1)}, u32[]{:S(2)}, u32[]{:S(2)}) async-start(bf16[8,3,128,256]{3,2,1,0:T(8,128)(2,1)} %maximum_bitcast_fusion), calls=%async_computation | async-start | bytes 3145728 | tf_op jit(solution)/shard_map/all_to_all | solution.py:393
  52.4 33.0 %collective-permute-start.6 = (bf16[128,3072]{1,0:T(8,128)(2,1)}, bf16[128,3072]{1,0:T(8,128)(2,1)}, u32[]{:S(2)}, u32[]{:S(2)}) collective-permute-start(bf16[128,3072]{1,0:T(8,128)(2,1)} %collective-permute-done.5.refs_4_), channel_id=1, source_target_pairs={{0,6},{1,7},{2,0},{3,1},{4,2},{5,3},{6,4},{7,5},{8,14},{9,15},{10,... | collective-permute-start | bytes 2359304 | tf_op jit(solution)/shard_map/ppermute | solution.py:78
  56.9 31.4 %collective-permute-start.8 = (bf16[128,3072]{1,0:T(8,128)(2,1)}, bf16[128,3072]{1,0:T(8,128)(2,1)}, u32[]{:S(2)}, u32[]{:S(2)}) collective-permute-start(bf16[128,3072]{1,0:T(8,128)(2,1)} %collective-permute-done.5.refs_4_), channel_id=1, source_target_pairs={{0,2},{1,3},{2,4},{3,5},{4,6},{5,7},{6,0},{7,1},{8,10},{9,11},{10,... | collective-permute-start | bytes 2359304 | tf_op jit(solution)/shard_map/ppermute | solution.py:78
  63.7 24.7 %collective-permute-start.7 = (bf16[2,128,1536]{2,1,0:T(8,128)(2,1)S(1)}, bf16[2,128,1536]{2,1,0:T(8,128)(2,1)}, u32[]{:S(2)}, u32[]{:S(2)}) collective-permute-start(bf16[2,128,1536]{2,1,0:T(8,128)(2,1)S(1)} %pad_maximum_fusion.1.refs_2_), channel_id=1, source_target_pairs={{0,1},{1,0},{2,3},{3,2},{4,5},{5,4},{6,7},{7,6},{8,9},{9,8},{10,11... | collective-permute-start | bytes 2359304 | tf_op jit(solution)/shard_map/ppermute | solution.py:78
  73.2 19.5 %copy-start = (bf16[8,3,128,256]{3,2,1,0:T(8,128)(2,1)}, bf16[8,3,128,256]{3,2,1,0:T(8,128)(2,1)S(1)}, u32[]{:S(2)}) copy-start(bf16[8,3,128,256]{3,2,1,0:T(8,128)(2,1)S(1)} %all-to-all-done.x_ref.refs_9_) | copy-start | bytes 4718596
  73.2 15.2 %copy-start.2 = (bf16[128,3072]{1,0:T(8,128)(2,1)S(1)}, bf16[128,3072]{1,0:T(8,128)(2,1)}, u32[]{:S(2)}) copy-start(bf16[128,3072]{1,0:T(8,128)(2,1)} %copy-done.1) | copy-start | bytes 2359300
  73.2 15.2 %copy-start.5 = (bf16[128,3072]{1,0:T(8,128)(2,1)S(1)}, bf16[128,3072]{1,0:T(8,128)(2,1)}, u32[]{:S(2)}) copy-start(bf16[128,3072]{1,0:T(8,128)(2,1)} %copy-done.4) | copy-start | bytes 2359300
  82.4 10.2 %copy-start.7 = (bf16[1024,256]{1,0:T(8,128)(2,1)}, bf16[1024,256]{1,0:T(8,128)(2,1)S(1)}, u32[]{:S(2)}) copy-start(bf16[1024,256]{1,0:T(8,128)(2,1)S(1)} %get-tuple-element.28.refs_8_.refs_11_) | copy-start | bytes 1572868
  92.7 4.2 %collective-permute-start.9 = (bf16[8,4,48,256]{3,2,1,0:T(8,128)(2,1)S(1)}, bf16[8,4,48,256]{3,2,1,0:T(8,128)(2,1)S(1)}, u32[]{:S(2)}, u32[]{:S(2)}) collective-permute-start(bf16[8,4,48,256]{3,2,1,0:T(8,128)(2,1)S(1)} %get-tuple-element.27), channel_id=1, source_target_pairs={{0,8},{1,9},{2,10},{3,11},{4,12},{5,13},{6,14},{7,15},{8,0},{9,1},... | collective-permute-start | bytes 2359304 | tf_op jit(solution)/shard_map/ppermute | solution.py:78
  96.8 7.7 %copy-start.3 = (bf16[128,3072]{1,0:T(8,128)(2,1)S(1)}, bf16[128,3072]{1,0:T(8,128)(2,1)}, u32[]{:S(2)}) copy-start(bf16[128,3072]{1,0:T(8,128)(2,1)} %copy-done.1) | copy-start | bytes 2359300
  96.9 7.8 %copy-start.6 = (bf16[128,3072]{1,0:T(8,128)(2,1)S(1)}, bf16[128,3072]{1,0:T(8,128)(2,1)}, u32[]{:S(2)}) copy-start(bf16[128,3072]{1,0:T(8,128)(2,1)} %copy-done.4) | copy-start | bytes 2359300
  98.0 28.0 %all-to-all-start.1 = ((bf16[8,4,48,256]{3,2,1,0:T(8,128)(2,1)}), bf16[8,4,48,256]{3,2,1,0:T(8,128)(2,1)}, u32[]{:S(2)}, u32[]{:S(2)}) async-start(bf16[8,4,48,256]{3,2,1,0:T(8,128)(2,1)} %add_convert_fusion), calls=%async_computation.1 | async-start | bytes 1572864 | tf_op jit(solution)/shard_map/all_to_all | solution.py:409
  104.6 1.0 copy-start.8
  126.0 30.0 %all-to-all-start.2 = ((bf16[8,3,128,256]{3,2,1,0:T(8,128)(2,1)}), bf16[8,3,128,256]{3,2,1,0:T(8,128)(2,1)S(1)}, u32[]{:S(2)}, u32[]{:S(2)}) async-start(bf16[8,3,128,256]{3,2,1,0:T(8,128)(2,1)} %project_and_backward.1), calls=%async_computation.2 | async-start | bytes 3145728 | tf_op jit(solution)/shard_map/all_to_all | solution.py:413
  132.1 15.5 %collective-permute-start.10 = (bf16[2,48,256]{2,1,0:T(8,128)(2,1)S(1)}, bf16[2,48,256]{2,1,0:T(8,128)(2,1)S(1)}, u32[]{:S(2)}, u32[]{:S(2)}) collective-permute-start(bf16[2,48,256]{2,1,0:T(8,128)(2,1)S(1)} %dynamic-slice_bitcast_fusion), channel_id=1, source_target_pairs={{0,128},{1,129},{2,130},{3,131},{4,132},{5,133},{6,134},{7,135},{8... | collective-permute-start | bytes 147464 | tf_op jit(solution)/shard_map/ppermute | solution.py:78
  147.6 10.3 %collective-permute-start.11 = (bf16[48,256]{1,0:T(8,128)(2,1)S(1)}, bf16[48,256]{1,0:T(8,128)(2,1)S(1)}, u32[]{:S(2)}, u32[]{:S(2)}) collective-permute-start(bf16[48,256]{1,0:T(8,128)(2,1)S(1)} %fusion.1), channel_id=1, source_target_pairs={{0,64},{1,65},{2,66},{3,67},{4,68},{5,69},{6,70},{7,71},{8,72},{9,... | collective-permute-start | bytes 73736 | tf_op jit(solution)/shard_map/ppermute | solution.py:78
Sparse Core Ops, SparseCore 0:
  16.0 77.4 all-gather.2

commit v7 on v6

--- a/solution.py
+++ b/solution.py
@@ -396,6 +396,7 @@
     far = jnp.stack(
         [send(by_y[1][:, :HALF], FROM_Y[1]), send(by_y[3][:, HALF:], FROM_Y[3])]
     )
+    far, across = lax.optimization_barrier((far, across))
     pieces = [own, by_y[1], far, by_y[3]] + [
         across,
         send(across, FROM_Y[1]),

time: 166 us -> 166 us (level)
    ppermute x12, waiting for transfers between devices: 20.6 us -> 27.1 us  [send(): return lax.ppermute(x, AXES, pairs)]
    all_to_all x1, waiting for transfers between devices: 7.35 us -> 1.48 us  [local(): x = lax.all_to_all(x, 'sp', 0, 0, tiled=True)]
where the time goes in v7:
time: 166 us; the launch traced here: 165 us
  starting transfers between devices  74.8 us (45%)
  waiting for transfers between devices  35.1 us (21%)
  Pallas kernels  30.3 us (18%)
  between operations  14.5 us (9%)
  other arithmetic  7.15 us (4%)
  local copies, waits for them, and re-layouts  3.57 us (2%)
    ppermute x12, starting transfers between devices, send(): return lax.ppermute(x, AXES, pairs)  55.9 us
    ppermute x12, waiting for transfers between devices, send(): return lax.ppermute(x, AXES, pairs)  27.1 us
    pallas_call x1, Pallas kernels, backward(): pl.pallas_call(backward_kernel, out_shape=jax.ShapeDtypeStruct((SP, 3, TO...  13.8 us
    pallas_call x1, Pallas kernels, forward(): pl.pallas_call(forward_kernel, out_shape=(jax.ShapeDtypeStruct((LENGTH, C...  9.23 us
    all_to_all x1, starting transfers between devices, local(): x = lax.all_to_all(x, 'sp', 0, 0, tiled=True)  7.47 us
    all_to_all x1, starting transfers between devices, local(): lax.all_to_all(total, AXES, 0, 0, axis_index_groups=NEAR_GROUPS, tiled=True)  6.62 us
    all_to_all x1, waiting for transfers between devices, local(): lax.all_to_all(total, AXES, 0, 0, axis_index_groups=NEAR_GROUPS, tiled=True)  6.53 us
    all_to_all x1, starting transfers between devices, local(): back = lax.all_to_all(back, 'sp', 0, 0, tiled=True)  4.8 us
  transfers between devices with their start and end apart: 16, of which 10 were waited for; matrix products, arithmetic and copies ran while one was open for 4% of the time, Pallas kernels for 17%

profile of v7, /device:TPU:4, one launch (start us, length us, event | category | flops | bytes accessed | tf_op | source)
XLA Modules:
  0.0 165.4 jit_solution(8849845206497551630)
XLA Ops:
  7.2 0.0 all-gather.3.cloned.1.call-start
  7.2 1.6 dequantize.1
  8.9 3.2 %collective-permute-start = (bf16[2,48,256]{2,1,0:T(8,128)(2,1)}, bf16[2,48,256]{2,1,0:T(8,128)(2,1)S(1)}, u32[]{:S(2)}, u32[]{:S(2)}) collective-permute-start(bf16[2,48,256]{2,1,0:T(8,128)(2,1)} %dequantize.1), channel_id=1, source_target_pairs={{0,256},{1,257},{2,258},{3,259},{4,260},{5,261},{6,262},{7,263},{8... | collective-permute-start | bytes 147464 | tf_op jit(solution)/shard_map/ppermute | solution.py:78
  12.1 1.2 pad_maximum_fusion.refs_0_
  13.3 1.9 %collective-permute-done = bf16[2,48,256]{2,1,0:T(8,128)(2,1)S(1)} collective-permute-done((bf16[2,48,256]{2,1,0:T(8,128)(2,1)}, bf16[2,48,256]{2,1,0:T(8,128)(2,1)S(1)}, u32[]{:S(2)}, u32[]{:S(2)}) %collective-permute-start) | collective-permute-done | bytes 49184 | tf_op jit(solution)/shard_map/ppermute | solution.py:78
  15.2 0.7 pad_maximum_fusion.2
  15.8 0.0 all-gather.3.cloned.1.call-update
  15.9 4.9 %collective-permute-start.1 = (bf16[128,3072]{1,0:T(8,128)(2,1)S(1)}, bf16[128,3072]{1,0:T(8,128)(2,1)S(1)}, u32[]{:S(2)}, u32[]{:S(2)}) collective-permute-start(bf16[128,3072]{1,0:T(8,128)(2,1)S(1)} %pad_maximum_fusion.refs_0_), channel_id=1, source_target_pairs={{0,6},{1,7},{2,0},{3,1},{4,2},{5,3},{6,4},{7,5},{8,14},{9,15},{10,... | collective-permute-start | bytes 2359304 | tf_op jit(solution)/shard_map/ppermute | solution.py:78
  20.8 1.9 %collective-permute-start.3 = (bf16[128,3072]{1,0:T(8,128)(2,1)S(1)}, bf16[128,3072]{1,0:T(8,128)(2,1)S(1)}, u32[]{:S(2)}, u32[]{:S(2)}) collective-permute-start(bf16[128,3072]{1,0:T(8,128)(2,1)S(1)} %pad_maximum_fusion.refs_0_), channel_id=1, source_target_pairs={{0,2},{1,3},{2,4},{3,5},{4,6},{5,7},{6,0},{7,1},{8,10},{9,11},{10,... | collective-permute-start | bytes 2359304 | tf_op jit(solution)/shard_map/ppermute | solution.py:78
  22.7 0.4 copy.16
  23.1 0.3 copy.14
  23.4 0.7 copy-done.10
  24.1 0.1 copy.15
  24.2 0.1 copy.13
  24.3 6.8 %collective-permute-start.5 = (bf16[128,3072]{1,0:T(8,128)(2,1)S(1)}, bf16[128,3072]{1,0:T(8,128)(2,1)}, u32[]{:S(2)}, u32[]{:S(2)}) collective-permute-start(bf16[128,3072]{1,0:T(8,128)(2,1)S(1)} %pad_maximum_fusion.refs_0_), channel_id=1, source_target_pairs={{0,1},{1,0},{2,3},{3,2},{4,5},{5,4},{6,7},{7,6},{8,9},{9,8},{10,11... | collective-permute-start | bytes 2359304 | tf_op jit(solution)/shard_map/ppermute | solution.py:78
  31.1 1.3 maximum_bitcast_fusion
  32.3 4.1 %collective-permute-done.1.refs_1_ = bf16[128,3072]{1,0:T(8,128)(2,1)S(1)} collective-permute-done((bf16[128,3072]{1,0:T(8,128)(2,1)S(1)}, bf16[128,3072]{1,0:T(8,128)(2,1)S(1)}, u32[]{:S(2)}, u32[]{:S(2)}) %collective-permute-start.1) | collective-permute-done | bytes 786464 | tf_op jit(solution)/shard_map/ppermute | solution.py:78
  36.5 5.6 %collective-permute-start.2 = (bf16[128,1536]{1,0:T(8,128)(2,1)S(1)}, bf16[128,1536]{1,0:T(8,128)(2,1)S(1)}, u32[]{:S(2)}, u32[]{:S(2)}) collective-permute-start(bf16[128,1536]{1,0:T(8,128)(2,1)S(1)} %slice.6), channel_id=1, source_target_pairs={{0,6},{1,7},{2,0},{3,1},{4,2},{5,3},{6,4},{7,5},{8,14},{9,15},{10,... | collective-permute-start | bytes 1179656 | tf_op jit(solution)/shard_map/ppermute | solution.py:78
  42.1 0.8 copy-done.4
  43.0 1.9 %collective-permute-start.4 = (bf16[128,1536]{1,0:T(8,128)(2,1)S(1)}, bf16[128,1536]{1,0:T(8,128)(2,1)}, u32[]{:S(2)}, u32[]{:S(2)}) collective-permute-start(bf16[128,1536]{1,0:T(8,128)(2,1)S(1)} %slice.8), channel_id=1, source_target_pairs={{0,2},{1,3},{2,4},{3,5},{4,6},{5,7},{6,0},{7,1},{8,10},{9,11},{10,... | collective-permute-start | bytes 1179656 | tf_op jit(solution)/shard_map/ppermute | solution.py:78
  44.9 7.5 %all-to-all-start = ((bf16[8,3,128,256]{3,2,1,0:T(8,128)(2,1)}), bf16[8,3,128,256]{3,2,1,0:T(8,128)(2,1)S(1)}, u32[]{:S(2)}, u32[]{:S(2)}) async-start(bf16[8,3,128,256]{3,2,1,0:T(8,128)(2,1)} %maximum_bitcast_fusion), calls=%async_computation | async-start | bytes 3145728 | tf_op jit(solution)/shard_map/all_to_all | solution.py:393
  52.4 10.3 %collective-permute-done.4 = bf16[128,1536]{1,0:T(8,128)(2,1)} collective-permute-done((bf16[128,1536]{1,0:T(8,128)(2,1)S(1)}, bf16[128,1536]{1,0:T(8,128)(2,1)}, u32[]{:S(2)}, u32[]{:S(2)}) %collective-permute-start.4) | collective-permute-done | bytes 393248 | tf_op jit(solution)/shard_map/ppermute | solution.py:78
  62.6 1.1 pad_maximum_fusion.1.refs_2_
  63.7 1.9 %collective-permute-start.6 = (bf16[128,3072]{1,0:T(8,128)(2,1)}, bf16[128,3072]{1,0:T(8,128)(2,1)}, u32[]{:S(2)}, u32[]{:S(2)}) collective-permute-start(bf16[128,3072]{1,0:T(8,128)(2,1)} %collective-permute-done.5.refs_4_), channel_id=1, source_target_pairs={{0,6},{1,7},{2,0},{3,1},{4,2},{5,3},{6,4},{7,5},{8,14},{9,15},{10,... | collective-permute-start | bytes 2359304 | tf_op jit(solution)/shard_map/ppermute | solution.py:78
  65.6 3.9 %collective-permute-start.8 = (bf16[128,3072]{1,0:T(8,128)(2,1)}, bf16[128,3072]{1,0:T(8,128)(2,1)}, u32[]{:S(2)}, u32[]{:S(2)}) collective-permute-start(bf16[128,3072]{1,0:T(8,128)(2,1)} %collective-permute-done.5.refs_4_), channel_id=1, source_target_pairs={{0,2},{1,3},{2,4},{3,5},{4,6},{5,7},{6,0},{7,1},{8,10},{9,11},{10,... | collective-permute-start | bytes 2359304 | tf_op jit(solution)/shard_map/ppermute | solution.py:78
  69.6 1.9 %collective-permute-start.7 = (bf16[2,128,1536]{2,1,0:T(8,128)(2,1)S(1)}, bf16[2,128,1536]{2,1,0:T(8,128)(2,1)}, u32[]{:S(2)}, u32[]{:S(2)}) collective-permute-start(bf16[2,128,1536]{2,1,0:T(8,128)(2,1)S(1)} %pad_maximum_fusion.1.refs_2_), channel_id=1, source_target_pairs={{0,1},{1,0},{2,3},{3,2},{4,5},{5,4},{6,7},{7,6},{8,9},{9,8},{10,11... | collective-permute-start | bytes 2359304 | tf_op jit(solution)/shard_map/ppermute | solution.py:78
  71.6 0.1 stack.61.place_ref
  71.7 1.5 all-to-all-done.x_ref.refs_9_
  73.2 9.2 %attention_forward.1 = (bf16[1024,256]{1,0:T(8,128)(2,1)S(1)}, bf16[2,1024,1024]{2,1,0:T(8,128)(2,1)}) custom-call(bf16[8,3,128,256]{3,2,1,0:T(8,128)(2,1)S(1)} %all-to-all-done.x_ref.refs_9_), custom_call_target="tpu_custom_call" | custom-call | flops 1000 | bytes 1000 | tf_op jit(solution)/shard_map/attention_forward/pallas_call | solution.py:138
  82.4 2.9 %collective-permute-done.6.refs_5_ = bf16[128,3072]{1,0:T(8,128)(2,1)} collective-permute-done((bf16[128,3072]{1,0:T(8,128)(2,1)}, bf16[128,3072]{1,0:T(8,128)(2,1)}, u32[]{:S(2)}, u32[]{:S(2)}) %collective-permute-start.6) | collective-permute-done | bytes 786464 | tf_op jit(solution)/shard_map/ppermute | solution.py:78
  85.3 3.0 %collective-permute-done.8.refs_7_ = bf16[128,3072]{1,0:T(8,128)(2,1)} collective-permute-done((bf16[128,3072]{1,0:T(8,128)(2,1)}, bf16[128,3072]{1,0:T(8,128)(2,1)}, u32[]{:S(2)}, u32[]{:S(2)}) %collective-permute-start.8) | collective-permute-done | bytes 786464 | tf_op jit(solution)/shard_map/ppermute | solution.py:78
  88.4 4.3 %weight_term.1 = (bf16[8,4,48,256]{3,2,1,0:T(8,128)(2,1)S(1)}, bf16[8,4,48,256]{3,2,1,0:T(8,128)(2,1)S(1)}) custom-call(s32[10]{0:T(128)S(1)} %stack.61.place_ref, bf16[128,3072]{1,0:T(8,128)(2,1)S(1)} %pad_maximum_fusion.refs_0_, bf16[128,3072]{1,0:T(8,128)(2,1)S(1)} %copy-done.2, bf16[2,128,1536]{2,1,0:T(8,128)(2,1)S(1)} %pad_maximum_fusion.1.refs_2_, ...), custom_call_target="tpu_custom_call" | custom-call | flops 1000 | bytes 1000 | tf_op jit(solution)/shard_map/weight_term/pallas_call | solution.py:207
  92.7 1.9 %collective-permute-start.9 = (bf16[8,4,48,256]{3,2,1,0:T(8,128)(2,1)S(1)}, bf16[8,4,48,256]{3,2,1,0:T(8,128)(2,1)S(1)}, u32[]{:S(2)}, u32[]{:S(2)}) collective-permute-start(bf16[8,4,48,256]{3,2,1,0:T(8,128)(2,1)S(1)} %get-tuple-element.31), channel_id=1, source_target_pairs={{0,8},{1,9},{2,10},{3,11},{4,12},{5,13},{6,14},{7,15},{8,0},{9,1},... | collective-permute-start | bytes 2359304 | tf_op jit(solution)/shard_map/ppermute | solution.py:78
  94.6 2.3 %collective-permute-done.9 = bf16[8,4,48,256]{3,2,1,0:T(8,128)(2,1)S(1)} collective-permute-done((bf16[8,4,48,256]{3,2,1,0:T(8,128)(2,1)S(1)}, bf16[8,4,48,256]{3,2,1,0:T(8,128)(2,1)S(1)}, u32[]{:S(2)}, u32[]{:S(2)}) %collective-permute-start.9) | collective-permute-done | bytes 786464 | tf_op jit(solution)/shard_map/ppermute | solution.py:78
  96.9 1.1 add_convert_fusion
  98.0 6.6 %all-to-all-start.1 = ((bf16[8,4,48,256]{3,2,1,0:T(8,128)(2,1)}), bf16[8,4,48,256]{3,2,1,0:T(8,128)(2,1)}, u32[]{:S(2)}, u32[]{:S(2)}) async-start(bf16[8,4,48,256]{3,2,1,0:T(8,128)(2,1)} %add_convert_fusion), calls=%async_computation.1 | async-start | bytes 1572864 | tf_op jit(solution)/shard_map/all_to_all | solution.py:410
  104.6 0.0 all-gather.3.cloned.1.call-done
  104.6 1.0 copy-done.8
  105.7 13.8 %project_and_backward.1 = bf16[8,3,128,256]{3,2,1,0:T(8,128)(2,1)} custom-call(s32[10]{0:T(128)S(1)} %stack.61.place_ref, bf16[128,3072]{1,0:T(8,128)(2,1)S(1)} %pad_maximum_fusion.refs_0_, bf16[128,3072]{1,0:T(8,128)(2,1)S(1)} %copy-done.3, bf16[2,128,1536]{2,1,0:T(8,128)(2,1)S(1)} %pad_maximum_fusion.1.refs_2_, bf16[128,3072]{1,0:T(8,128)(2,1)S(1)} %copy-done.6, ...), custom_call_target="tpu_custom_call" | custom-call | flops 3758096384 | bytes 34603008 | tf_op jit(solution)/shard_map/project_and_backward/pallas_call | solution.py:302
  119.5 6.5 %all-to-all-done.1 = bf16[8,4,48,256]{3,2,1,0:T(8,128)(2,1)} async-done(((bf16[8,4,48,256]{3,2,1,0:T(8,128)(2,1)}), bf16[8,4,48,256]{3,2,1,0:T(8,128)(2,1)}, u32[]{:S(2)}, u32[]{:S(2)}) %all-to-all-start.1) | async-done | bytes 786464 | tf_op jit(solution)/shard_map/all_to_all | solution.py:410
  126.0 4.8 %all-to-all-start.2 = ((bf16[8,3,128,256]{3,2,1,0:T(8,128)(2,1)}), bf16[8,3,128,256]{3,2,1,0:T(8,128)(2,1)S(1)}, u32[]{:S(2)}, u32[]{:S(2)}) async-start(bf16[8,3,128,256]{3,2,1,0:T(8,128)(2,1)} %project_and_backward.1), calls=%async_computation.2 | async-start | bytes 3145728 | tf_op jit(solution)/shard_map/all_to_all | solution.py:414
  130.8 1.2 reduce_sum.12
  132.1 13.5 %collective-permute-start.10 = (bf16[2,48,256]{2,1,0:T(8,128)(2,1)S(1)}, bf16[2,48,256]{2,1,0:T(8,128)(2,1)S(1)}, u32[]{:S(2)}, u32[]{:S(2)}) collective-permute-start(bf16[2,48,256]{2,1,0:T(8,128)(2,1)S(1)} %dynamic-slice_bitcast_fusion), channel_id=1, source_target_pairs={{0,128},{1,129},{2,130},{3,131},{4,132},{5,133},{6,134},{7,135},{8... | collective-permute-start | bytes 147464 | tf_op jit(solution)/shard_map/ppermute | solution.py:78
  145.6 2.0 %collective-permute-done.10 = bf16[2,48,256]{2,1,0:T(8,128)(2,1)S(1)} collective-permute-done((bf16[2,48,256]{2,1,0:T(8,128)(2,1)S(1)}, bf16[2,48,256]{2,1,0:T(8,128)(2,1)S(1)}, u32[]{:S(2)}, u32[]{:S(2)}) %collective-permute-start.10) | collective-permute-done | bytes 49184 | tf_op jit(solution)/shard_map/ppermute | solution.py:78
  147.6 8.3 %collective-permute-start.11 = (bf16[48,256]{1,0:T(8,128)(2,1)S(1)}, bf16[48,256]{1,0:T(8,128)(2,1)S(1)}, u32[]{:S(2)}, u32[]{:S(2)}) collective-permute-start(bf16[48,256]{1,0:T(8,128)(2,1)S(1)} %fusion.1), channel_id=1, source_target_pairs={{0,64},{1,65},{2,66},{3,67},{4,68},{5,69},{6,70},{7,71},{8,72},{9,... | collective-permute-start | bytes 73736 | tf_op jit(solution)/shard_map/ppermute | solution.py:78
  156.0 1.3 spread_features.1
  157.4 0.6 collective-permute-done.11
  158.0 0.6 fusion
  (31 shorter events, 0.1 us)
Async XLA Ops:
  7.2 15.6 %copy-start.9 = (bf16[1,3,96,2048]{3,2,1,0:T(8,128)(2,1)S(1)}, bf16[1,3,96,2048]{3,2,1,0:T(8,128)(2,1)}, u32[]{:S(2)}) copy-start(bf16[1,3,96,2048]{3,2,1,0:T(8,128)(2,1)} %param.9) | copy-start | bytes 3538948
  7.2 97.4 %all-gather.3.cloned.1.call-start = ((), (), s32[]{:S(2)}) async-start(), calls=%async_computation.3 | async-start | bytes 3244032 | tf_op jit(solution)/shard_map/all_gather | solution.py:373
  8.9 6.3 %copy-start.11 = (bf16[2,48,256]{2,1,0:T(8,128)(2,1)S(1)}, bf16[2,48,256]{2,1,0:T(8,128)(2,1)}, u32[]{:S(2)}) copy-start(bf16[2,48,256]{2,1,0:T(8,128)(2,1)} %dequantize.1) | copy-start | bytes 147460
  8.9 6.3 %collective-permute-start = (bf16[2,48,256]{2,1,0:T(8,128)(2,1)}, bf16[2,48,256]{2,1,0:T(8,128)(2,1)S(1)}, u32[]{:S(2)}, u32[]{:S(2)}) collective-permute-start(bf16[2,48,256]{2,1,0:T(8,128)(2,1)} %dequantize.1), channel_id=1, source_target_pairs={{0,256},{1,257},{2,258},{3,259},{4,260},{5,261},{6,262},{7,263},{8... | collective-permute-start | bytes 147464 | tf_op jit(solution)/shard_map/ppermute | solution.py:78
  15.9 20.6 %collective-permute-start.1 = (bf16[128,3072]{1,0:T(8,128)(2,1)S(1)}, bf16[128,3072]{1,0:T(8,128)(2,1)S(1)}, u32[]{:S(2)}, u32[]{:S(2)}) collective-permute-start(bf16[128,3072]{1,0:T(8,128)(2,1)S(1)} %pad_maximum_fusion.refs_0_), channel_id=1, source_target_pairs={{0,6},{1,7},{2,0},{3,1},{4,2},{5,3},{6,4},{7,5},{8,14},{9,15},{10,... | collective-permute-start | bytes 2359304 | tf_op jit(solution)/shard_map/ppermute | solution.py:78
  20.8 21.3 %collective-permute-start.3 = (bf16[128,3072]{1,0:T(8,128)(2,1)S(1)}, bf16[128,3072]{1,0:T(8,128)(2,1)S(1)}, u32[]{:S(2)}, u32[]{:S(2)}) collective-permute-start(bf16[128,3072]{1,0:T(8,128)(2,1)S(1)} %pad_maximum_fusion.refs_0_), channel_id=1, source_target_pairs={{0,2},{1,3},{2,4},{3,5},{4,6},{5,7},{6,0},{7,1},{8,10},{9,11},{10,... | collective-permute-start | bytes 2359304 | tf_op jit(solution)/shard_map/ppermute | solution.py:78
  23.1 1.0 copy-start.10
  24.3 39.5 %collective-permute-start.5 = (bf16[128,3072]{1,0:T(8,128)(2,1)S(1)}, bf16[128,3072]{1,0:T(8,128)(2,1)}, u32[]{:S(2)}, u32[]{:S(2)}) collective-permute-start(bf16[128,3072]{1,0:T(8,128)(2,1)S(1)} %pad_maximum_fusion.refs_0_), channel_id=1, source_target_pairs={{0,1},{1,0},{2,3},{3,2},{4,5},{5,4},{6,7},{7,6},{8,9},{9,8},{10,11... | collective-permute-start | bytes 2359304 | tf_op jit(solution)/shard_map/ppermute | solution.py:78
  36.4 5.7 %copy-start.1 = (bf16[128,3072]{1,0:T(8,128)(2,1)}, bf16[128,3072]{1,0:T(8,128)(2,1)S(1)}, u32[]{:S(2)}) copy-start(bf16[128,3072]{1,0:T(8,128)(2,1)S(1)} %collective-permute-done.1.refs_1_) | copy-start | bytes 2359300
  36.5 15.9 %collective-permute-start.2 = (bf16[128,1536]{1,0:T(8,128)(2,1)S(1)}, bf16[128,1536]{1,0:T(8,128)(2,1)S(1)}, u32[]{:S(2)}, u32[]{:S(2)}) collective-permute-start(bf16[128,1536]{1,0:T(8,128)(2,1)S(1)} %slice.6), channel_id=1, source_target_pairs={{0,6},{1,7},{2,0},{3,1},{4,2},{5,3},{6,4},{7,5},{8,14},{9,15},{10,... | collective-permute-start | bytes 1179656 | tf_op jit(solution)/shard_map/ppermute | solution.py:78
  42.1 0.9 copy-start.4
  43.0 19.7 %collective-permute-start.4 = (bf16[128,1536]{1,0:T(8,128)(2,1)S(1)}, bf16[128,1536]{1,0:T(8,128)(2,1)}, u32[]{:S(2)}, u32[]{:S(2)}) collective-permute-start(bf16[128,1536]{1,0:T(8,128)(2,1)S(1)} %slice.8), channel_id=1, source_target_pairs={{0,2},{1,3},{2,4},{3,5},{4,6},{5,7},{6,0},{7,1},{8,10},{9,11},{10,... | collective-permute-start | bytes 1179656 | tf_op jit(solution)/shard_map/ppermute | solution.py:78
  44.9 28.3 %all-to-all-start = ((bf16[8,3,128,256]{3,2,1,0:T(8,128)(2,1)}), bf16[8,3,128,256]{3,2,1,0:T(8,128)(2,1)S(1)}, u32[]{:S(2)}, u32[]{:S(2)}) async-start(bf16[8,3,128,256]{3,2,1,0:T(8,128)(2,1)} %maximum_bitcast_fusion), calls=%async_computation | async-start | bytes 3145728 | tf_op jit(solution)/shard_map/all_to_all | solution.py:393
  63.7 21.6 %collective-permute-start.6 = (bf16[128,3072]{1,0:T(8,128)(2,1)}, bf16[128,3072]{1,0:T(8,128)(2,1)}, u32[]{:S(2)}, u32[]{:S(2)}) collective-permute-start(bf16[128,3072]{1,0:T(8,128)(2,1)} %collective-permute-done.5.refs_4_), channel_id=1, source_target_pairs={{0,6},{1,7},{2,0},{3,1},{4,2},{5,3},{6,4},{7,5},{8,14},{9,15},{10,... | collective-permute-start | bytes 2359304 | tf_op jit(solution)/shard_map/ppermute | solution.py:78
  65.6 22.7 %collective-permute-start.8 = (bf16[128,3072]{1,0:T(8,128)(2,1)}, bf16[128,3072]{1,0:T(8,128)(2,1)}, u32[]{:S(2)}, u32[]{:S(2)}) collective-permute-start(bf16[128,3072]{1,0:T(8,128)(2,1)} %collective-permute-done.5.refs_4_), channel_id=1, source_target_pairs={{0,2},{1,3},{2,4},{3,5},{4,6},{5,7},{6,0},{7,1},{8,10},{9,11},{10,... | collective-permute-start | bytes 2359304 | tf_op jit(solution)/shard_map/ppermute | solution.py:78
  69.6 18.8 %collective-permute-start.7 = (bf16[2,128,1536]{2,1,0:T(8,128)(2,1)S(1)}, bf16[2,128,1536]{2,1,0:T(8,128)(2,1)}, u32[]{:S(2)}, u32[]{:S(2)}) collective-permute-start(bf16[2,128,1536]{2,1,0:T(8,128)(2,1)S(1)} %pad_maximum_fusion.1.refs_2_), channel_id=1, source_target_pairs={{0,1},{1,0},{2,3},{3,2},{4,5},{5,4},{6,7},{7,6},{8,9},{9,8},{10,11... | collective-permute-start | bytes 2359304 | tf_op jit(solution)/shard_map/ppermute | solution.py:78
  73.2 19.5 %copy-start = (bf16[8,3,128,256]{3,2,1,0:T(8,128)(2,1)}, bf16[8,3,128,256]{3,2,1,0:T(8,128)(2,1)S(1)}, u32[]{:S(2)}) copy-start(bf16[8,3,128,256]{3,2,1,0:T(8,128)(2,1)S(1)} %all-to-all-done.x_ref.refs_9_) | copy-start | bytes 4718596
  73.2 15.2 %copy-start.2 = (bf16[128,3072]{1,0:T(8,128)(2,1)S(1)}, bf16[128,3072]{1,0:T(8,128)(2,1)}, u32[]{:S(2)}) copy-start(bf16[128,3072]{1,0:T(8,128)(2,1)} %copy-done.1) | copy-start | bytes 2359300
  73.2 15.2 %copy-start.5 = (bf16[128,3072]{1,0:T(8,128)(2,1)S(1)}, bf16[128,3072]{1,0:T(8,128)(2,1)}, u32[]{:S(2)}) copy-start(bf16[128,3072]{1,0:T(8,128)(2,1)} %copy-done.4) | copy-start | bytes 2359300
  82.4 10.2 %copy-start.7 = (bf16[1024,256]{1,0:T(8,128)(2,1)}, bf16[1024,256]{1,0:T(8,128)(2,1)S(1)}, u32[]{:S(2)}) copy-start(bf16[1024,256]{1,0:T(8,128)(2,1)S(1)} %get-tuple-element.32.refs_8_.refs_11_) | copy-start | bytes 1572868
  92.7 4.2 %collective-permute-start.9 = (bf16[8,4,48,256]{3,2,1,0:T(8,128)(2,1)S(1)}, bf16[8,4,48,256]{3,2,1,0:T(8,128)(2,1)S(1)}, u32[]{:S(2)}, u32[]{:S(2)}) collective-permute-start(bf16[8,4,48,256]{3,2,1,0:T(8,128)(2,1)S(1)} %get-tuple-element.31), channel_id=1, source_target_pairs={{0,8},{1,9},{2,10},{3,11},{4,12},{5,13},{6,14},{7,15},{8,0},{9,1},... | collective-permute-start | bytes 2359304 | tf_op jit(solution)/shard_map/ppermute | solution.py:78
  96.9 7.7 %copy-start.3 = (bf16[128,3072]{1,0:T(8,128)(2,1)S(1)}, bf16[128,3072]{1,0:T(8,128)(2,1)}, u32[]{:S(2)}) copy-start(bf16[128,3072]{1,0:T(8,128)(2,1)} %copy-done.1) | copy-start | bytes 2359300
  96.9 7.8 %copy-start.6 = (bf16[128,3072]{1,0:T(8,128)(2,1)S(1)}, bf16[128,3072]{1,0:T(8,128)(2,1)}, u32[]{:S(2)}) copy-start(bf16[128,3072]{1,0:T(8,128)(2,1)} %copy-done.4) | copy-start | bytes 2359300
  98.0 28.0 %all-to-all-start.1 = ((bf16[8,4,48,256]{3,2,1,0:T(8,128)(2,1)}), bf16[8,4,48,256]{3,2,1,0:T(8,128)(2,1)}, u32[]{:S(2)}, u32[]{:S(2)}) async-start(bf16[8,4,48,256]{3,2,1,0:T(8,128)(2,1)} %add_convert_fusion), calls=%async_computation.1 | async-start | bytes 1572864 | tf_op jit(solution)/shard_map/all_to_all | solution.py:410
  104.6 1.0 copy-start.8
  126.0 30.0 %all-to-all-start.2 = ((bf16[8,3,128,256]{3,2,1,0:T(8,128)(2,1)}), bf16[8,3,128,256]{3,2,1,0:T(8,128)(2,1)S(1)}, u32[]{:S(2)}, u32[]{:S(2)}) async-start(bf16[8,3,128,256]{3,2,1,0:T(8,128)(2,1)} %project_and_backward.1), calls=%async_computation.2 | async-start | bytes 3145728 | tf_op jit(solution)/shard_map/all_to_all | solution.py:414
  132.1 15.5 %collective-permute-start.10 = (bf16[2,48,256]{2,1,0:T(8,128)(2,1)S(1)}, bf16[2,48,256]{2,1,0:T(8,128)(2,1)S(1)}, u32[]{:S(2)}, u32[]{:S(2)}) collective-permute-start(bf16[2,48,256]{2,1,0:T(8,128)(2,1)S(1)} %dynamic-slice_bitcast_fusion), channel_id=1, source_target_pairs={{0,128},{1,129},{2,130},{3,131},{4,132},{5,133},{6,134},{7,135},{8... | collective-permute-start | bytes 147464 | tf_op jit(solution)/shard_map/ppermute | solution.py:78
  147.6 10.3 %collective-permute-start.11 = (bf16[48,256]{1,0:T(8,128)(2,1)S(1)}, bf16[48,256]{1,0:T(8,128)(2,1)S(1)}, u32[]{:S(2)}, u32[]{:S(2)}) collective-permute-start(bf16[48,256]{1,0:T(8,128)(2,1)S(1)} %fusion.1), channel_id=1, source_target_pairs={{0,64},{1,65},{2,66},{3,67},{4,68},{5,69},{6,70},{7,71},{8,72},{9,... | collective-permute-start | bytes 73736 | tf_op jit(solution)/shard_map/ppermute | solution.py:78
Sparse Core Ops, SparseCore 0:
  16.0 77.3 all-gather.2
